TPU v7x, 512 devices: a whole 4x8x8 slice. The times are simulated.
512 devices in a mesh: section: 64 (over y, z_hi, core), tp: 8 (over z_lo, x).
Axes of the slice: x: 4, y: 8, z: 8 (z_hi: 4, z_lo: 2; z = z_hi * 2 + z_lo), core: 2. Of those that a mesh axis runs over, the one named last changes fastest.
Arguments:
- arriving: bfloat16 [64, 96, 2048], P('section'), may hold values from -10.8 to 10.8
- norm_gain: bfloat16 [64, 2048], P('section'), may hold values from 0.099609375 to 1.8984375
- w_qkv: bfloat16 [64, 2048, 3072], P('section', None, 'tp'), may hold values from -0.09375 to 0.09375
- w_out: bfloat16 [64, 2048, 2048], P('section', 'tp'), may hold values from -0.125 to 0.125
- cache: bfloat16 [64, 4, 48, 16, 1024], P('section', None, None, None, 'tp')
- lengths: int32 [32, 96], replicated, may hold values from 1 to 16, as said below
- talk_gain: bfloat16 [2, 2048], P(None, 'tp'), may hold values from 0.5 to 1.5
- w_adapt: bfloat16 [2, 2048, 3072], P(None, 'tp', 'section'), may hold values from -0.09375 to 0.09375
- codebooks: bfloat16 [4, 2048, 3072], P(None, 'tp', 'section'), may hold values from -3 to 3
- codes: int32 [4, 96, 4], replicated, may hold values from 0 to 2048, as said below
Outputs:
- leaving: float32 [64, 96, 2048], P('section')
- talker_in: float32 [4, 96, 3072], P(None, None, 'section')
Inputs may be any that keep to these rules, and one draw needn't show every extreme that they name: `lengths`: every micro-batch holds one or more streams of length 16. 2048 marks a codebook not yet started under the delay pattern: if codes[k, b, q] is 2048, so is codes[k, b, q'] for every q' > q.
All inputs are finite; a program needn't handle non-finite values.
Results may differ from a plain program's by a relative error of at most 0.034.
Values may be sent and summed in bfloat16 or wider, within the bound.
No kernel may reach another device: no remote copies, remote signals or barrier semaphores. Data moves between devices by JAX's collectives and lax.ppermute only.
A program may use at most 64 MiB of HBM per device.

v0:
```python
import math

import jax
import jax.numpy as jnp
from jax import lax
from jax.sharding import PartitionSpec as P

D = 4096
H = 32
KVH = 8
HD = 64
NQ = 4
TICKS = 4
B = 96
CACHE = 16


epsilon = 1e-05


def broadcast(value, axis, source):
    kept = jnp.where(lax.axis_index(axis) == source, value, 0).astype(value.dtype)
    return lax.psum(kept, axis)


def swapped(value, axis, distance):
    mask = 2**distance
    pairs = [(source, source ^ mask) for source in range(lax.axis_size(axis))]
    return lax.ppermute(value, axis, pairs)


def shifted(block, axis, distance):
    devices = range(lax.axis_size(axis))
    route = [(i - distance, i) for i in devices if i - distance in devices]
    return lax.ppermute(block, axis, route)


def attend_half(queries, keys_new, values_new, cached_now, stream_lens):
    cache_keys = cached_now[:, :, :, 0, :]
    cache_values = cached_now[:, :, :, 1, :]
    score_scale = 1.0 / math.sqrt(HD)
    scores = (
        jnp.einsum("bgrd,bjgd->bgrj", queries, cache_keys, preferred_element_type=jnp.float32)
        * score_scale
    )
    own_score = (
        jnp.einsum("bgrd,bgd->bgr", queries, keys_new, preferred_element_type=jnp.float32)
        * score_scale
    )
    visible = (jnp.arange(CACHE, dtype=jnp.int32)[None, :] < stream_lens[:, None])[:, None, None, :]
    row_max = jnp.maximum(jnp.max(jnp.where(visible, scores, -jnp.inf), axis=-1), own_score)
    weights = jnp.where(visible, jnp.exp(scores - row_max[..., None]), 0.0)
    own_weight = jnp.exp(own_score - row_max)
    denom_sum = jnp.sum(weights, axis=-1) + own_weight
    weights = (weights / denom_sum[..., None]).astype(jnp.bfloat16)
    own_weight = (own_weight / denom_sum).astype(jnp.bfloat16)
    mixed_out = jnp.einsum(
        "bgrj,bjgd->bgrd", weights, cache_values, preferred_element_type=jnp.float32
    )
    mixed_out = (
        mixed_out
        + own_weight.astype(jnp.float32)[..., None] * values_new.astype(jnp.float32)[:, :, None, :]
    )
    return mixed_out.astype(jnp.bfloat16)


def from_last(last_piece, root_index):
    return broadcast(last_piece.astype(jnp.bfloat16), "section", root_index).astype(
        last_piece.dtype
    )


def talker_rows(low_rows, high_rows, talk_gain, w_adapt, codebooks, codes_now, column):
    tick_count = low_rows.shape[0]
    block_width = low_rows.shape[2]
    squares = jnp.sum(low_rows * low_rows, axis=-1) + jnp.sum(high_rows * high_rows, axis=-1)
    gain_pair = talk_gain.astype(jnp.float32)
    scaled_low = (low_rows * gain_pair[0]).astype(jnp.bfloat16).reshape(tick_count * B, block_width)
    scaled_high = (
        (high_rows * gain_pair[1]).astype(jnp.bfloat16).reshape(tick_count * B, block_width)
    )
    adapted = jnp.dot(scaled_low, w_adapt[0], preferred_element_type=jnp.float32)
    adapted = adapted + jnp.dot(scaled_high, w_adapt[1], preferred_element_type=jnp.float32)
    entries = codebooks.shape[1]
    local_ids = codes_now.reshape(tick_count * B, NQ) - column * entries
    one_hot = (local_ids[:, :, None] == jnp.arange(entries, dtype=jnp.int32)[None, None, :]).astype(
        jnp.bfloat16
    )
    one_hot = one_hot.reshape(tick_count * B, NQ * entries)
    embedded = jnp.dot(
        one_hot, codebooks.reshape(NQ * entries, -1), preferred_element_type=jnp.float32
    )
    adapted, embedded, squares = (
        lax.psum(adapted.astype(jnp.bfloat16), "tp").astype(jnp.float32),
        lax.psum(embedded.astype(jnp.bfloat16), "tp").astype(jnp.float32),
        lax.psum(squares.reshape(tick_count * B).astype(jnp.bfloat16), "tp").astype(jnp.float32),
    )
    talk_rms = lax.rsqrt(squares / D + epsilon)
    return (adapted * talk_rms[:, None] + embedded).reshape(tick_count, B, -1)


def body(arriving, norm_gain, w_qkv, w_out, cache, lengths, talk_gain, w_adapt, codebooks, codes):
    section_count = lax.axis_size("section")
    tp_count = lax.axis_size("tp")
    position = lax.axis_index("section")
    column = lax.axis_index("tp")
    pair_side = position % 2
    section_pos = position // 2
    half_rows = B // 2
    groups = KVH // tp_count
    head_ratio = H // KVH
    rows_now = arriving[0].astype(jnp.float32)
    block_width = rows_now.shape[1] // tp_count
    norm_scale = norm_gain[0].astype(jnp.float32)
    qkv_weight = w_qkv[0]
    out_weight = w_out[0]
    latest = rows_now
    talker_list = []
    for tick_index in range(TICKS):
        micro_batch = section_pos - tick_index
        row_lens = lax.dynamic_slice_in_dim(lengths, jnp.maximum(micro_batch, 0), 1, 0)[0]
        half_lens = lax.dynamic_slice_in_dim(row_lens, pair_side * half_rows, half_rows, 0)
        stream_lens = jnp.where(micro_batch >= 0, half_lens, 0)
        rows_f = rows_now
        squares = jnp.sum(rows_f * rows_f, axis=-1)
        scaled = (rows_f * norm_scale).astype(jnp.bfloat16)
        partial_value = jnp.dot(scaled, qkv_weight, preferred_element_type=jnp.float32)
        mine_start = pair_side * half_rows
        other_start = (1 - pair_side) * half_rows
        other_part = lax.dynamic_slice_in_dim(partial_value, other_start, half_rows, 0)
        other_squares = lax.dynamic_slice_in_dim(squares, other_start, half_rows, 0)
        got_part, got_squares = swapped((other_part, other_squares), "section", 0)
        mixed_proj = lax.dynamic_slice_in_dim(partial_value, mine_start, half_rows, 0) + got_part
        row_squares = lax.dynamic_slice_in_dim(squares, mine_start, half_rows, 0) + got_squares
        inv_rms = lax.rsqrt(row_squares / D + epsilon)
        mixed_proj = (mixed_proj * inv_rms[:, None]).reshape(half_rows, groups, head_ratio + 2, HD)
        queries = mixed_proj[:, :, :head_ratio].astype(jnp.bfloat16)
        keys_new = mixed_proj[:, :, head_ratio].astype(jnp.bfloat16)
        values_new = mixed_proj[:, :, head_ratio + 1].astype(jnp.bfloat16)
        cached_now = cache[0, tick_index].reshape(half_rows, CACHE, groups, 2, HD)
        head_rows = attend_half(queries, keys_new, values_new, cached_now, stream_lens)
        head_rows = head_rows.reshape(half_rows, groups * head_ratio * HD)
        partner = swapped(head_rows, "section", 0)
        lower_rows = jnp.where(pair_side == 0, head_rows, partner)
        upper_rows = jnp.where(pair_side == 0, partner, head_rows)
        all_heads = jnp.concatenate([lower_rows, upper_rows], axis=0)
        update_terms = jnp.dot(all_heads, out_weight, preferred_element_type=jnp.float32)
        produced = rows_f + lax.psum(update_terms, "tp")
        last_piece = lax.dynamic_slice_in_dim(produced, column * block_width, block_width, 1)
        if tick_index == 0:
            latest = produced
        else:
            latest = jnp.where(section_pos >= tick_index, produced, latest)
        low_rows = from_last(last_piece[None], section_count - 2)
        high_rows = from_last(last_piece[None], section_count - 1)
        talker_list.append(
            talker_rows(
                low_rows,
                high_rows,
                talk_gain,
                w_adapt,
                codebooks,
                codes[tick_index : tick_index + 1],
                column,
            )
        )
        if tick_index + 1 < TICKS:
            rows_now = shifted(produced, "section", 2)
    talker_out = jnp.concatenate(talker_list, axis=0)
    return (latest[None], talker_out)


def solution(mesh):
    placed = (
        P("section", None, None),
        P("section", None),
        P("section", None, "tp"),
        P("section", "tp", None),
        P("section", None, None, None, "tp"),
        P(),
        P(None, "tp"),
        P(None, "tp", "section"),
        P(None, "tp", "section"),
        P(),
    )
    return jax.shard_map(
        body,
        mesh=mesh,
        in_specs=placed,
        out_specs=(P("section", None, None), P(None, None, "section")),
        check_vma=False,
    )
```

profile of v0, /device:TPU:1, one launch (start us, length us, event | category | flops | bytes accessed | tf_op | source)
XLA Modules:
  0.0 1185.1 jit_solution(3303476510609473514)
XLA Ops:
  7.3 1.3 fusion.30
  8.7 8.8 collective-permute-start.1
  18.2 1.4 fusion.6
  20.2 1.9 collective-permute-start
  27.6 1.1 fusion.118
  28.7 1.2 select_reduce_fusion.3
  30.6 2.4 collective-permute-start.2
  33.8 1.2 fusion.26
  35.1 80.8 %all-reduce.9.cloned.1.call-done = f32[96,2048]{1,0:T(8,128)} async-done(((f32[96,2048]{1,0:T(8,128)}), f32[96,2048]{1,0:T(8,128)}) %all-reduce.9.cloned.1.call-update) | async-done | bytes 786448 | tf_op jit(solution)/shard_map/psum | solution.py:148
  115.9 2.1 fusion.28
  118.0 4.3 collective-permute-start.3
  122.4 1.9 reshape_squeeze.13
  124.3 2.7 fusion.161
  127.0 6.9 collective-permute-done.3
  134.1 8.5 collective-permute-start.5
  143.0 1.9 collective-permute-start.4
  145.0 1.1 collective-permute-done.4
  147.9 1.1 fusion.119
  149.0 1.4 select_reduce_fusion.2
  150.6 1.3 fusion.9
  152.1 2.1 collective-permute-start.6
  154.1 1.0 collective-permute-done.6
  155.1 1.2 fusion.24
  156.4 99.7 %all-reduce.11.cloned.1.call-done = f32[96,2048]{1,0:T(8,128)} async-done(((f32[96,2048]{1,0:T(8,128)}), f32[96,2048]{1,0:T(8,128)}) %all-reduce.11.cloned.1.call-update) | async-done | bytes 786448 | tf_op jit(solution)/shard_map/psum | solution.py:148
  256.1 2.1 add.252
  258.2 4.3 collective-permute-start.7
  262.6 1.9 reshape_squeeze.14
  264.5 2.7 fusion.160
  267.2 6.8 collective-permute-done.7
  274.3 8.5 collective-permute-start.9
  283.2 1.9 collective-permute-start.8
  285.2 1.1 collective-permute-done.8
  288.1 1.1 fusion.120
  289.2 1.4 select_reduce_fusion.1
  290.9 1.3 fusion.10
  292.3 2.1 collective-permute-start.10
  295.4 1.2 fusion.22
  296.7 99.7 %all-reduce.13.cloned.1.call-done = f32[96,2048]{1,0:T(8,128)} async-done(((f32[96,2048]{1,0:T(8,128)}), f32[96,2048]{1,0:T(8,128)}) %all-reduce.13.cloned.1.call-update) | async-done | bytes 786448 | tf_op jit(solution)/shard_map/psum | solution.py:148
  396.4 2.1 add.258
  398.5 4.3 collective-permute-start.11
  402.8 1.9 reshape_squeeze.15
  405.3 2.7 fusion.159
  408.0 6.3 collective-permute-done.11
  414.5 8.5 collective-permute-start.13
  423.4 1.9 collective-permute-start.12
  425.4 1.1 collective-permute-done.12
  427.0 1.3 select_reduce_fusion
  428.6 1.3 fusion.11
  430.0 2.1 collective-permute-start.14
  432.1 1.8 fusion.13
  433.8 1.2 fusion.20
  435.1 1.8 fusion.15
  436.9 1.8 fusion.19
  438.7 1.5 select_bitcast_fusion.7
  440.2 1.5 select_bitcast_fusion.5
  441.7 1.5 select_bitcast_fusion.3
  443.3 91.7 %all-reduce.15.cloned.1.call-done = f32[96,2048]{1,0:T(8,128)} async-done(((f32[96,2048]{1,0:T(8,128)}), f32[96,2048]{1,0:T(8,128)}) %all-reduce.15.cloned.1.call-update) | async-done | bytes 786448 | tf_op jit(solution)/shard_map/psum | solution.py:148
  535.0 2.5 select_bitcast_fusion
  539.2 540.5 %all-reduce.17.cloned.1.call-done = (bf16[1,96,256]{2,1,0:T(8,128)(2,1)}, bf16[1,96,256]{2,1,0:T(8,128)(2,1)}, bf16[1,96,256]{2,1,0:T(8,128)(2,1)}, bf16[1,96,25...) async-done(((bf16[1,96,256]{2,1,0:T(8,128)(2,1)}, ...) | async-done | bytes 393232 | tf_op jit(solution)/shard_map/psum | solution.py:23
  1083.5 1.6 fusion.18
  1085.0 1.5 fusion.16
  1088.5 1.6 fusion.14
  1091.9 1.6 fusion.12
  1095.6 76.6 %all-reduce.19.cloned.1.call-done = (bf16[96,48]{0,1:T(8,128)(2,1)}, bf16[96,48]{0,1:T(8,128)(2,1)}, bf16[96]{0:T(256)(128)(2,1)}, bf16[96,48]{0,1:T(8,128)(2,1)...) async-done(((bf16[96,48]{0,1:T(8,128)(2,1)}, ...) | async-done | bytes 74512 | tf_op jit(solution)/shard_map/psum | solution.py:95
  (126 shorter events, 34.9 us)
Async XLA Ops:
  7.2 11.0 copy-start
  7.2 15.0 %copy-start.3 = (bf16[1,4,48,16,128]{4,3,2,1,0:T(8,128)(2,1)S(1)}, bf16[1,4,48,16,128]{4,3,2,1,0:T(8,128)(2,1)}, u32[]{:S(2)}) copy-start(bf16[1,4,48,16,128]{4,3,2,1,0:T(8,128)(2,1)} %param.14) | copy-start | bytes 2359300
  7.2 108.7 %all-reduce.9.cloned.1.call-start = ((), (), s32[]{:S(2)}) async-start(), calls=%async_computation | async-start | bytes 1572864 | tf_op jit(solution)/shard_map/psum | solution.py:148
  8.7 16.1 %collective-permute-start.1 = (f32[48]{0:T(128)S(1)}, f32[48]{0:T(128)S(1)}, u32[]{:S(2)}, u32[]{:S(2)}) collective-permute-start(f32[48]{0:T(128)S(1)} %dynamic_slice.80), channel_id=1, source_target_pairs={{0,8},{8,0},{16,24},{24,16},{32,40},{40,32},{48,56},{56,48},{64,72... | collective-permute-start | bytes 584 | tf_op jit(solution)/shard_map/ppermute | solution.py:29
  20.2 4.7 collective-permute-start
  25.9 8.0 copy-start.1
  30.5 85.5 %copy-start.2 = (bf16[1,96,2048]{2,1,0:T(8,128)(2,1)S(1)}, bf16[1,96,2048]{2,1,0:T(8,128)(2,1)}, u32[]{:S(2)}) copy-start(bf16[1,96,2048]{2,1,0:T(8,128)(2,1)} %param.10) | copy-start | bytes 1179652
  30.6 3.2 collective-permute-start.2
  35.0 221.1 %all-reduce.11.cloned.1.call-start = ((), (), s32[]{:S(2)}) async-start(), calls=%async_computation.1 | async-start | bytes 1572864 | tf_op jit(solution)/shard_map/psum | solution.py:148
  118.0 15.8 %collective-permute-start.3 = (f32[96,2048]{1,0:T(8,128)}, f32[96,2048]{1,0:T(8,128)S(1)}, u32[]{:S(2)}, u32[]{:S(2)}) collective-permute-start(f32[96,2048]{1,0:T(8,128)} %fusion.28), channel_id=1, source_target_pairs={{0,16},{8,24},{16,32},{24,40},{32,48},{40,56},{48,64},{56,72},{64,... | collective-permute-start | bytes 2359304 | tf_op jit(solution)/shard_map/ppermute | solution.py:35
  134.1 10.8 collective-permute-start.5
  143.0 3.2 collective-permute-start.4
  152.1 3.1 collective-permute-start.6
  156.4 240.0 %all-reduce.13.cloned.1.call-start = ((), (), s32[]{:S(2)}) async-start(), calls=%async_computation.2 | async-start | bytes 1572864 | tf_op jit(solution)/shard_map/psum | solution.py:148
  258.2 15.8 %collective-permute-start.7 = (f32[96,2048]{1,0:T(8,128)}, f32[96,2048]{1,0:T(8,128)S(1)}, u32[]{:S(2)}, u32[]{:S(2)}) collective-permute-start(f32[96,2048]{1,0:T(8,128)} %add.252), channel_id=1, source_target_pairs={{0,16},{8,24},{16,32},{24,40},{32,48},{40,56},{48,64},{56,72},{64,... | collective-permute-start | bytes 2359304 | tf_op jit(solution)/shard_map/ppermute | solution.py:35
  274.3 10.8 collective-permute-start.9
  283.2 3.2 collective-permute-start.8
  292.3 3.1 collective-permute-start.10
  296.6 108.1 %copy-start.5 = (s32[4,96,4]{1,2,0:T(4,128)S(1)}, s32[4,96,4]{1,2,0:T(4,128)}, u32[]{:S(2)}) copy-start(s32[4,96,4]{1,2,0:T(4,128)} %param.19) | copy-start | bytes 18436
  296.6 238.4 %all-reduce.15.cloned.1.call-start = ((), (), s32[]{:S(2)}) async-start(), calls=%async_computation.3 | async-start | bytes 1572864 | tf_op jit(solution)/shard_map/psum | solution.py:148
  398.5 15.8 %collective-permute-start.11 = (f32[96,2048]{1,0:T(8,128)}, f32[96,2048]{1,0:T(8,128)S(1)}, u32[]{:S(2)}, u32[]{:S(2)}) collective-permute-start(f32[96,2048]{1,0:T(8,128)} %add.258), channel_id=1, source_target_pairs={{0,16},{8,24},{16,32},{24,40},{32,48},{40,56},{48,64},{56,72},{64,... | collective-permute-start | bytes 2359304 | tf_op jit(solution)/shard_map/ppermute | solution.py:35
  414.5 10.8 collective-permute-start.13
  423.4 3.2 collective-permute-start.12
  429.9 5.3 copy-start.8
  430.0 3.9 collective-permute-start.14
  432.0 4.9 copy-start.7
  435.1 644.6 %all-reduce.17.cloned.1.call-start = ((), (), s32[]{:S(2)}) async-start(), calls=%async_computation.4 | async-start | bytes 786432 | tf_op jit(solution)/shard_map/psum | solution.py:23
  443.3 95.0 %copy-start.6 = (bf16[2,256]{1,0:T(2,128)(2,1)S(1)}, bf16[2,256]{1,0:T(2,128)(2,1)}, u32[]{:S(2)}) copy-start(bf16[2,256]{1,0:T(2,128)(2,1)} %param.16) | copy-start | bytes 3076
  443.3 95.0 %copy-start.9 = (bf16[4,256,48]{1,2,0:T(8,128)(2,1)S(1)}, bf16[4,256,48]{1,2,0:T(8,128)(2,1)}, u32[]{:S(2)}) copy-start(bf16[4,256,48]{1,2,0:T(8,128)(2,1)} %param.18) | copy-start | bytes 294916
  443.3 637.4 %copy-start.4 = (bf16[2,256,48]{1,2,0:T(8,128)(2,1)S(1)}, bf16[2,256,48]{1,2,0:T(8,128)(2,1)}, u32[]{:S(2)}) copy-start(bf16[2,256,48]{1,2,0:T(8,128)(2,1)} %param.17) | copy-start | bytes 147460
  538.2 634.0 %all-reduce.19.cloned.1.call-start = ((), (), s32[]{:S(2)}) async-start(), calls=%async_computation.5 | async-start | bytes 200704 | tf_op jit(solution)/shard_map/psum | solution.py:95
Sparse Core Ops, SparseCore 0:
  35.2 80.7 all-reduce.8
  156.5 99.6 all-reduce.10
  296.7 99.5 all-reduce.12
  435.2 99.7 all-reduce.14
  538.9 540.6 all-reduce.16
  1095.7 76.4 all-reduce.18
where the time goes:
time: 1190 us
  waiting for transfers between devices  1020 us (86%)
  starting transfers between devices  63.7 us (5%)
  matrix products  36.5 us (3%)
  other arithmetic  35.7 us (3%)
  local copies, waits for them, and re-layouts  19.2 us (2%)
  between operations  14.7 us (1%)
    psum x1, waiting for transfers between devices, broadcast(): return lax.psum(kept, axis)  541 us
    psum x4, waiting for transfers between devices, body(): produced = rows_f + lax.psum(update_terms, 'tp')  372 us
    psum x1, waiting for transfers between devices, talker_rows(): lax.psum(embedded.astype(jnp.bfloat16), 'tp').astype(jnp.float32)  76.6 us
    ppermute x12, starting transfers between devices, swapped(): return lax.ppermute(value, axis, pairs)  50.4 us
  transfers between devices with their start and end apart: 21, of which 15 were waited for; matrix products, arithmetic and copies ran while one was open for 3% of the time, Pallas kernels for 0%

commit v1 on v0

v1 whole, which is shorter than its diff:
```python
import functools

import jax
import jax.numpy as jnp
from jax import lax
from jax.experimental import pallas as pl
from jax.experimental.pallas import tpu as pltpu
from jax.sharding import PartitionSpec as P

D = 4096
H = 32
KVH = 8
HD = 64
NQ = 4
TICKS = 4
B = 96
CACHE = 16
HALF = B // 2
RATIO = H // KVH

epsilon = 1e-05
f32 = jnp.float32
bf16 = jnp.bfloat16
VMEM = pltpu.VMEM


def section_core(tick, scaled, total_squares, hi_ref, w_own, w_oth, o_own, o_oth, cache_ref, out_ref):
    shards, block = out_ref.shape[0], out_ref.shape[2] // 2
    proj = jnp.zeros((HALF, w_own.shape[1]), f32)
    for own_rows, oth_rows, low, high in scaled:
        proj = proj + jnp.dot(own_rows, w_own[low:high, :], preferred_element_type=f32)
        proj = proj + jnp.dot(oth_rows, w_oth[low:high, :], preferred_element_type=f32)
    proj = proj * lax.rsqrt(total_squares / D + epsilon)
    stacked = jnp.concatenate([proj[:, r * HD : (r + 1) * HD] for r in range(RATIO)], axis=0)
    queries = (stacked.astype(bf16).astype(f32) * (HD**-0.5)).astype(bf16)
    queries = jnp.concatenate([queries, jnp.zeros_like(queries)], axis=1)
    pair_new = proj[:, RATIO * HD :].astype(bf16)
    pairs = cache_ref[tick]
    contract_last = (((1,), (1,)), ((), ()))
    scores = lax.dot_general(queries, pairs, contract_last, preferred_element_type=f32)
    own_scores = lax.dot_general(queries, pair_new, contract_last, preferred_element_type=f32)
    rows = RATIO * HALF
    stream = lax.rem(lax.broadcasted_iota(jnp.int32, (rows, 1), 0), HALF)
    place = lax.broadcasted_iota(jnp.int32, (rows, HALF * CACHE), 1)
    visible = jnp.logical_and(place >= stream * CACHE, place < hi_ref[tick])
    scores = jnp.where(visible, scores, -jnp.inf)
    own_place = lax.broadcasted_iota(jnp.int32, (rows, HALF), 1)
    own_scores = jnp.where(own_place == stream, own_scores, -jnp.inf)
    row_max = jnp.maximum(
        jnp.max(scores, axis=-1, keepdims=True), jnp.max(own_scores, axis=-1, keepdims=True)
    )
    weights = jnp.exp(scores - row_max)
    own_weights = jnp.exp(own_scores - row_max)
    total = jnp.sum(weights, axis=-1, keepdims=True) + jnp.sum(own_weights, axis=-1, keepdims=True)
    share = 1.0 / total
    mixed = jnp.dot((weights * share).astype(bf16), pairs, preferred_element_type=f32)
    mixed = mixed + jnp.dot(
        (own_weights * share).astype(bf16), pair_new, preferred_element_type=f32
    )
    mixed = mixed[:, HD:].astype(bf16)
    heads = jnp.concatenate([mixed[r * HALF : (r + 1) * HALF] for r in range(RATIO)], axis=1)
    for j in range(shards):
        span = slice(j * block, (j + 1) * block)
        out_ref[j, :, :block] = jnp.dot(heads, o_own[:, span], preferred_element_type=f32).astype(
            bf16
        )
        out_ref[j, :, block:] = jnp.dot(heads, o_oth[:, span], preferred_element_type=f32).astype(
            bf16
        )


def first_kernel(
    tick, x_own, x_oth, g_own, g_oth, hi_ref, w_own, w_oth, o_own, o_oth, cache_ref, out_ref
):
    own = x_own[...].astype(f32)
    oth = x_oth[...].astype(f32)
    squares = jnp.sum(own * own + oth * oth, axis=-1, keepdims=True)
    scaled_own = (own * g_own[...]).astype(bf16)
    scaled_oth = (oth * g_oth[...]).astype(bf16)
    scaled = [(scaled_own, scaled_oth, 0, x_own.shape[1])]
    section_core(
        tick, scaled, squares, hi_ref, w_own, w_oth, o_own, o_oth, cache_ref, out_ref
    )


def later_kernel(tick, x_ref, inverse_gain, hi_ref, w_own, w_oth, o_own, o_oth, cache_ref, out_ref):
    shards, block = x_ref.shape[0], x_ref.shape[2] // 2
    squares = jnp.zeros(x_ref.shape[1:], f32)
    scaled = []
    for j in range(shards):
        rows = x_ref[j]
        plain = rows.astype(f32) * inverse_gain[j : j + 1, :]
        squares = squares + plain * plain
        scaled.append((rows[:, :block], rows[:, block:], j * block, (j + 1) * block))
    squares = jnp.sum(squares, axis=-1, keepdims=True)
    section_core(
        tick, scaled, squares, hi_ref, w_own, w_oth, o_own, o_oth, cache_ref, out_ref
    )


def run_kernel(kernel, shards, block, *operands):
    return pl.pallas_call(
        kernel,
        out_shape=jax.ShapeDtypeStruct((shards, HALF, 2 * block), bf16),
        in_specs=[pl.BlockSpec(memory_space=VMEM)] * len(operands),
        out_specs=pl.BlockSpec(memory_space=VMEM),
        compiler_params=pltpu.CompilerParams(vmem_limit_bytes=32 * 2**20),
    )(*operands)


def to_partner(value):
    pairs = [(i, i ^ 1) for i in range(lax.axis_size("section"))]
    return lax.ppermute(value, "section", pairs)


def to_next(value):
    count = lax.axis_size("section")
    return lax.ppermute(value, "section", [(i, i + 2) for i in range(count - 2)])


def exchange(blocks):
    return lax.all_to_all(blocks, "tp", 0, 0, tiled=True)


def gather(block):
    count = lax.axis_size("tp")
    return exchange(jnp.broadcast_to(block[None], (count,) + block.shape))


def from_last(value, position):
    count = lax.axis_size("section")
    line = 8
    base = count - line
    total = jnp.where(position // 2 == count // 2 - 1, value, jnp.zeros_like(value))
    for z in range(0, line - 2, 2):
        total = total + lax.ppermute(
            value, "section", [(count - 2 + c, base + z + c) for c in range(2)]
        )
    result = jnp.where(position >= base, total, jnp.zeros_like(value))
    for start in range(0, base, line):
        result = result + lax.ppermute(
            total, "section", [(base + i, start + i) for i in range(line)]
        )
    return result


def body(arriving, norm_gain, w_qkv, w_out, cache, lengths, talk_gain, w_adapt, codebooks, codes):
    position = lax.axis_index("section")
    column = lax.axis_index("tp")
    shards = lax.axis_size("tp")
    side = lax.rem(position, 2)
    section = position // 2
    width = arriving.shape[2]
    block = width // shards

    rows = arriving[0]
    mine = lax.dynamic_slice_in_dim(rows, side * HALF, HALF, 0)
    theirs = lax.dynamic_slice_in_dim(rows, (1 - side) * HALF, HALF, 0)
    got = to_partner(jnp.concatenate([theirs, norm_gain], axis=0))
    w_own = w_qkv[0]
    w_oth = to_partner(w_own)
    o_own = w_out[0]
    o_oth = to_partner(o_own)
    x_oth = got[:HALF]
    g_own = norm_gain.astype(f32)
    g_oth = got[HALF:].astype(f32)
    cache_rows = cache[0].reshape(TICKS, HALF * CACHE, -1)

    batches = jnp.maximum(section - jnp.arange(TICKS, dtype=jnp.int32), 0)
    lens = lax.dynamic_slice_in_dim(lengths, side * HALF, HALF, 1)[batches]
    hi = lens + jnp.arange(HALF, dtype=jnp.int32)[None, :] * CACHE
    hi = jnp.tile(hi, (1, RATIO))[:, :, None]

    gains = jnp.concatenate([g_own.reshape(shards, block), g_oth.reshape(shards, block)], axis=1)
    inverse_gains = 1.0 / gains
    my_gain = lax.dynamic_slice_in_dim(gains, column, 1, 0)
    x_shard = jnp.concatenate(
        [
            lax.dynamic_slice_in_dim(mine, column * block, block, 1),
            lax.dynamic_slice_in_dim(x_oth, column * block, block, 1),
        ],
        axis=1,
    ).astype(f32)

    shared = (hi, w_own, w_oth, o_own, o_oth, cache_rows)
    latest = None
    finals = []
    for tick in range(TICKS):
        if tick == 0:
            terms = run_kernel(
                functools.partial(first_kernel, tick),
                shards, block, mine, x_oth, g_own, g_oth, *shared,
            )
        else:
            scaled = gather((x_shard * my_gain).astype(bf16))
            terms = run_kernel(
                functools.partial(later_kernel, tick),
                shards, block, scaled, inverse_gains, *shared,
            )
        produced = x_shard + jnp.sum(exchange(terms).astype(f32), axis=0)
        latest = produced if tick == 0 else jnp.where(section >= tick, produced, latest)
        rounded = produced.astype(bf16)
        finals.append(rounded)
        if tick + 1 < TICKS:
            x_shard = to_next(rounded).astype(f32)

    def whole_rows(value):
        other = to_partner(value)
        other = jnp.concatenate([other[..., block:], other[..., :block]], axis=-1)
        first = jnp.where(side == 0, value, other)
        second = jnp.where(side == 0, other, value)
        return jnp.concatenate([first, second], axis=-2)

    last_rows = whole_rows(latest.astype(bf16))
    leaving = gather(last_rows[:, :block])
    leaving = leaving.transpose(1, 0, 2).reshape(B, width).astype(f32)

    early = whole_rows(from_last(jnp.stack(finals[:-1]), position))
    final = from_last(last_rows, position)
    talk_rows = jnp.concatenate([early, final[None]], axis=0).astype(f32).reshape(TICKS * B, -1)
    squares = jnp.sum(talk_rows * talk_rows, axis=-1)
    ordered_gain = jnp.where(side == 0, talk_gain, talk_gain[::-1]).astype(f32).reshape(-1)
    ordered_adapt = jnp.where(side == 0, w_adapt, w_adapt[::-1]).reshape(2 * block, -1)
    adapted = jnp.dot(
        (talk_rows * ordered_gain).astype(bf16), ordered_adapt, preferred_element_type=f32
    )
    entries = codebooks.shape[1]
    local_ids = codes.reshape(TICKS * B, NQ) - column * entries
    one_hot = local_ids[:, :, None] == jnp.arange(entries, dtype=jnp.int32)
    one_hot = one_hot.astype(bf16).reshape(TICKS * B, NQ * entries)
    embedded = jnp.dot(
        one_hot, codebooks.reshape(NQ * entries, -1), preferred_element_type=f32
    )
    squares_high = squares.astype(bf16)
    squares_low = (squares - squares_high.astype(f32)).astype(bf16)
    columns = adapted.shape[1]
    payload = jnp.concatenate(
        [
            adapted.astype(bf16),
            embedded.astype(bf16),
            squares_high[:, None],
            squares_low[:, None],
            jnp.zeros((TICKS * B, 126 - 2 * columns), bf16),
        ],
        axis=1,
    )
    sums = jnp.sum(gather(payload).astype(f32), axis=0)
    talk_squares = sums[:, 2 * columns : 2 * columns + 1] + sums[:, 2 * columns + 1 : 2 * columns + 2]
    talk_rms = lax.rsqrt(talk_squares / D + epsilon)
    talk = sums[:, :columns] * talk_rms + sums[:, columns : 2 * columns]
    return (leaving[None], talk.reshape(TICKS, B, columns))


def solution(mesh):
    placed = (
        P("section", None, None),
        P("section", None),
        P("section", None, "tp"),
        P("section", "tp", None),
        P("section", None, None, None, "tp"),
        P(),
        P(None, "tp"),
        P(None, "tp", "section"),
        P(None, "tp", "section"),
        P(),
    )
    return jax.shard_map(
        body,
        mesh=mesh,
        in_specs=placed,
        out_specs=(P("section", None, None), P(None, None, "section")),
        check_vma=False,
    )
```

time: 1190 us -> 238 us (0.20)
  the two profiles are of different devices: /device:TPU:1 before, /device:TPU:56 now
where the time goes in v1:
time: 238 us; the launch traced here: 235 us
  starting transfers between devices  79.8 us (34%)
  waiting for transfers between devices  60.5 us (25%)
  local copies, waits for them, and re-layouts  33.6 us (14%)
  blocking collectives  31.7 us (13%)
  Pallas kernels  13.5 us (6%)
  other arithmetic  12.5 us (5%)
    all_to_all x3, blocking collectives, exchange(): return lax.all_to_all(blocks, 'tp', 0, 0, tiled=True)  31.7 us
    all_to_all x6, starting transfers between devices, exchange(): return lax.all_to_all(blocks, 'tp', 0, 0, tiled=True)  31.4 us
    all_to_all x6, waiting for transfers between devices, exchange(): return lax.all_to_all(blocks, 'tp', 0, 0, tiled=True)  30.6 us
    ppermute x14, starting transfers between devices, from_last(): lax.ppermute(total, 'section', [(base + i, start + i) for i in range(line)])  21.7 us
    ppermute x3, waiting for transfers between devices, to_next(): lax.ppermute(value, 'section', [(i, i + 2) for i in range(count - 2)])  20.9 us
    unnamed x81, local copies, waits for them, and re-layouts  15.8 us
    pallas_call x4, Pallas kernels, run_kernel(): pl.pallas_call(kernel, out_shape=jax.ShapeDtypeStruct((shards, HALF, 2 *...  13.5 us
    ppermute x5, starting transfers between devices, to_partner(): return lax.ppermute(value, 'section', pairs)  10.2 us
  transfers between devices with their start and end apart: 34, of which 9 were waited for; matrix products, arithmetic and copies ran while one was open for 11% of the time, Pallas kernels for 1%

profile of v1, /device:TPU:56, one launch (start us, length us, event | category | flops | bytes accessed | tf_op | source)
XLA Modules:
  0.0 235.3 jit_solution(5378164019824227549)
XLA Ops:
  0.7 2.1 collective-permute-start.1
  2.7 1.7 dynamic-slice_bitcast_fusion.1
  4.5 1.4 pad_maximum_fusion.1
  5.9 2.4 %collective-permute-start = (bf16[49,2048]{1,0:T(8,128)(2,1)}, bf16[49,2048]{1,0:T(8,128)(2,1)}, u32[]{:S(2)}, u32[]{:S(2)}) collective-permute-start(bf16[49,2048]{1,0:T(8,128)(2,1)} %pad_maximum_fusion.1), channel_id=1, source_target_pairs={{0,8},{8,0},{16,24},{24,16},{32,40},{40,32},{48,56},{56,48},{64,72... | collective-permute-start | bytes 602120 | tf_op jit(solution)/shard_map/ppermute | solution.py:113
  8.3 1.9 collective-permute-start.2
  15.0 1.2 copy-done.2
  16.2 1.1 copy-done.5
  19.3 3.3 %shard_map.113 = bf16[8,48,512]{2,1,0:T(8,128)(2,1)S(1)} custom-call(bf16[48,2048]{1,0:T(8,128)(2,1)S(1)} %copy-done.13, bf16[48,2048]{1,0:T(8,128)(2,1)S(1)} %slice.46.x_oth, f32[1,2048]{1,0:T(1,128)S(1)} %convert_element_type.155.g_own, f32[1,2048]{1,0:T(1,128)S(1)} %slice_convert_fusion.g_oth, s32[4,192,1]{2,1,0:T(8,128)S(1)} %copy-done.8, ...), custom_call_target="tpu_custom_call" | custom-call | tf_op jit(solution)/shard_map/pallas_call | solution.py:102
  23.4 6.1 %all-to-all-start = ((bf16[8,48,512]{2,1,0:T(8,128)(2,1)}), bf16[8,48,512]{2,1,0:T(8,128)(2,1)}, u32[]{:S(2)}, u32[]{:S(2)}) async-start(bf16[8,48,512]{2,1,0:T(8,128)(2,1)} %copy-done.12), calls=%async_computation | async-start | bytes 786432 | tf_op jit(solution)/shard_map/all_to_all | solution.py:122
  29.5 1.5 fusion.28
  32.4 6.0 %all-to-all-done = bf16[8,48,512]{2,1,0:T(8,128)(2,1)} async-done(((bf16[8,48,512]{2,1,0:T(8,128)(2,1)}), bf16[8,48,512]{2,1,0:T(8,128)(2,1)}, u32[]{:S(2)}, u32[]{:S(2)}) %all-to-all-start) | async-done | bytes 393248 | tf_op jit(solution)/shard_map/all_to_all | solution.py:122
  38.4 1.1 convert_reduce_fusion.4
  40.3 6.1 %collective-permute-start.3 = (bf16[48,512]{1,0:T(8,128)(2,1)S(1)}, bf16[48,512]{1,0:T(8,128)(2,1)S(1)}, u32[]{:S(2)}, u32[]{:S(2)}) collective-permute-start(bf16[48,512]{1,0:T(8,128)(2,1)S(1)} %fusion.16), channel_id=1, source_target_pairs={{0,16},{8,24},{16,32},{24,40},{32,48},{40,56},{48,64},{56,72},{64,... | collective-permute-start | bytes 147464 | tf_op jit(solution)/shard_map/ppermute | solution.py:118
  46.4 7.3 %collective-permute-done.3 = bf16[48,512]{1,0:T(8,128)(2,1)S(1)} collective-permute-done((bf16[48,512]{1,0:T(8,128)(2,1)S(1)}, bf16[48,512]{1,0:T(8,128)(2,1)S(1)}, u32[]{:S(2)}, u32[]{:S(2)}) %collective-permute-start.3) | collective-permute-done | bytes 49184 | tf_op jit(solution)/shard_map/ppermute | solution.py:118
  55.1 4.1 %all-to-all-start.1 = ((bf16[8,48,512]{2,1,0:T(8,128)(2,1)}), bf16[8,48,512]{2,1,0:T(8,128)(2,1)}, u32[]{:S(2)}, u32[]{:S(2)}) async-start(bf16[8,48,512]{2,1,0:T(8,128)(2,1)} %broadcast_in_dim.14), calls=%async_computation.1 | async-start | bytes 786432 | tf_op jit(solution)/shard_map/all_to_all | solution.py:122
  59.9 7.0 %all-to-all-done.1.x_ref = bf16[8,48,512]{2,1,0:T(8,128)(2,1)} async-done(((bf16[8,48,512]{2,1,0:T(8,128)(2,1)}), bf16[8,48,512]{2,1,0:T(8,128)(2,1)}, u32[]{:S(2)}, u32[]{:S(2)}) %all-to-all-start.1) | async-done | bytes 393248 | tf_op jit(solution)/shard_map/all_to_all | solution.py:122
  67.0 1.2 copy-done.3
  68.2 1.1 copy-done.6
  70.3 3.4 %shard_map.114 = bf16[8,48,512]{2,1,0:T(8,128)(2,1)S(1)} custom-call(bf16[8,48,512]{2,1,0:T(8,128)(2,1)} %all-to-all-done.1.x_ref, f32[8,512]{1,0:T(8,128)S(1)} %broadcast_divide_fusion.inverse_gain, s32[4,192,1]{2,1,0:T(8,128)S(1)} %copy-done.9, bf16[2048,384]{1,0:T(8,128)(2,1)S(1)} %bitcast.45, bf16[2048,384]{1,0:T(8,128)(2,1)S(1)} %collective-permute-done.1.w_oth, ...), custom_call_target="tpu_custom_call" | custom-call | tf_op jit(solution)/shard_map/pallas_call | solution.py:102
  73.8 10.7 %all_to_all.45 = bf16[8,48,512]{2,1,0:T(8,128)(2,1)S(1)} all-to-all(bf16[8,48,512]{2,1,0:T(8,128)(2,1)S(1)} %shard_map.114), channel_id=1, replica_groups=mesh['section'=64,'tp'=8] {'tp'}, dimensions={0} | all-to-all | bytes 786432 | tf_op jit(solution)/shard_map/all_to_all | solution.py:122
  84.6 1.9 collective-permute-start.4
  86.5 7.2 %collective-permute-done.4 = bf16[48,512]{1,0:T(8,128)(2,1)S(1)} collective-permute-done((bf16[48,512]{1,0:T(8,128)(2,1)S(1)}, bf16[48,512]{1,0:T(8,128)(2,1)S(1)}, u32[]{:S(2)}, u32[]{:S(2)}) %collective-permute-start.4) | collective-permute-done | bytes 49184 | tf_op jit(solution)/shard_map/ppermute | solution.py:118
  93.8 10.4 %all_to_all.46.x_ref = bf16[8,48,512]{2,1,0:T(8,128)(2,1)S(1)} all-to-all(bf16[8,48,512]{2,1,0:T(8,128)(2,1)S(1)} %broadcast_in_dim.15), channel_id=1, replica_groups=mesh['section'=64,'tp'=8] {'tp'}, dimensions={0} | all-to-all | bytes 786432 | tf_op jit(solution)/shard_map/all_to_all | solution.py:122
  104.2 3.3 %shard_map.115 = bf16[8,48,512]{2,1,0:T(8,128)(2,1)S(1)} custom-call(bf16[8,48,512]{2,1,0:T(8,128)(2,1)S(1)} %all_to_all.46.x_ref, f32[8,512]{1,0:T(8,128)S(1)} %broadcast_divide_fusion.inverse_gain, s32[4,192,1]{2,1,0:T(8,128)S(1)} %copy-done.9, bf16[2048,384]{1,0:T(8,128)(2,1)S(1)} %bitcast.46, bf16[2048,384]{1,0:T(8,128)(2,1)S(1)} %collective-permute-done.1.w_oth, ...), custom_call_target="tpu_custom_call" | custom-call | tf_op jit(solution)/shard_map/pallas_call | solution.py:102
  107.5 10.5 %all_to_all.47 = bf16[8,48,512]{2,1,0:T(8,128)(2,1)S(1)} all-to-all(bf16[8,48,512]{2,1,0:T(8,128)(2,1)S(1)} %shard_map.115), channel_id=1, replica_groups=mesh['section'=64,'tp'=8] {'tp'}, dimensions={0} | all-to-all | bytes 786432 | tf_op jit(solution)/shard_map/all_to_all | solution.py:122
  119.4 1.9 collective-permute-start.5
  121.9 6.5 %collective-permute-done.5 = bf16[48,512]{1,0:T(8,128)(2,1)S(1)} collective-permute-done((bf16[48,512]{1,0:T(8,128)(2,1)S(1)}, bf16[48,512]{1,0:T(8,128)(2,1)S(1)}, u32[]{:S(2)}, u32[]{:S(2)}) %collective-permute-start.5) | collective-permute-done | bytes 49184 | tf_op jit(solution)/shard_map/ppermute | solution.py:118
  129.8 4.1 %all-to-all-start.5 = ((bf16[8,48,512]{2,1,0:T(8,128)(2,1)}), bf16[8,48,512]{2,1,0:T(8,128)(2,1)}, u32[]{:S(2)}, u32[]{:S(2)}) async-start(bf16[8,48,512]{2,1,0:T(8,128)(2,1)} %broadcast_in_dim.16), calls=%async_computation.5 | async-start | bytes 786432 | tf_op jit(solution)/shard_map/all_to_all | solution.py:122
  133.9 1.5 constant_dynamic-slice_fusion.3
  135.3 1.2 rev.6
  136.5 1.3 copy.44
  137.8 1.4 sub.51
  139.2 1.7 fusion.2
  141.7 1.5 pad_maximum_fusion.2
  143.3 1.3 collective-permute-start.9
  144.6 1.3 collective-permute-start.8
  145.9 1.3 collective-permute-start.7
  147.2 1.2 copy-done.4
  148.5 1.1 copy-done.7
  150.6 3.4 %shard_map.116 = bf16[8,48,512]{2,1,0:T(8,128)(2,1)S(1)} custom-call(bf16[8,48,512]{2,1,0:T(8,128)(2,1)} %all-to-all-done.5.x_ref, f32[8,512]{1,0:T(8,128)S(1)} %broadcast_divide_fusion.inverse_gain, s32[4,192,1]{2,1,0:T(8,128)S(1)} %copy-done.10, bf16[2048,384]{1,0:T(8,128)(2,1)S(1)} %bitcast.47, bf16[2048,384]{1,0:T(8,128)(2,1)S(1)} %collective-permute-done.1.w_oth, ...), custom_call_target="tpu_custom_call" | custom-call | tf_op jit(solution)/shard_map/pallas_call | solution.py:102
  154.8 5.7 %all-to-all-start.6 = ((bf16[8,48,512]{2,1,0:T(8,128)(2,1)}), bf16[8,48,512]{2,1,0:T(8,128)(2,1)S(1)}, u32[]{:S(2)}, u32[]{:S(2)}) async-start(bf16[8,48,512]{2,1,0:T(8,128)(2,1)} %copy-done.11), calls=%async_computation.6 | async-start | bytes 786432 | tf_op jit(solution)/shard_map/all_to_all | solution.py:122
  161.5 1.1 add_add_fusion.1
  162.6 3.3 %collective-permute-start.16 = (bf16[3,48,512]{2,1,0:T(8,128)(2,1)S(1)}, bf16[3,48,512]{2,1,0:T(8,128)(2,1)S(1)}, u32[]{:S(2)}, u32[]{:S(2)}) collective-permute-start(bf16[3,48,512]{2,1,0:T(8,128)(2,1)S(1)} %add_add_fusion.1), channel_id=1, source_target_pairs={{448,384},{456,392},{464,400},{472,408},{480,416},{488,424},{496,4... | collective-permute-start | bytes 442376 | tf_op jit(solution)/shard_map/ppermute | solution.py:141
  165.9 1.5 collective-permute-start.15
  167.4 2.7 %collective-permute-start.14 = (bf16[3,48,512]{2,1,0:T(8,128)(2,1)S(1)}, bf16[3,48,512]{2,1,0:T(8,128)(2,1)S(1)}, u32[]{:S(2)}, u32[]{:S(2)}) collective-permute-start(bf16[3,48,512]{2,1,0:T(8,128)(2,1)S(1)} %add_add_fusion.1), channel_id=1, source_target_pairs={{448,256},{456,264},{464,272},{472,280},{480,288},{488,296},{496,3... | collective-permute-start | bytes 442376 | tf_op jit(solution)/shard_map/ppermute | solution.py:141
  170.2 1.3 collective-permute-start.13
  171.5 1.3 collective-permute-start.12
  172.8 1.3 collective-permute-start.11
  174.2 1.3 collective-permute-start.10
  175.6 1.9 collective-permute-start.6
  178.6 1.9 collective-permute-start.17
  182.0 1.3 collective-permute-start.18
  183.3 7.9 %collective-permute-done.18 = bf16[96,512]{1,0:T(8,128)(2,1)S(1)} collective-permute-done((bf16[96,512]{1,0:T(8,128)(2,1)S(1)}, bf16[96,512]{1,0:T(8,128)(2,1)S(1)}, u32[]{:S(2)}, u32[]{:S(2)}) %collective-permute-start.18) | collective-permute-done | bytes 98336 | tf_op jit(solution)/shard_map/ppermute | solution.py:136
  191.3 1.3 collective-permute-start.27
  192.6 1.3 collective-permute-start.26
  194.0 1.3 collective-permute-start.25
  195.3 1.3 collective-permute-start.24
  196.6 1.3 collective-permute-start.23
  197.9 1.3 collective-permute-start.22
  199.2 1.3 collective-permute-start.21
  201.3 7.8 %all-to-all-start.7 = ((bf16[8,96,256]{2,1,0:T(8,128)(2,1)}), bf16[8,96,256]{2,1,0:T(8,128)(2,1)S(1)}, u32[]{:S(2)}, u32[]{:S(2)}) async-start(bf16[8,96,256]{2,1,0:T(8,128)(2,1)} %broadcast_in_dim.17), calls=%async_computation.7 | async-start | bytes 786432 | tf_op jit(solution)/shard_map/all_to_all | solution.py:122
  210.3 7.5 %all-to-all-done.7 = bf16[8,96,256]{2,1,0:T(8,128)(2,1)S(1)} async-done(((bf16[8,96,256]{2,1,0:T(8,128)(2,1)}), bf16[8,96,256]{2,1,0:T(8,128)(2,1)S(1)}, u32[]{:S(2)}, u32[]{:S(2)}) %all-to-all-start.7) | async-done | bytes 393248 | tf_op jit(solution)/shard_map/all_to_all | solution.py:122
  218.8 3.5 %all-to-all-start.8 = ((bf16[8,384,128]{2,1,0:T(8,128)(2,1)}), bf16[8,384,128]{2,1,0:T(8,128)(2,1)S(1)}, u32[]{:S(2)}, u32[]{:S(2)}) async-start(bf16[8,384,128]{2,1,0:T(8,128)(2,1)} %broadcast_in_dim.20), calls=%async_computation.8 | async-start | bytes 1572864 | tf_op jit(solution)/shard_map/all_to_all | solution.py:122
  223.9 10.1 %all-to-all-done.8 = bf16[8,384,128]{2,1,0:T(8,128)(2,1)S(1)} async-done(((bf16[8,384,128]{2,1,0:T(8,128)(2,1)}), bf16[8,384,128]{2,1,0:T(8,128)(2,1)S(1)}, u32[]{:S(2)}, u32[]{:S(2)}) %all-to-all-start.8) | async-done | bytes 786464 | tf_op jit(solution)/shard_map/all_to_all | solution.py:122
  (165 shorter events, 28.0 us)
Async XLA Ops:
  0.6 138.6 %copy-start = (bf16[4,256,48]{1,2,0:T(8,128)(2,1)S(1)}, bf16[4,256,48]{1,2,0:T(8,128)(2,1)}, u32[]{:S(2)}) copy-start(bf16[4,256,48]{1,2,0:T(8,128)(2,1)} %param.18) | copy-start | bytes 294916
  0.6 14.3 %copy-start.1 = (bf16[1,2048,384]{2,1,0:T(8,128)(2,1)S(1)}, bf16[1,2048,384]{2,1,0:T(8,128)(2,1)}, u32[]{:S(2)}) copy-start(bf16[1,2048,384]{2,1,0:T(8,128)(2,1)} %param.12) | copy-start | bytes 4718596
  0.7 14.3 %collective-permute-start.1 = (bf16[2048,384]{1,0:T(8,128)(2,1)}, bf16[2048,384]{1,0:T(8,128)(2,1)S(1)}, u32[]{:S(2)}, u32[]{:S(2)}) collective-permute-start(bf16[2048,384]{1,0:T(8,128)(2,1)} %bitcast.43), channel_id=1, source_target_pairs={{0,8},{8,0},{16,24},{24,16},{32,40},{40,32},{48,56},{56,48},{64,72... | collective-permute-start | bytes 4718600 | tf_op jit(solution)/shard_map/ppermute | solution.py:113
  5.9 7.4 %collective-permute-start = (bf16[49,2048]{1,0:T(8,128)(2,1)}, bf16[49,2048]{1,0:T(8,128)(2,1)}, u32[]{:S(2)}, u32[]{:S(2)}) collective-permute-start(bf16[49,2048]{1,0:T(8,128)(2,1)} %pad_maximum_fusion.1), channel_id=1, source_target_pairs={{0,8},{8,0},{16,24},{24,16},{32,40},{40,32},{48,56},{56,48},{64,72... | collective-permute-start | bytes 602120 | tf_op jit(solution)/shard_map/ppermute | solution.py:113
  8.3 6.7 %collective-permute-start.2 = (bf16[256,2048]{1,0:T(8,128)(2,1)}, bf16[256,2048]{1,0:T(8,128)(2,1)}, u32[]{:S(2)}, u32[]{:S(2)}) collective-permute-start(bf16[256,2048]{1,0:T(8,128)(2,1)} %bitcast.48), channel_id=1, source_target_pairs={{0,8},{8,0},{16,24},{24,16},{32,40},{40,32},{48,56},{56,48},{64,72... | collective-permute-start | bytes 3145736 | tf_op jit(solution)/shard_map/ppermute | solution.py:113
  15.0 1.2 copy-start.2
  16.2 1.1 copy-start.5
  17.4 1.0 copy-start.8
  19.3 10.2 %copy-start.31 = (bf16[1,2048]{1,0:T(2,128)(2,1)S(1)}, bf16[1,2048]{1,0:T(2,128)(2,1)}, u32[]{:S(2)}) copy-start(bf16[1,2048]{1,0:T(2,128)(2,1)} %param.11) | copy-start | bytes 12292
  23.4 15.1 %all-to-all-start = ((bf16[8,48,512]{2,1,0:T(8,128)(2,1)}), bf16[8,48,512]{2,1,0:T(8,128)(2,1)}, u32[]{:S(2)}, u32[]{:S(2)}) async-start(bf16[8,48,512]{2,1,0:T(8,128)(2,1)} %copy-done.12), calls=%async_computation | async-start | bytes 786432 | tf_op jit(solution)/shard_map/all_to_all | solution.py:122
  31.8 23.3 %copy-start.32 = (f32[8,512]{1,0:T(8,128)}, f32[8,512]{1,0:T(8,128)S(1)}, u32[]{:S(2)}) copy-start(f32[8,512]{1,0:T(8,128)S(1)} %constant_dynamic-update-slice_fusion) | copy-start | bytes 49156
  40.3 13.4 %collective-permute-start.3 = (bf16[48,512]{1,0:T(8,128)(2,1)S(1)}, bf16[48,512]{1,0:T(8,128)(2,1)S(1)}, u32[]{:S(2)}, u32[]{:S(2)}) collective-permute-start(bf16[48,512]{1,0:T(8,128)(2,1)S(1)} %fusion.16), channel_id=1, source_target_pairs={{0,16},{8,24},{16,32},{24,40},{32,48},{40,56},{48,64},{56,72},{64,... | collective-permute-start | bytes 147464 | tf_op jit(solution)/shard_map/ppermute | solution.py:118
  46.4 7.3 %copy-start.34 = (f32[1,512]{1,0:T(1,128)}, f32[1,512]{1,0:T(1,128)S(1)}, u32[]{:S(2)}) copy-start(f32[1,512]{1,0:T(1,128)S(1)} %constant_dynamic-slice_fusion) | copy-start | bytes 6148
  55.1 11.9 %all-to-all-start.1 = ((bf16[8,48,512]{2,1,0:T(8,128)(2,1)}), bf16[8,48,512]{2,1,0:T(8,128)(2,1)}, u32[]{:S(2)}, u32[]{:S(2)}) async-start(bf16[8,48,512]{2,1,0:T(8,128)(2,1)} %broadcast_in_dim.14), calls=%async_computation.1 | async-start | bytes 786432 | tf_op jit(solution)/shard_map/all_to_all | solution.py:122
  67.0 1.2 copy-start.3
  68.2 1.1 copy-start.6
  70.3 14.2 %copy-start.19 = (bf16[48,512]{1,0:T(8,128)(2,1)S(1)}, bf16[48,512]{1,0:T(8,128)(2,1)}, u32[]{:S(2)}) copy-start(bf16[48,512]{1,0:T(8,128)(2,1)} %copy-done.18) | copy-start | bytes 147460
  70.3 23.4 %copy-start.35 = (f32[1,512]{1,0:T(1,128)S(1)}, f32[1,512]{1,0:T(1,128)}, u32[]{:S(2)}) copy-start(f32[1,512]{1,0:T(1,128)} %copy-done.34) | copy-start | bytes 6148
  84.5 9.2 %copy-start.14 = (f32[48,512]{1,0:T(8,128)}, f32[48,512]{1,0:T(8,128)S(1)}, u32[]{:S(2)}) copy-start(f32[48,512]{1,0:T(8,128)S(1)} %convert_reduce_fusion.3) | copy-start | bytes 294916
  84.6 9.1 %copy-start.23 = (bf16[48,512]{1,0:T(8,128)(2,1)}, bf16[48,512]{1,0:T(8,128)(2,1)S(1)}, u32[]{:S(2)}) copy-start(bf16[48,512]{1,0:T(8,128)(2,1)S(1)} %fusion.17) | copy-start | bytes 147460
  84.6 9.1 %collective-permute-start.4 = (bf16[48,512]{1,0:T(8,128)(2,1)S(1)}, bf16[48,512]{1,0:T(8,128)(2,1)S(1)}, u32[]{:S(2)}, u32[]{:S(2)}) collective-permute-start(bf16[48,512]{1,0:T(8,128)(2,1)S(1)} %fusion.17), channel_id=1, source_target_pairs={{0,16},{8,24},{16,32},{24,40},{32,48},{40,56},{48,64},{56,72},{64,... | collective-permute-start | bytes 147464 | tf_op jit(solution)/shard_map/ppermute | solution.py:118
  93.7 24.4 %copy-start.21 = (bf16[48,512]{1,0:T(8,128)(2,1)}, bf16[48,512]{1,0:T(8,128)(2,1)S(1)}, u32[]{:S(2)}) copy-start(bf16[48,512]{1,0:T(8,128)(2,1)S(1)} %collective-permute-done.4) | copy-start | bytes 147460
  104.2 17.1 %copy-start.36 = (s32[4,96,4]{1,2,0:T(4,128)S(1)}, s32[4,96,4]{1,2,0:T(4,128)}, u32[]{:S(2)}) copy-start(s32[4,96,4]{1,2,0:T(4,128)} %param.19) | copy-start | bytes 18436
  119.4 9.0 %collective-permute-start.5 = (bf16[48,512]{1,0:T(8,128)(2,1)S(1)}, bf16[48,512]{1,0:T(8,128)(2,1)S(1)}, u32[]{:S(2)}, u32[]{:S(2)}) collective-permute-start(bf16[48,512]{1,0:T(8,128)(2,1)S(1)} %fusion.18), channel_id=1, source_target_pairs={{0,16},{8,24},{16,32},{24,40},{32,48},{40,56},{48,64},{56,72},{64,... | collective-permute-start | bytes 147464 | tf_op jit(solution)/shard_map/ppermute | solution.py:118
  129.8 17.5 %all-to-all-start.5 = ((bf16[8,48,512]{2,1,0:T(8,128)(2,1)}), bf16[8,48,512]{2,1,0:T(8,128)(2,1)}, u32[]{:S(2)}, u32[]{:S(2)}) async-start(bf16[8,48,512]{2,1,0:T(8,128)(2,1)} %broadcast_in_dim.16), calls=%async_computation.5 | async-start | bytes 786432 | tf_op jit(solution)/shard_map/all_to_all | solution.py:122
  141.7 19.8 %copy-start.24 = (bf16[48,512]{1,0:T(8,128)(2,1)S(1)}, bf16[48,512]{1,0:T(8,128)(2,1)}, u32[]{:S(2)}) copy-start(bf16[48,512]{1,0:T(8,128)(2,1)} %copy-done.23) | copy-start | bytes 147460
  141.7 19.8 %copy-start.26 = (bf16[48,512]{1,0:T(8,128)(2,1)S(1)}, bf16[48,512]{1,0:T(8,128)(2,1)}, u32[]{:S(2)}) copy-start(bf16[48,512]{1,0:T(8,128)(2,1)} %copy-done.25) | copy-start | bytes 147460
  143.3 18.2 %collective-permute-start.9 = (bf16[3,48,512]{2,1,0:T(8,128)(2,1)}, bf16[3,48,512]{2,1,0:T(8,128)(2,1)}, u32[]{:S(2)}, u32[]{:S(2)}) collective-permute-start(bf16[3,48,512]{2,1,0:T(8,128)(2,1)} %pad_maximum_fusion.2), channel_id=1, source_target_pairs={{496,480},{504,488},{497,481},{505,489},{498,482},{506,490},{499,4... | collective-permute-start | bytes 442376 | tf_op jit(solution)/shard_map/ppermute | solution.py:136
  144.6 16.9 %collective-permute-start.8 = (bf16[3,48,512]{2,1,0:T(8,128)(2,1)}, bf16[3,48,512]{2,1,0:T(8,128)(2,1)}, u32[]{:S(2)}, u32[]{:S(2)}) collective-permute-start(bf16[3,48,512]{2,1,0:T(8,128)(2,1)} %pad_maximum_fusion.2), channel_id=1, source_target_pairs={{496,464},{504,472},{497,465},{505,473},{498,466},{506,474},{499,4... | collective-permute-start | bytes 442376 | tf_op jit(solution)/shard_map/ppermute | solution.py:136
  145.9 15.6 %collective-permute-start.7 = (bf16[3,48,512]{2,1,0:T(8,128)(2,1)}, bf16[3,48,512]{2,1,0:T(8,128)(2,1)}, u32[]{:S(2)}, u32[]{:S(2)}) collective-permute-start(bf16[3,48,512]{2,1,0:T(8,128)(2,1)} %pad_maximum_fusion.2), channel_id=1, source_target_pairs={{496,448},{504,456},{497,449},{505,457},{498,450},{506,458},{499,4... | collective-permute-start | bytes 442376 | tf_op jit(solution)/shard_map/ppermute | solution.py:136
  147.2 1.2 copy-start.4
  148.4 1.1 copy-start.7
  154.8 12.6 %copy-start.37 = (bf16[2,256]{1,0:T(2,128)(2,1)S(1)}, bf16[2,256]{1,0:T(2,128)(2,1)}, u32[]{:S(2)}) copy-start(bf16[2,256]{1,0:T(2,128)(2,1)} %param.16) | copy-start | bytes 3076
  154.8 12.6 %copy-start.38 = (bf16[2,256]{1,0:T(2,128)(2,1)S(1)}, bf16[2,256]{1,0:T(2,128)(2,1)}, u32[]{:S(2)}) copy-start(bf16[2,256]{1,0:T(2,128)(2,1)} %rev.6) | copy-start | bytes 3076
  154.8 20.7 %copy-start.15 = (f32[48,512]{1,0:T(8,128)S(1)}, f32[48,512]{1,0:T(8,128)}, u32[]{:S(2)}) copy-start(f32[48,512]{1,0:T(8,128)} %copy-done.14) | copy-start | bytes 294916
  154.8 20.7 %copy-start.17 = (f32[48,512]{1,0:T(8,128)S(1)}, f32[48,512]{1,0:T(8,128)}, u32[]{:S(2)}) copy-start(f32[48,512]{1,0:T(8,128)} %copy-done.16) | copy-start | bytes 294916
  154.8 20.7 %copy-start.20 = (bf16[48,512]{1,0:T(8,128)(2,1)S(1)}, bf16[48,512]{1,0:T(8,128)(2,1)}, u32[]{:S(2)}) copy-start(bf16[48,512]{1,0:T(8,128)(2,1)} %copy-done.18) | copy-start | bytes 147460
  154.8 20.7 %copy-start.22 = (bf16[48,512]{1,0:T(8,128)(2,1)S(1)}, bf16[48,512]{1,0:T(8,128)(2,1)}, u32[]{:S(2)}) copy-start(bf16[48,512]{1,0:T(8,128)(2,1)} %copy-done.21) | copy-start | bytes 147460
  154.8 20.7 %copy-start.27 = (bf16[48,256]{1,0:T(8,128)(2,1)S(1)}, bf16[48,256]{1,0:T(8,128)(2,1)}, u32[]{:S(2)}) copy-start(bf16[48,256]{1,0:T(8,128)(2,1)} %fusion.28) | copy-start | bytes 73732
  154.8 20.7 %copy-start.28 = (bf16[48,256]{1,0:T(8,128)(2,1)S(1)}, bf16[48,256]{1,0:T(8,128)(2,1)}, u32[]{:S(2)}) copy-start(bf16[48,256]{1,0:T(8,128)(2,1)} %constant_dynamic-slice_fusion.2) | copy-start | bytes 73732
  154.8 20.7 %copy-start.30 = (bf16[48,512]{1,0:T(8,128)(2,1)S(1)}, bf16[48,512]{1,0:T(8,128)(2,1)}, u32[]{:S(2)}) copy-start(bf16[48,512]{1,0:T(8,128)(2,1)} %copy-done.29) | copy-start | bytes 147460
  154.8 17.9 %all-to-all-start.6 = ((bf16[8,48,512]{2,1,0:T(8,128)(2,1)}), bf16[8,48,512]{2,1,0:T(8,128)(2,1)S(1)}, u32[]{:S(2)}, u32[]{:S(2)}) async-start(bf16[8,48,512]{2,1,0:T(8,128)(2,1)} %copy-done.11), calls=%async_computation.6 | async-start | bytes 786432 | tf_op jit(solution)/shard_map/all_to_all | solution.py:122
  162.6 10.2 %collective-permute-start.16 = (bf16[3,48,512]{2,1,0:T(8,128)(2,1)S(1)}, bf16[3,48,512]{2,1,0:T(8,128)(2,1)S(1)}, u32[]{:S(2)}, u32[]{:S(2)}) collective-permute-start(bf16[3,48,512]{2,1,0:T(8,128)(2,1)S(1)} %add_add_fusion.1), channel_id=1, source_target_pairs={{448,384},{456,392},{464,400},{472,408},{480,416},{488,424},{496,4... | collective-permute-start | bytes 442376 | tf_op jit(solution)/shard_map/ppermute | solution.py:141
  165.9 8.3 %collective-permute-start.15 = (bf16[3,48,512]{2,1,0:T(8,128)(2,1)S(1)}, bf16[3,48,512]{2,1,0:T(8,128)(2,1)S(1)}, u32[]{:S(2)}, u32[]{:S(2)}) collective-permute-start(bf16[3,48,512]{2,1,0:T(8,128)(2,1)S(1)} %add_add_fusion.1), channel_id=1, source_target_pairs={{448,320},{456,328},{464,336},{472,344},{480,352},{488,360},{496,3... | collective-permute-start | bytes 442376 | tf_op jit(solution)/shard_map/ppermute | solution.py:141
  167.4 8.2 %collective-permute-start.14 = (bf16[3,48,512]{2,1,0:T(8,128)(2,1)S(1)}, bf16[3,48,512]{2,1,0:T(8,128)(2,1)S(1)}, u32[]{:S(2)}, u32[]{:S(2)}) collective-permute-start(bf16[3,48,512]{2,1,0:T(8,128)(2,1)S(1)} %add_add_fusion.1), channel_id=1, source_target_pairs={{448,256},{456,264},{464,272},{472,280},{480,288},{488,296},{496,3... | collective-permute-start | bytes 442376 | tf_op jit(solution)/shard_map/ppermute | solution.py:141
  170.2 7.4 %collective-permute-start.13 = (bf16[3,48,512]{2,1,0:T(8,128)(2,1)S(1)}, bf16[3,48,512]{2,1,0:T(8,128)(2,1)S(1)}, u32[]{:S(2)}, u32[]{:S(2)}) collective-permute-start(bf16[3,48,512]{2,1,0:T(8,128)(2,1)S(1)} %add_add_fusion.1), channel_id=1, source_target_pairs={{448,192},{456,200},{464,208},{472,216},{480,224},{488,232},{496,2... | collective-permute-start | bytes 442376 | tf_op jit(solution)/shard_map/ppermute | solution.py:141
  171.5 6.1 %collective-permute-start.12 = (bf16[3,48,512]{2,1,0:T(8,128)(2,1)S(1)}, bf16[3,48,512]{2,1,0:T(8,128)(2,1)S(1)}, u32[]{:S(2)}, u32[]{:S(2)}) collective-permute-start(bf16[3,48,512]{2,1,0:T(8,128)(2,1)S(1)} %add_add_fusion.1), channel_id=1, source_target_pairs={{448,128},{456,136},{464,144},{472,152},{480,160},{488,168},{496,1... | collective-permute-start | bytes 442376 | tf_op jit(solution)/shard_map/ppermute | solution.py:141
  172.8 4.7 %collective-permute-start.11 = (bf16[3,48,512]{2,1,0:T(8,128)(2,1)S(1)}, bf16[3,48,512]{2,1,0:T(8,128)(2,1)S(1)}, u32[]{:S(2)}, u32[]{:S(2)}) collective-permute-start(bf16[3,48,512]{2,1,0:T(8,128)(2,1)S(1)} %add_add_fusion.1), channel_id=1, source_target_pairs={{448,64},{456,72},{464,80},{472,88},{480,96},{488,104},{496,112},{... | collective-permute-start | bytes 442376 | tf_op jit(solution)/shard_map/ppermute | solution.py:141
  174.2 4.4 %collective-permute-start.10 = (bf16[3,48,512]{2,1,0:T(8,128)(2,1)S(1)}, bf16[3,48,512]{2,1,0:T(8,128)(2,1)S(1)}, u32[]{:S(2)}, u32[]{:S(2)}) collective-permute-start(bf16[3,48,512]{2,1,0:T(8,128)(2,1)S(1)} %add_add_fusion.1), channel_id=1, source_target_pairs={{448,0},{456,8},{464,16},{472,24},{480,32},{488,40},{496,48},{504,... | collective-permute-start | bytes 442376 | tf_op jit(solution)/shard_map/ppermute | solution.py:141
  175.6 4.9 %collective-permute-start.6 = (bf16[48,512]{1,0:T(8,128)(2,1)S(1)}, bf16[48,512]{1,0:T(8,128)(2,1)S(1)}, u32[]{:S(2)}, u32[]{:S(2)}) collective-permute-start(bf16[48,512]{1,0:T(8,128)(2,1)S(1)} %fusion.14), channel_id=1, source_target_pairs={{0,8},{8,0},{16,24},{24,16},{32,40},{40,32},{48,56},{56,48},{64,72... | collective-permute-start | bytes 147464 | tf_op jit(solution)/shard_map/ppermute | solution.py:113
  178.6 4.7 %collective-permute-start.17 = (bf16[3,48,512]{2,1,0:T(8,128)(2,1)S(1)}, bf16[3,48,512]{2,1,0:T(8,128)(2,1)S(1)}, u32[]{:S(2)}, u32[]{:S(2)}) collective-permute-start(bf16[3,48,512]{2,1,0:T(8,128)(2,1)S(1)} %add_add_fusion), channel_id=1, source_target_pairs={{0,8},{8,0},{16,24},{24,16},{32,40},{40,32},{48,56},{56,48},{64,72... | collective-permute-start | bytes 442376 | tf_op jit(solution)/shard_map/ppermute | solution.py:113
  180.6 2.7 %collective-permute-start.20 = (bf16[96,512]{1,0:T(8,128)(2,1)S(1)}, bf16[96,512]{1,0:T(8,128)(2,1)S(1)}, u32[]{:S(2)}, u32[]{:S(2)}) collective-permute-start(bf16[96,512]{1,0:T(8,128)(2,1)S(1)} %pad_maximum_fusion.4), channel_id=1, source_target_pairs={{496,480},{504,488},{497,481},{505,489},{498,482},{506,490},{499,4... | collective-permute-start | bytes 294920 | tf_op jit(solution)/shard_map/ppermute | solution.py:136
  181.3 2.0 collective-permute-start.19
  182.0 9.3 %collective-permute-start.18 = (bf16[96,512]{1,0:T(8,128)(2,1)S(1)}, bf16[96,512]{1,0:T(8,128)(2,1)S(1)}, u32[]{:S(2)}, u32[]{:S(2)}) collective-permute-start(bf16[96,512]{1,0:T(8,128)(2,1)S(1)} %pad_maximum_fusion.4), channel_id=1, source_target_pairs={{496,448},{504,456},{497,449},{505,457},{498,450},{506,458},{499,4... | collective-permute-start | bytes 294920 | tf_op jit(solution)/shard_map/ppermute | solution.py:136
  191.3 6.6 %collective-permute-start.27 = (bf16[96,512]{1,0:T(8,128)(2,1)S(1)}, bf16[96,512]{1,0:T(8,128)(2,1)S(1)}, u32[]{:S(2)}, u32[]{:S(2)}) collective-permute-start(bf16[96,512]{1,0:T(8,128)(2,1)S(1)} %add_add_fusion.2), channel_id=1, source_target_pairs={{448,384},{456,392},{464,400},{472,408},{480,416},{488,424},{496,4... | collective-permute-start | bytes 294920 | tf_op jit(solution)/shard_map/ppermute | solution.py:141
  192.6 6.6 %collective-permute-start.26 = (bf16[96,512]{1,0:T(8,128)(2,1)S(1)}, bf16[96,512]{1,0:T(8,128)(2,1)S(1)}, u32[]{:S(2)}, u32[]{:S(2)}) collective-permute-start(bf16[96,512]{1,0:T(8,128)(2,1)S(1)} %add_add_fusion.2), channel_id=1, source_target_pairs={{448,320},{456,328},{464,336},{472,344},{480,352},{488,360},{496,3... | collective-permute-start | bytes 294920 | tf_op jit(solution)/shard_map/ppermute | solution.py:141
  194.0 15.2 %collective-permute-start.25 = (bf16[96,512]{1,0:T(8,128)(2,1)S(1)}, bf16[96,512]{1,0:T(8,128)(2,1)S(1)}, u32[]{:S(2)}, u32[]{:S(2)}) collective-permute-start(bf16[96,512]{1,0:T(8,128)(2,1)S(1)} %add_add_fusion.2), channel_id=1, source_target_pairs={{448,256},{456,264},{464,272},{472,280},{480,288},{488,296},{496,3... | collective-permute-start | bytes 294920 | tf_op jit(solution)/shard_map/ppermute | solution.py:141
  195.3 13.9 %collective-permute-start.24 = (bf16[96,512]{1,0:T(8,128)(2,1)S(1)}, bf16[96,512]{1,0:T(8,128)(2,1)S(1)}, u32[]{:S(2)}, u32[]{:S(2)}) collective-permute-start(bf16[96,512]{1,0:T(8,128)(2,1)S(1)} %add_add_fusion.2), channel_id=1, source_target_pairs={{448,192},{456,200},{464,208},{472,216},{480,224},{488,232},{496,2... | collective-permute-start | bytes 294920 | tf_op jit(solution)/shard_map/ppermute | solution.py:141
  196.6 12.6 %collective-permute-start.23 = (bf16[96,512]{1,0:T(8,128)(2,1)S(1)}, bf16[96,512]{1,0:T(8,128)(2,1)S(1)}, u32[]{:S(2)}, u32[]{:S(2)}) collective-permute-start(bf16[96,512]{1,0:T(8,128)(2,1)S(1)} %add_add_fusion.2), channel_id=1, source_target_pairs={{448,128},{456,136},{464,144},{472,152},{480,160},{488,168},{496,1... | collective-permute-start | bytes 294920 | tf_op jit(solution)/shard_map/ppermute | solution.py:141
  197.9 11.3 %collective-permute-start.22 = (bf16[96,512]{1,0:T(8,128)(2,1)S(1)}, bf16[96,512]{1,0:T(8,128)(2,1)S(1)}, u32[]{:S(2)}, u32[]{:S(2)}) collective-permute-start(bf16[96,512]{1,0:T(8,128)(2,1)S(1)} %add_add_fusion.2), channel_id=1, source_target_pairs={{448,64},{456,72},{464,80},{472,88},{480,96},{488,104},{496,112},{... | collective-permute-start | bytes 294920 | tf_op jit(solution)/shard_map/ppermute | solution.py:141
  199.2 10.0 %collective-permute-start.21 = (bf16[96,512]{1,0:T(8,128)(2,1)S(1)}, bf16[96,512]{1,0:T(8,128)(2,1)S(1)}, u32[]{:S(2)}, u32[]{:S(2)}) collective-permute-start(bf16[96,512]{1,0:T(8,128)(2,1)S(1)} %add_add_fusion.2), channel_id=1, source_target_pairs={{448,0},{456,8},{464,16},{472,24},{480,32},{488,40},{496,48},{504,... | collective-permute-start | bytes 294920 | tf_op jit(solution)/shard_map/ppermute | solution.py:141
  201.3 8.5 %copy-start.33 = (bf16[384,48]{0,1:T(8,128)(2,1)S(1)}, bf16[384,48]{0,1:T(8,128)(2,1)}, u32[]{:S(2)}) copy-start(bf16[384,48]{0,1:T(8,128)(2,1)} %fusion.2) | copy-start | bytes 110596
  201.3 16.5 %all-to-all-start.7 = ((bf16[8,96,256]{2,1,0:T(8,128)(2,1)}), bf16[8,96,256]{2,1,0:T(8,128)(2,1)S(1)}, u32[]{:S(2)}, u32[]{:S(2)}) async-start(bf16[8,96,256]{2,1,0:T(8,128)(2,1)} %broadcast_in_dim.17), calls=%async_computation.7 | async-start | bytes 786432 | tf_op jit(solution)/shard_map/all_to_all | solution.py:122
  218.8 15.2 %all-to-all-start.8 = ((bf16[8,384,128]{2,1,0:T(8,128)(2,1)}), bf16[8,384,128]{2,1,0:T(8,128)(2,1)S(1)}, u32[]{:S(2)}, u32[]{:S(2)}) async-start(bf16[8,384,128]{2,1,0:T(8,128)(2,1)} %broadcast_in_dim.20), calls=%async_computation.8 | async-start | bytes 1572864 | tf_op jit(solution)/shard_map/all_to_all | solution.py:122
  (9 other events, 6.9 us)

commit v2 on v1

v2 whole, which is shorter than its diff:
```python
import functools

import jax
import jax.numpy as jnp
from jax import lax
from jax.experimental import pallas as pl
from jax.experimental.pallas import tpu as pltpu
from jax.sharding import PartitionSpec as P

D = 4096
H = 32
KVH = 8
HD = 64
NQ = 4
TICKS = 4
B = 96
CACHE = 16
HALF = B // 2
RATIO = H // KVH
EARLY = TICKS - 1
LANES = 128
FIRST = 24

epsilon = 1e-05
f32 = jnp.float32
bf16 = jnp.bfloat16
i32 = jnp.int32
CONTRACT_LAST = (((1,), (1,)), ((), ()))


def last_visible(tick, place_ref, lengths_ref):
    side, section = place_ref[0], place_ref[1]
    lens = lengths_ref[pl.ds(jnp.maximum(section - tick, 0), 1), :]
    row = lax.broadcasted_iota(i32, (HALF, B), 0)
    lane = lax.broadcasted_iota(i32, (HALF, B), 1)
    lens = jnp.where(lane == row + side * HALF, lens, 0)
    lens = jnp.sum(lens, axis=1, keepdims=True)
    ends = lens + lax.broadcasted_iota(i32, (HALF, 1), 0) * CACHE
    return jnp.concatenate([ends] * RATIO, axis=0)


def attention_terms(proj, ends, o_own, o_oth, pairs_ref, out_ref):
    shards, block = out_ref.shape[0], out_ref.shape[2] // 2
    stacked = jnp.concatenate([proj[:, r * HD : (r + 1) * HD] for r in range(RATIO)], axis=0)
    queries = (stacked.astype(bf16).astype(f32) * (HD**-0.5)).astype(bf16)
    queries = jnp.concatenate([queries, jnp.zeros_like(queries)], axis=1)
    pair_new = proj[:, RATIO * HD :].astype(bf16)
    pairs = pairs_ref[...]
    scores = lax.dot_general(queries, pairs, CONTRACT_LAST, preferred_element_type=f32)
    own_scores = lax.dot_general(queries, pair_new, CONTRACT_LAST, preferred_element_type=f32)
    rows = RATIO * HALF
    stream = lax.rem(lax.broadcasted_iota(i32, (rows, 1), 0), HALF)
    place = lax.broadcasted_iota(i32, (rows, HALF * CACHE), 1)
    visible = jnp.logical_and(place >= stream * CACHE, place < ends)
    scores = jnp.where(visible, scores, -jnp.inf)
    own_place = lax.broadcasted_iota(i32, (rows, HALF), 1)
    own_scores = jnp.where(own_place == stream, own_scores, -jnp.inf)
    row_max = jnp.maximum(
        jnp.max(scores, axis=-1, keepdims=True), jnp.max(own_scores, axis=-1, keepdims=True)
    )
    weights = jnp.exp(scores - row_max)
    own_weights = jnp.exp(own_scores - row_max)
    total = jnp.sum(weights, axis=-1, keepdims=True) + jnp.sum(own_weights, axis=-1, keepdims=True)
    share = 1.0 / total
    mixed = jnp.dot((weights * share).astype(bf16), pairs, preferred_element_type=f32)
    mixed = mixed + jnp.dot(
        (own_weights * share).astype(bf16), pair_new, preferred_element_type=f32
    )
    mixed = mixed[:, HD:].astype(bf16)
    heads = jnp.concatenate([mixed[r * HALF : (r + 1) * HALF] for r in range(RATIO)], axis=1)
    for j in range(shards):
        span = slice(j * block, (j + 1) * block)
        own = jnp.dot(heads, o_own[:, span], preferred_element_type=f32)
        oth = jnp.dot(heads, o_oth[:, span], preferred_element_type=f32)
        out_ref[j, :, :block] = own.astype(bf16)
        out_ref[j, :, block:] = oth.astype(bf16)


def first_kernel(place_ref, *refs):
    count = (len(refs) - 3) // 2
    sources, (out_ref, shard_ref), held = refs[:count], refs[count : count + 2], refs[count + 2 : -1]
    semaphores = refs[-1]
    copies = [
        pltpu.make_async_copy(source, target, semaphores.at[i])
        for i, (source, target) in enumerate(zip(sources, held))
    ]
    for copy in copies:
        copy.start()
    rows_own, rows_oth, g_own, g_oth, lengths_ref, w_own, w_oth, o_own, o_oth = held[:9]
    side, column = place_ref[0], place_ref[2]
    block = shard_ref.shape[1] // 2
    mine = pl.ds(pl.multiple_of(side * HALF, HALF), HALF)
    for copy in copies[:5]:
        copy.wait()
    own = rows_own[mine, :].astype(f32)
    oth = rows_oth[mine, :].astype(f32)
    squares = jnp.sum(own * own + oth * oth, axis=-1, keepdims=True)
    scaled_own = (own * g_own[...].astype(f32)).astype(bf16)
    scaled_oth = (oth * g_oth[...].astype(f32)).astype(bf16)
    part = pl.ds(pl.multiple_of(column * block, block), block)
    shard_ref[:, :block] = rows_own[mine, part]
    shard_ref[:, block:] = rows_oth[mine, part]
    ends = last_visible(0, place_ref, lengths_ref)
    copies[5].wait()
    proj = jnp.dot(scaled_own, w_own[...], preferred_element_type=f32)
    copies[6].wait()
    proj = proj + jnp.dot(scaled_oth, w_oth[...], preferred_element_type=f32)
    proj = proj * lax.rsqrt(squares / D + epsilon)
    for copy in copies[7:]:
        copy.wait()
    attention_terms(proj, ends, o_own, o_oth, held[9].at[0], out_ref)


def later_kernel(
    tick, place_ref, lengths_ref, g_own, g_oth, w_own, w_oth, o_own, o_oth, cache_ref, x_ref,
    out_ref, inverse_ref,
):
    shards, block = x_ref.shape[0], x_ref.shape[2] // 2
    squares = jnp.zeros(x_ref.shape[1:], f32)
    proj = jnp.zeros((HALF, w_own.shape[1]), f32)
    for j in range(shards):
        span = slice(j * block, (j + 1) * block)
        rows = x_ref[j].astype(f32)
        squares = squares + rows * rows
        own = (rows[:, :block] * g_own[:, span].astype(f32)).astype(bf16)
        oth = (rows[:, block:] * g_oth[:, span].astype(f32)).astype(bf16)
        proj = proj + jnp.dot(own, w_own[span, :], preferred_element_type=f32)
        proj = proj + jnp.dot(oth, w_oth[span, :], preferred_element_type=f32)
    inverse_rms = lax.rsqrt(jnp.sum(squares, axis=-1, keepdims=True) / D + epsilon)
    inverse_ref[...] = jnp.broadcast_to(inverse_rms, inverse_ref.shape)
    proj = proj * inverse_rms
    ends = last_visible(tick, place_ref, lengths_ref)
    attention_terms(proj, ends, o_own, o_oth, cache_ref.at[tick], out_ref)


def sum_kernel(tick, place_ref, got_ref, shard_ref, inverse_ref, out_ref):
    section = place_ref[1]
    shard = shard_ref[...].astype(f32)
    total = shard
    for j in range(got_ref.shape[0]):
        total = total + got_ref[j].astype(f32)
    if tick:
        passed = shard * jnp.where(section == 0, inverse_ref[:, :1], 1.0)
        total = jnp.where(section >= tick, total, passed)
    out_ref[...] = total.astype(bf16)


def latest_kernel(place_ref, last_ref, early_0, early_1, early_2, out_ref):
    section = place_ref[1]
    latest = last_ref[...].astype(f32)
    for tick, early in ((2, early_2), (1, early_1), (0, early_0)):
        latest = jnp.where(section <= tick, early[...].astype(f32), latest)
    out_ref[...] = latest.astype(bf16)


def holder_of(tick):
    return EARLY if tick == EARLY else EARLY - 1 - tick


def talk_kernel(
    place_ref, own_ref, other_ref, latest_own, latest_oth, talk_gain, adapt_ref, books_ref, codes_ref,
    out_ref,
):
    side, column = place_ref[0], place_ref[2]
    block = own_ref.shape[2] // 2
    columns = adapt_ref.shape[1]
    entries = books_ref.shape[2]
    gains = talk_gain[...].astype(f32)

    def whole(tick):
        own = own_ref[holder_of(tick)].astype(f32)
        other = other_ref[holder_of(tick)].astype(f32)
        first = jnp.where(side == 0, own, other)
        second = jnp.where(side == 0, other, own)
        return (
            jnp.concatenate([first[:, :block], second[:, block:]], axis=0),
            jnp.concatenate([first[:, block:], second[:, :block]], axis=0),
        )

    def embedded(tick):
        total = jnp.zeros((columns, B), f32)
        for q in range(NQ):
            ids = codes_ref[tick, q : q + 1, :] - column * entries
            hot = lax.broadcasted_iota(i32, (entries, B), 0) == ids
            hot = jnp.where(hot, 1.0, 0.0).astype(bf16)
            total = total + jnp.dot(books_ref[q], hot, preferred_element_type=f32)
        return total

    def adapted(low, high):
        return lax.dot_general(
            adapt_ref[0], low.astype(bf16), CONTRACT_LAST, preferred_element_type=f32
        ) + lax.dot_general(
            adapt_ref[1], high.astype(bf16), CONTRACT_LAST, preferred_element_type=f32
        )

    out_ref[: (TICKS + 1) * columns + 16] = jnp.zeros(((TICKS + 1) * columns + 16, LANES), bf16)
    for tick in range(TICKS):
        low, high = whole(tick)
        rows = adapted(low * gains[0:1], high * gains[1:2])
        base = tick * columns
        if tick < EARLY:
            rows = rows + embedded(tick)
        else:
            out_ref[base + columns : base + 2 * columns, :B] = embedded(tick).astype(bf16)
        out_ref[base : base + columns, :B] = rows.astype(bf16)
    squares = jnp.sum(low * low + high * high, axis=1, keepdims=True)
    diagonal = lax.broadcasted_iota(i32, (B, B), 0) == lax.broadcasted_iota(i32, (B, B), 1)
    squares = jnp.sum(jnp.where(diagonal, squares, 0.0), axis=0, keepdims=True)
    upper = squares.astype(bf16).astype(f32)
    tail_row = lax.broadcasted_iota(i32, (16, B), 0)
    tail = jnp.where(tail_row == 0, upper, jnp.where(tail_row == 1, squares - upper, 0.0))
    base = (TICKS + 1) * columns + 16
    out_ref[base - 16 : base, :B] = tail.astype(bf16)
    own = latest_own[:, :block].astype(f32)
    oth = latest_oth[:, block:].astype(f32)
    first = jnp.where(side == 0, own, oth).astype(bf16)
    second = jnp.where(side == 0, oth, own).astype(bf16)
    for i in range(block // LANES):
        span = slice(i * LANES, (i + 1) * LANES)
        out_ref[base + i * B : base + i * B + HALF, :] = first[:, span]
        out_ref[base + i * B + HALF : base + (i + 1) * B, :] = second[:, span]


def finish_kernel(got_ref, out_ref, leaving_ref):
    columns = out_ref.shape[1]
    end = (TICKS + 1) * columns + 16
    pieces = (got_ref.shape[1] - end) // B
    total = got_ref[0, :end].astype(f32)
    for j in range(1, got_ref.shape[0]):
        total = total + got_ref[j, :end].astype(f32)
    for j in range(got_ref.shape[0]):
        for i in range(pieces):
            lane = (j * pieces + i) * LANES
            rows = got_ref[j, end + i * B : end + (i + 1) * B, :]
            leaving_ref[:, lane : lane + LANES] = rows.astype(f32)
    for tick in range(EARLY):
        out_ref[tick] = total[tick * columns : (tick + 1) * columns, :B]
    base, at = EARLY * columns, (TICKS + 1) * columns
    squares = total[at : at + 1, :] + total[at + 1 : at + 2, :]
    rows = total[base : base + columns] * lax.rsqrt(squares / D + epsilon)
    rows = rows + total[base + columns : base + 2 * columns]
    out_ref[EARLY] = rows[:, :B]


def run(kernel, outs, *operands, scalars=True, limit=16):
    specs = [pl.BlockSpec(memory_space=pltpu.VMEM)] * len(operands)
    if scalars:
        specs[0] = pl.BlockSpec(memory_space=pltpu.SMEM)
    out_specs = jax.tree.map(lambda _: pl.BlockSpec(memory_space=pltpu.VMEM), outs)
    return pl.pallas_call(
        kernel,
        out_shape=outs,
        in_specs=specs,
        out_specs=out_specs,
        compiler_params=pltpu.CompilerParams(vmem_limit_bytes=limit * 2**20),
    )(*operands)


def shaped(*shape, dtype=bf16):
    return jax.ShapeDtypeStruct(shape, dtype)


SECTION = ("line", "place", "core")
LINES, PLACES = 8, 4
LINE = 2 * PLACES


def to_partner(value):
    return lax.ppermute(value, "core", [(0, 1), (1, 0)])


def to_next(value):
    count = LINES * LINE
    return lax.ppermute(value, SECTION, [(i, (i + 2) % count) for i in range(count)])


def exchange(blocks, axis="tp"):
    return lax.all_to_all(blocks, axis, 0, 0, tiled=True)


def replicate(block, count):
    return jnp.broadcast_to(block[None], (count,) + block.shape)


def across_lines(value, holds):
    home = [LINES - 1 if place == EARLY else 0 for place in range(PLACES)]
    steps = sorted(range(1, LINES), key=lambda d: -min(d, LINES - d))
    result = jnp.where(holds, value, jnp.zeros_like(value))
    for d in steps:
        pairs = [
            (home[i // 2] * LINE + i, (home[i // 2] + d) % LINES * LINE + i) for i in range(LINE)
        ]
        result = result + lax.ppermute(value, SECTION, pairs)
    return result


def body(arriving, norm_gain, w_qkv, w_out, cache, lengths, talk_gain, w_adapt, codebooks, codes):
    position = lax.axis_index(SECTION)
    column = lax.axis_index("tp")
    shards = lax.axis_size("tp")
    section = position // 2
    width = arriving.shape[2]
    block = width // shards
    columns = w_adapt.shape[2]
    place = jnp.stack([lax.rem(position, 2), section, column]).astype(i32)

    w_own, o_own, rows_own = w_qkv[0], w_out[0], arriving[0]
    rows_oth = to_partner(rows_own)
    w_oth = to_partner(w_own)
    g_oth = to_partner(norm_gain)
    o_oth = to_partner(o_own)
    cache_rows = cache[0].reshape(TICKS, HALF * CACHE, -1)
    blocks = shaped(shards, HALF, 2 * block)
    piece = shaped(HALF, 2 * block)

    rows_own, norm_gain, lengths, w_own, o_own, cache_rows = (
        pltpu.with_memory_space_constraint(v, pltpu.HBM)
        for v in (rows_own, norm_gain, lengths, w_own, o_own, cache_rows)
    )
    held = [rows_own, rows_oth, norm_gain, g_oth, lengths, w_own, w_oth, o_own, o_oth, cache_rows]
    there = pl.BlockSpec(memory_space=pltpu.HBM)
    here = pl.BlockSpec(memory_space=pltpu.VMEM)
    terms, shard, _, _, *held = pl.pallas_call(
        first_kernel,
        out_shape=(blocks, piece, *(shaped(*v.shape, dtype=v.dtype) for v in held)),
        in_specs=[pl.BlockSpec(memory_space=pltpu.SMEM)] + [there] * len(held),
        out_specs=(here,) * (len(held) + 2),
        scratch_shapes=[pltpu.SemaphoreType.DMA((len(held),))],
        compiler_params=pltpu.CompilerParams(vmem_limit_bytes=FIRST * 2**20),
    )(place, *held)
    g_own, g_oth, lengths, *weights = held
    shared = (place, lengths, g_own, g_oth, *weights)
    finals = []
    inverse = jnp.zeros((HALF, LANES), f32)
    for tick in range(EARLY):
        got = exchange(terms)
        finals.append(run(functools.partial(sum_kernel, tick), piece, place, got, shard, inverse))
        shard = to_next(finals[-1])
        rows = exchange(replicate(shard, shards))
        terms, inverse = run(
            functools.partial(later_kernel, tick + 1),
            (blocks, shaped(HALF, LANES, dtype=f32)),
            *shared, rows,
        )
    got = exchange(terms)
    held_rows = run(functools.partial(sum_kernel, EARLY), piece, place, got, shard, inverse)

    holds = jnp.logical_or(section < EARLY, section == LINES * PLACES - 1)
    talk_rows = across_lines(held_rows, holds)
    latest = run(latest_kernel, piece, place, held_rows, *finals)
    latest_oth = to_partner(latest)
    talk_rows, latest_oth = lax.optimization_barrier((talk_rows, latest_oth))
    talk_rows = exchange(replicate(talk_rows, PLACES), "place")
    payload = run(
        talk_kernel,
        shaped((TICKS + 1) * columns + 16 + B * block // LANES, LANES),
        place, talk_rows, to_partner(talk_rows), latest, latest_oth, talk_gain,
        w_adapt.transpose(0, 2, 1), codebooks.transpose(0, 2, 1), codes.transpose(0, 2, 1),
    )
    sums = exchange(replicate(payload, shards))
    talk, leaving = run(
        finish_kernel,
        (shaped(TICKS, columns, B, dtype=f32), shaped(B, width, dtype=f32)),
        sums,
        scalars=False,
    )
    return (leaving[None], talk.transpose(0, 2, 1))


def solution(mesh):
    devices = mesh.devices
    grid = jax.sharding.Mesh(
        devices.reshape(LINES, PLACES, 2, devices.shape[1]), SECTION + ("tp",)
    )
    placed = (
        P(SECTION, None, None),
        P(SECTION, None),
        P(SECTION, None, "tp"),
        P(SECTION, "tp", None),
        P(SECTION, None, None, None, "tp"),
        P(),
        P(None, "tp"),
        P(None, "tp", SECTION),
        P(None, "tp", SECTION),
        P(),
    )
    return jax.shard_map(
        body,
        mesh=grid,
        in_specs=placed,
        out_specs=(P(SECTION, None, None), P(None, None, SECTION)),
        check_vma=False,
    )
```

time: 238 us -> 190 us (0.80)
  the two profiles are of different devices: /device:TPU:56 before, /device:TPU:1 now
where the time goes in v2:
time: 190 us; the launch traced here: 189 us
  blocking collectives  93.6 us (49%)
  starting transfers between devices  49.7 us (26%)
  waiting for transfers between devices  26.3 us (14%)
  Pallas kernels  18 us (9%)
    all_to_all x9, blocking collectives, exchange(): return lax.all_to_all(blocks, axis, 0, 0, tiled=True)  93.6 us
    ppermute x6, starting transfers between devices, to_partner(): return lax.ppermute(value, 'core', [(0, 1), (1, 0)])  33 us
    ppermute x3, waiting for transfers between devices, to_next(): lax.ppermute(value, SECTION, [(i, (i + 2) % count) for i in range(count)])  23.2 us
    pallas_call x10, Pallas kernels, run(): pl.pallas_call(kernel, out_shape=outs, in_specs=specs, out_specs=out_spec...  12.9 us
    ppermute x7, starting transfers between devices, across_lines(): result = result + lax.ppermute(value, SECTION, pairs)  9.31 us
    ppermute x3, starting transfers between devices, to_next(): lax.ppermute(value, SECTION, [(i, (i + 2) % count) for i in range(count)])  7.48 us
    pallas_call x1, Pallas kernels, body(): pl.pallas_call(first_kernel, out_shape=(blocks, piece, *(shaped(*v.shape,...  5.18 us
  transfers between devices with their start and end apart: 16, of which 6 were waited for; matrix products, arithmetic and copies ran while one was open for 0% of the time, Pallas kernels for 0%

profile of v2, /device:TPU:1, one launch (start us, length us, event | category | flops | bytes accessed | tf_op | source)
XLA Modules:
  0.0 189.0 jit_solution(12023375174590066395)
XLA Ops:
  0.6 8.8 %collective-permute-start.2 = (bf16[2048,384]{1,0:T(8,128)(2,1)}, bf16[2048,384]{1,0:T(8,128)(2,1)S(1)}, u32[]{:S(2)}, u32[]{:S(2)}) collective-permute-start(bf16[2048,384]{1,0:T(8,128)(2,1)} %bitcast.15), channel_id=1, source_target_pairs={{0,8},{8,0},{1,9},{9,1},{2,10},{10,2},{3,11},{11,3},{4,12},{12,4},... | collective-permute-start | bytes 4718600 | tf_op jit(solution)/shard_map/ppermute | solution.py:269
  9.4 1.9 %collective-permute-start.3 = (bf16[256,2048]{1,0:T(8,128)(2,1)}, bf16[256,2048]{1,0:T(8,128)(2,1)S(1)}, u32[]{:S(2)}, u32[]{:S(2)}) collective-permute-start(bf16[256,2048]{1,0:T(8,128)(2,1)} %bitcast.17), channel_id=1, source_target_pairs={{0,8},{8,0},{1,9},{9,1},{2,10},{10,2},{3,11},{11,3},{4,12},{12,4},... | collective-permute-start | bytes 3145736 | tf_op jit(solution)/shard_map/ppermute | solution.py:269
  11.4 2.4 %collective-permute-start = (bf16[96,2048]{1,0:T(8,128)(2,1)}, bf16[96,2048]{1,0:T(8,128)(2,1)S(1)}, u32[]{:S(2)}, u32[]{:S(2)}) collective-permute-start(bf16[96,2048]{1,0:T(8,128)(2,1)} %bitcast.20), channel_id=1, source_target_pairs={{0,8},{8,0},{1,9},{9,1},{2,10},{10,2},{3,11},{11,3},{4,12},{12,4},... | collective-permute-start | bytes 1179656 | tf_op jit(solution)/shard_map/ppermute | solution.py:269
  13.8 1.9 %collective-permute-start.1 = (bf16[1,2048]{1,0:T(2,128)(2,1)}, bf16[1,2048]{1,0:T(2,128)(2,1)S(1)}, u32[]{:S(2)}, u32[]{:S(2)}) collective-permute-start(bf16[1,2048]{1,0:T(2,128)(2,1)} %refs_2_.1), channel_id=1, source_target_pairs={{0,8},{8,0},{1,9},{9,1},{2,10},{10,2},{3,11},{11,3},{4,12},{12,4},... | collective-permute-start | bytes 12296 | tf_op jit(solution)/shard_map/ppermute | solution.py:269
  15.7 0.1 pad_add_fusion.place_ref
  15.8 1.3 collective-permute-done.1.refs_3_
  17.1 0.0 collective-permute-done.refs_1_
  17.1 0.0 collective-permute-done.3.refs_8_
  17.1 0.0 collective-permute-done.2.refs_6_
  17.1 5.2 %shard_map.113 = (bf16[8,48,512]{2,1,0:T(8,128)(2,1)S(1)}, bf16[48,512]{1,0:T(8,128)(2,1)S(1)}, bf16[96,2048]{1,0:T(8,128)(2,1)}, bf16[96,2048]{1,0:T(8,128)(2,1...) custom-call(s32[3]{0:T(128)S(1)} %pad_add_fusion.place_ref, ...), custom_call_target="tpu_custom_call" | custom-call | tf_op jit(solution)/shard_map/pallas_call | solution.py:323
  22.3 10.4 %all_to_all.45.got_ref = bf16[8,48,512]{2,1,0:T(8,128)(2,1)S(1)} all-to-all(bf16[8,48,512]{2,1,0:T(8,128)(2,1)S(1)} %get-tuple-element.30), channel_id=1, replica_groups=mesh['line'=8,'place'=4,'core'=2,'tp'=8] {'tp'}, dimensions={0} | all-to-all | bytes 786432 | tf_op jit(solution)/shard_map/all_to_all | solution.py:278
  32.7 0.6 shard_map.114.early_0
  33.3 3.6 %collective-permute-start.4 = (bf16[48,512]{1,0:T(8,128)(2,1)S(1)}, bf16[48,512]{1,0:T(8,128)(2,1)S(1)}, u32[]{:S(2)}, u32[]{:S(2)}) collective-permute-start(bf16[48,512]{1,0:T(8,128)(2,1)S(1)} %shard_map.114.early_0), channel_id=1, source_target_pairs={{0,16},{8,24},{16,32},{24,40},{32,48},{40,56},{48,64},{56,72},{64,... | collective-permute-start | bytes 147464 | tf_op jit(solution)/shard_map/ppermute | solution.py:274
  36.9 8.4 %collective-permute-done.4.shard_ref = bf16[48,512]{1,0:T(8,128)(2,1)S(1)} collective-permute-done((bf16[48,512]{1,0:T(8,128)(2,1)S(1)}, bf16[48,512]{1,0:T(8,128)(2,1)S(1)}, u32[]{:S(2)}, u32[]{:S(2)}) %collective-permute-start.4) | collective-permute-done | bytes 49184 | tf_op jit(solution)/shard_map/ppermute | solution.py:274
  45.3 10.3 %all_to_all.46.x_ref = bf16[8,48,512]{2,1,0:T(8,128)(2,1)S(1)} all-to-all(bf16[8,48,512]{2,1,0:T(8,128)(2,1)S(1)} %broadcast_in_dim.17), channel_id=1, replica_groups=mesh['line'=8,'place'=4,'core'=2,'tp'=8] {'tp'}, dimensions={0} | all-to-all | bytes 786432 | tf_op jit(solution)/shard_map/all_to_all | solution.py:278
  55.6 2.6 %shard_map.115 = (bf16[8,48,512]{2,1,0:T(8,128)(2,1)S(1)}, f32[48,128]{1,0:T(8,128)S(1)}) custom-call(s32[3]{0:T(128)S(1)} %pad_add_fusion.place_ref, s32[32,96]{1,0:T(8,128)S(1)} %get-tuple-element.22.lengths_ref, bf16[1,2048]{1,0:T(2,128)(2,1)S(1)} %get-tuple-element.23.g_own, bf16[1,2048]{1,0:T(2,128)(2,1)S(1)} %get-tuple-element.24.g_oth, ...), custom_call_target="tpu_custom_call" | custom-call | tf_op jit(solution)/shard_map/pallas_call | solution.py:250
  58.2 9.2 %all_to_all.47.got_ref = bf16[8,48,512]{2,1,0:T(8,128)(2,1)S(1)} all-to-all(bf16[8,48,512]{2,1,0:T(8,128)(2,1)S(1)} %get-tuple-element.32), channel_id=1, replica_groups=mesh['line'=8,'place'=4,'core'=2,'tp'=8] {'tp'}, dimensions={0} | all-to-all | bytes 786432 | tf_op jit(solution)/shard_map/all_to_all | solution.py:278
  67.5 0.6 shard_map.116.early_1
  68.1 1.9 %collective-permute-start.5 = (bf16[48,512]{1,0:T(8,128)(2,1)S(1)}, bf16[48,512]{1,0:T(8,128)(2,1)S(1)}, u32[]{:S(2)}, u32[]{:S(2)}) collective-permute-start(bf16[48,512]{1,0:T(8,128)(2,1)S(1)} %shard_map.116.early_1), channel_id=1, source_target_pairs={{0,16},{8,24},{16,32},{24,40},{32,48},{40,56},{48,64},{56,72},{64,... | collective-permute-start | bytes 147464 | tf_op jit(solution)/shard_map/ppermute | solution.py:274
  70.0 7.6 %collective-permute-done.5.shard_ref = bf16[48,512]{1,0:T(8,128)(2,1)S(1)} collective-permute-done((bf16[48,512]{1,0:T(8,128)(2,1)S(1)}, bf16[48,512]{1,0:T(8,128)(2,1)S(1)}, u32[]{:S(2)}, u32[]{:S(2)}) %collective-permute-start.5) | collective-permute-done | bytes 49184 | tf_op jit(solution)/shard_map/ppermute | solution.py:274
  77.7 9.2 %all_to_all.48.x_ref = bf16[8,48,512]{2,1,0:T(8,128)(2,1)S(1)} all-to-all(bf16[8,48,512]{2,1,0:T(8,128)(2,1)S(1)} %broadcast_in_dim.18), channel_id=1, replica_groups=mesh['line'=8,'place'=4,'core'=2,'tp'=8] {'tp'}, dimensions={0} | all-to-all | bytes 786432 | tf_op jit(solution)/shard_map/all_to_all | solution.py:278
  86.9 2.6 %shard_map.117 = (bf16[8,48,512]{2,1,0:T(8,128)(2,1)S(1)}, f32[48,128]{1,0:T(8,128)S(1)}) custom-call(s32[3]{0:T(128)S(1)} %pad_add_fusion.place_ref, s32[32,96]{1,0:T(8,128)S(1)} %get-tuple-element.22.lengths_ref, bf16[1,2048]{1,0:T(2,128)(2,1)S(1)} %get-tuple-element.23.g_own, bf16[1,2048]{1,0:T(2,128)(2,1)S(1)} %get-tuple-element.24.g_oth, ...), custom_call_target="tpu_custom_call" | custom-call | tf_op jit(solution)/shard_map/pallas_call | solution.py:250
  89.5 9.2 %all_to_all.49.got_ref = bf16[8,48,512]{2,1,0:T(8,128)(2,1)S(1)} all-to-all(bf16[8,48,512]{2,1,0:T(8,128)(2,1)S(1)} %get-tuple-element.34), channel_id=1, replica_groups=mesh['line'=8,'place'=4,'core'=2,'tp'=8] {'tp'}, dimensions={0} | all-to-all | bytes 786432 | tf_op jit(solution)/shard_map/all_to_all | solution.py:278
  98.7 0.6 shard_map.118.early_2
  99.3 1.9 %collective-permute-start.6 = (bf16[48,512]{1,0:T(8,128)(2,1)S(1)}, bf16[48,512]{1,0:T(8,128)(2,1)S(1)}, u32[]{:S(2)}, u32[]{:S(2)}) collective-permute-start(bf16[48,512]{1,0:T(8,128)(2,1)S(1)} %shard_map.118.early_2), channel_id=1, source_target_pairs={{0,16},{8,24},{16,32},{24,40},{32,48},{40,56},{48,64},{56,72},{64,... | collective-permute-start | bytes 147464 | tf_op jit(solution)/shard_map/ppermute | solution.py:274
  101.3 7.2 %collective-permute-done.6.shard_ref = bf16[48,512]{1,0:T(8,128)(2,1)S(1)} collective-permute-done((bf16[48,512]{1,0:T(8,128)(2,1)S(1)}, bf16[48,512]{1,0:T(8,128)(2,1)S(1)}, u32[]{:S(2)}, u32[]{:S(2)}) %collective-permute-start.6) | collective-permute-done | bytes 49184 | tf_op jit(solution)/shard_map/ppermute | solution.py:274
  108.5 9.2 %all_to_all.50.x_ref = bf16[8,48,512]{2,1,0:T(8,128)(2,1)S(1)} all-to-all(bf16[8,48,512]{2,1,0:T(8,128)(2,1)S(1)} %broadcast_in_dim.19), channel_id=1, replica_groups=mesh['line'=8,'place'=4,'core'=2,'tp'=8] {'tp'}, dimensions={0} | all-to-all | bytes 786432 | tf_op jit(solution)/shard_map/all_to_all | solution.py:278
  117.8 2.6 %shard_map.119 = (bf16[8,48,512]{2,1,0:T(8,128)(2,1)S(1)}, f32[48,128]{1,0:T(8,128)S(1)}) custom-call(s32[3]{0:T(128)S(1)} %pad_add_fusion.place_ref, s32[32,96]{1,0:T(8,128)S(1)} %get-tuple-element.22.lengths_ref, bf16[1,2048]{1,0:T(2,128)(2,1)S(1)} %get-tuple-element.23.g_own, bf16[1,2048]{1,0:T(2,128)(2,1)S(1)} %get-tuple-element.24.g_oth, ...), custom_call_target="tpu_custom_call" | custom-call | tf_op jit(solution)/shard_map/pallas_call | solution.py:250
  120.4 0.0 copy-start
  120.4 0.0 copy-start.1
  120.4 0.0 copy-start.2
  120.4 0.0 copy-start.3
  120.4 9.4 %all_to_all.51.got_ref = bf16[8,48,512]{2,1,0:T(8,128)(2,1)S(1)} all-to-all(bf16[8,48,512]{2,1,0:T(8,128)(2,1)S(1)} %get-tuple-element.36), channel_id=1, replica_groups=mesh['line'=8,'place'=4,'core'=2,'tp'=8] {'tp'}, dimensions={0} | all-to-all | bytes 786432 | tf_op jit(solution)/shard_map/all_to_all | solution.py:278
  129.8 0.6 shard_map.120.last_ref
  130.4 1.3 collective-permute-start.10
  131.7 1.3 collective-permute-start.11
  133.0 1.3 collective-permute-start.12
  134.3 1.3 collective-permute-start.13
  135.6 1.6 collective-permute-start.7
  137.2 0.0 collective-permute-done.10
  137.2 1.3 collective-permute-start.8
  138.5 0.0 collective-permute-done.11
  138.5 1.3 collective-permute-start.9
  139.8 0.6 shard_map.121.latest_own
  140.4 0.0 collective-permute-done.12
  140.4 13.7 %collective-permute-start.14 = (bf16[48,512]{1,0:T(8,128)(2,1)S(1)}, bf16[48,512]{1,0:T(8,128)(2,1)S(1)}, u32[]{:S(2)}, u32[]{:S(2)}) collective-permute-start(bf16[48,512]{1,0:T(8,128)(2,1)S(1)} %shard_map.121.latest_own), channel_id=1, source_target_pairs={{0,8},{8,0},{1,9},{9,1},{2,10},{10,2},{3,11},{11,3},{4,12},{12,4},... | collective-permute-start | bytes 147464 | tf_op jit(solution)/shard_map/ppermute | solution.py:269
  154.1 0.0 collective-permute-done.13
  154.2 0.0 collective-permute-done.7
  154.2 0.0 collective-permute-done.8
  154.2 0.0 collective-permute-done.9
  154.2 0.8 collective-permute-done.14.latest_oth
  155.0 10.6 %all_to_all.52.own_ref = bf16[4,48,512]{2,1,0:T(8,128)(2,1)S(1)} all-to-all(bf16[4,48,512]{2,1,0:T(8,128)(2,1)S(1)} %broadcast_in_dim.21), channel_id=1, replica_groups=mesh['line'=8,'place'=4,'core'=2,'tp'=8] {'place'}, dimensions={0} | all-to-all | bytes 393216 | tf_op jit(solution)/shard_map/all_to_all | solution.py:278
  165.6 4.2 %collective-permute-start.15 = (bf16[4,48,512]{2,1,0:T(8,128)(2,1)S(1)}, bf16[4,48,512]{2,1,0:T(8,128)(2,1)S(1)}, u32[]{:S(2)}, u32[]{:S(2)}) collective-permute-start(bf16[4,48,512]{2,1,0:T(8,128)(2,1)S(1)} %all_to_all.52.own_ref), channel_id=1, source_target_pairs={{0,8},{8,0},{1,9},{9,1},{2,10},{10,2},{3,11},{11,3},{4,12},{12,4},... | collective-permute-start | bytes 589832 | tf_op jit(solution)/shard_map/ppermute | solution.py:269
  169.8 1.0 collective-permute-done.15.other_ref
  170.8 0.0 copy-done
  170.8 0.0 copy-done.1
  170.8 0.0 copy-done.2
  170.8 0.0 copy-done.3
  170.9 1.1 shard_map.122
  171.9 0.1 broadcast_in_dim.22
  172.0 16.0 %all_to_all.53.got_ref = bf16[8,448,128]{2,1,0:T(8,128)(2,1)S(1)} all-to-all(bf16[8,448,128]{2,1,0:T(8,128)(2,1)S(1)} %broadcast_in_dim.22), channel_id=1, replica_groups=mesh['line'=8,'place'=4,'core'=2,'tp'=8] {'tp'}, dimensions={0} | all-to-all | bytes 1835008 | tf_op jit(solution)/shard_map/all_to_all | solution.py:278
  188.0 1.0 shard_map.123
  (6 shorter events, 0.1 us)
Async XLA Ops:
  0.6 16.4 %collective-permute-start.2 = (bf16[2048,384]{1,0:T(8,128)(2,1)}, bf16[2048,384]{1,0:T(8,128)(2,1)S(1)}, u32[]{:S(2)}, u32[]{:S(2)}) collective-permute-start(bf16[2048,384]{1,0:T(8,128)(2,1)} %bitcast.15), channel_id=1, source_target_pairs={{0,8},{8,0},{1,9},{9,1},{2,10},{10,2},{3,11},{11,3},{4,12},{12,4},... | collective-permute-start | bytes 4718600 | tf_op jit(solution)/shard_map/ppermute | solution.py:269
  9.4 7.6 %collective-permute-start.3 = (bf16[256,2048]{1,0:T(8,128)(2,1)}, bf16[256,2048]{1,0:T(8,128)(2,1)S(1)}, u32[]{:S(2)}, u32[]{:S(2)}) collective-permute-start(bf16[256,2048]{1,0:T(8,128)(2,1)} %bitcast.17), channel_id=1, source_target_pairs={{0,8},{8,0},{1,9},{9,1},{2,10},{10,2},{3,11},{11,3},{4,12},{12,4},... | collective-permute-start | bytes 3145736 | tf_op jit(solution)/shard_map/ppermute | solution.py:269
  11.4 5.7 %collective-permute-start = (bf16[96,2048]{1,0:T(8,128)(2,1)}, bf16[96,2048]{1,0:T(8,128)(2,1)S(1)}, u32[]{:S(2)}, u32[]{:S(2)}) collective-permute-start(bf16[96,2048]{1,0:T(8,128)(2,1)} %bitcast.20), channel_id=1, source_target_pairs={{0,8},{8,0},{1,9},{9,1},{2,10},{10,2},{3,11},{11,3},{4,12},{12,4},... | collective-permute-start | bytes 1179656 | tf_op jit(solution)/shard_map/ppermute | solution.py:269
  13.8 3.3 %collective-permute-start.1 = (bf16[1,2048]{1,0:T(2,128)(2,1)}, bf16[1,2048]{1,0:T(2,128)(2,1)S(1)}, u32[]{:S(2)}, u32[]{:S(2)}) collective-permute-start(bf16[1,2048]{1,0:T(2,128)(2,1)} %refs_2_.1), channel_id=1, source_target_pairs={{0,8},{8,0},{1,9},{9,1},{2,10},{10,2},{3,11},{11,3},{4,12},{12,4},... | collective-permute-start | bytes 12296 | tf_op jit(solution)/shard_map/ppermute | solution.py:269
  33.3 12.0 %collective-permute-start.4 = (bf16[48,512]{1,0:T(8,128)(2,1)S(1)}, bf16[48,512]{1,0:T(8,128)(2,1)S(1)}, u32[]{:S(2)}, u32[]{:S(2)}) collective-permute-start(bf16[48,512]{1,0:T(8,128)(2,1)S(1)} %shard_map.114.early_0), channel_id=1, source_target_pairs={{0,16},{8,24},{16,32},{24,40},{32,48},{40,56},{48,64},{56,72},{64,... | collective-permute-start | bytes 147464 | tf_op jit(solution)/shard_map/ppermute | solution.py:274
  68.1 9.5 %collective-permute-start.5 = (bf16[48,512]{1,0:T(8,128)(2,1)S(1)}, bf16[48,512]{1,0:T(8,128)(2,1)S(1)}, u32[]{:S(2)}, u32[]{:S(2)}) collective-permute-start(bf16[48,512]{1,0:T(8,128)(2,1)S(1)} %shard_map.116.early_1), channel_id=1, source_target_pairs={{0,16},{8,24},{16,32},{24,40},{32,48},{40,56},{48,64},{56,72},{64,... | collective-permute-start | bytes 147464 | tf_op jit(solution)/shard_map/ppermute | solution.py:274
  99.3 9.2 %collective-permute-start.6 = (bf16[48,512]{1,0:T(8,128)(2,1)S(1)}, bf16[48,512]{1,0:T(8,128)(2,1)S(1)}, u32[]{:S(2)}, u32[]{:S(2)}) collective-permute-start(bf16[48,512]{1,0:T(8,128)(2,1)S(1)} %shard_map.118.early_2), channel_id=1, source_target_pairs={{0,16},{8,24},{16,32},{24,40},{32,48},{40,56},{48,64},{56,72},{64,... | collective-permute-start | bytes 147464 | tf_op jit(solution)/shard_map/ppermute | solution.py:274
  120.4 50.5 %copy-start = (bf16[4,256,48]{1,2,0:T(8,128)(2,1)S(1)}, bf16[4,256,48]{1,2,0:T(8,128)(2,1)}, u32[]{:S(2)}) copy-start(bf16[4,256,48]{1,2,0:T(8,128)(2,1)} %param.18) | copy-start | bytes 294916
  120.4 50.5 %copy-start.1 = (bf16[2,256,48]{1,2,0:T(8,128)(2,1)S(1)}, bf16[2,256,48]{1,2,0:T(8,128)(2,1)}, u32[]{:S(2)}) copy-start(bf16[2,256,48]{1,2,0:T(8,128)(2,1)} %param.17) | copy-start | bytes 147460
  120.4 50.5 %copy-start.2 = (s32[4,96,4]{1,2,0:T(4,128)S(1)}, s32[4,96,4]{1,2,0:T(4,128)}, u32[]{:S(2)}) copy-start(s32[4,96,4]{1,2,0:T(4,128)} %param.19) | copy-start | bytes 18436
  120.4 50.5 %copy-start.3 = (bf16[2,256]{1,0:T(2,128)(2,1)S(1)}, bf16[2,256]{1,0:T(2,128)(2,1)}, u32[]{:S(2)}) copy-start(bf16[2,256]{1,0:T(2,128)(2,1)} %talk_gain.1) | copy-start | bytes 3076
  130.4 6.8 %collective-permute-start.10 = (bf16[48,512]{1,0:T(8,128)(2,1)S(1)}, bf16[48,512]{1,0:T(8,128)(2,1)S(1)}, u32[]{:S(2)}, u32[]{:S(2)}) collective-permute-start(bf16[48,512]{1,0:T(8,128)(2,1)S(1)} %shard_map.120.last_ref), channel_id=1, source_target_pairs={{0,128},{8,136},{16,144},{24,152},{32,160},{40,168},{496,112},{504... | collective-permute-start | bytes 147464 | tf_op jit(solution)/shard_map/ppermute | solution.py:293
  131.7 6.8 %collective-permute-start.11 = (bf16[48,512]{1,0:T(8,128)(2,1)S(1)}, bf16[48,512]{1,0:T(8,128)(2,1)S(1)}, u32[]{:S(2)}, u32[]{:S(2)}) collective-permute-start(bf16[48,512]{1,0:T(8,128)(2,1)S(1)} %shard_map.120.last_ref), channel_id=1, source_target_pairs={{0,384},{8,392},{16,400},{24,408},{32,416},{40,424},{496,368},{504... | collective-permute-start | bytes 147464 | tf_op jit(solution)/shard_map/ppermute | solution.py:293
  133.0 7.4 %collective-permute-start.12 = (bf16[48,512]{1,0:T(8,128)(2,1)S(1)}, bf16[48,512]{1,0:T(8,128)(2,1)S(1)}, u32[]{:S(2)}, u32[]{:S(2)}) collective-permute-start(bf16[48,512]{1,0:T(8,128)(2,1)S(1)} %shard_map.120.last_ref), channel_id=1, source_target_pairs={{0,64},{8,72},{16,80},{24,88},{32,96},{40,104},{496,48},{504,56},{... | collective-permute-start | bytes 147464 | tf_op jit(solution)/shard_map/ppermute | solution.py:293
  134.3 19.8 %collective-permute-start.13 = (bf16[48,512]{1,0:T(8,128)(2,1)S(1)}, bf16[48,512]{1,0:T(8,128)(2,1)S(1)}, u32[]{:S(2)}, u32[]{:S(2)}) collective-permute-start(bf16[48,512]{1,0:T(8,128)(2,1)S(1)} %shard_map.120.last_ref), channel_id=1, source_target_pairs={{0,448},{8,456},{16,464},{24,472},{32,480},{40,488},{496,432},{504... | collective-permute-start | bytes 147464 | tf_op jit(solution)/shard_map/ppermute | solution.py:293
  135.6 18.5 %collective-permute-start.7 = (bf16[48,512]{1,0:T(8,128)(2,1)S(1)}, bf16[48,512]{1,0:T(8,128)(2,1)S(1)}, u32[]{:S(2)}, u32[]{:S(2)}) collective-permute-start(bf16[48,512]{1,0:T(8,128)(2,1)S(1)} %shard_map.120.last_ref), channel_id=1, source_target_pairs={{0,256},{8,264},{16,272},{24,280},{32,288},{40,296},{496,240},{504... | collective-permute-start | bytes 147464 | tf_op jit(solution)/shard_map/ppermute | solution.py:293
  137.2 17.0 %collective-permute-start.8 = (bf16[48,512]{1,0:T(8,128)(2,1)S(1)}, bf16[48,512]{1,0:T(8,128)(2,1)S(1)}, u32[]{:S(2)}, u32[]{:S(2)}) collective-permute-start(bf16[48,512]{1,0:T(8,128)(2,1)S(1)} %shard_map.120.last_ref), channel_id=1, source_target_pairs={{0,192},{8,200},{16,208},{24,216},{32,224},{40,232},{496,176},{504... | collective-permute-start | bytes 147464 | tf_op jit(solution)/shard_map/ppermute | solution.py:293
  138.5 15.7 %collective-permute-start.9 = (bf16[48,512]{1,0:T(8,128)(2,1)S(1)}, bf16[48,512]{1,0:T(8,128)(2,1)S(1)}, u32[]{:S(2)}, u32[]{:S(2)}) collective-permute-start(bf16[48,512]{1,0:T(8,128)(2,1)S(1)} %shard_map.120.last_ref), channel_id=1, source_target_pairs={{0,320},{8,328},{16,336},{24,344},{32,352},{40,360},{496,304},{504... | collective-permute-start | bytes 147464 | tf_op jit(solution)/shard_map/ppermute | solution.py:293
  140.4 14.6 %collective-permute-start.14 = (bf16[48,512]{1,0:T(8,128)(2,1)S(1)}, bf16[48,512]{1,0:T(8,128)(2,1)S(1)}, u32[]{:S(2)}, u32[]{:S(2)}) collective-permute-start(bf16[48,512]{1,0:T(8,128)(2,1)S(1)} %shard_map.121.latest_own), channel_id=1, source_target_pairs={{0,8},{8,0},{1,9},{9,1},{2,10},{10,2},{3,11},{11,3},{4,12},{12,4},... | collective-permute-start | bytes 147464 | tf_op jit(solution)/shard_map/ppermute | solution.py:269
  165.6 5.2 %collective-permute-start.15 = (bf16[4,48,512]{2,1,0:T(8,128)(2,1)S(1)}, bf16[4,48,512]{2,1,0:T(8,128)(2,1)S(1)}, u32[]{:S(2)}, u32[]{:S(2)}) collective-permute-start(bf16[4,48,512]{2,1,0:T(8,128)(2,1)S(1)} %all_to_all.52.own_ref), channel_id=1, source_target_pairs={{0,8},{8,0},{1,9},{9,1},{2,10},{10,2},{3,11},{11,3},{4,12},{12,4},... | collective-permute-start | bytes 589832 | tf_op jit(solution)/shard_map/ppermute | solution.py:269

commit v3 on v2

v3 whole, which is shorter than its diff:
```python
import functools

import jax
import jax.numpy as jnp
from jax import lax
from jax.experimental import pallas as pl
from jax.experimental.pallas import tpu as pltpu
from jax.sharding import PartitionSpec as P

D = 4096
H = 32
KVH = 8
HD = 64
NQ = 4
TICKS = 4
B = 96
CACHE = 16
HALF = B // 2
RATIO = H // KVH
EARLY = TICKS - 1
LANES = 128
FIRST = 24

epsilon = 1e-05
f32 = jnp.float32
bf16 = jnp.bfloat16
i32 = jnp.int32
CONTRACT_LAST = (((1,), (1,)), ((), ()))


def last_visible(tick, place_ref, lengths_ref):
    side, section = place_ref[0], place_ref[1]
    lens = lengths_ref[pl.ds(jnp.maximum(section - tick, 0), 1), :]
    row = lax.broadcasted_iota(i32, (HALF, B), 0)
    lane = lax.broadcasted_iota(i32, (HALF, B), 1)
    lens = jnp.where(lane == row + side * HALF, lens, 0)
    lens = jnp.sum(lens, axis=1, keepdims=True)
    ends = lens + lax.broadcasted_iota(i32, (HALF, 1), 0) * CACHE
    return jnp.concatenate([ends] * RATIO, axis=0)


def attention_terms(proj, ends, o_own, o_oth, pairs_ref, out_ref):
    shards, block = out_ref.shape[0], out_ref.shape[2] // 2
    stacked = jnp.concatenate([proj[:, r * HD : (r + 1) * HD] for r in range(RATIO)], axis=0)
    queries = (stacked.astype(bf16).astype(f32) * (HD**-0.5)).astype(bf16)
    queries = jnp.concatenate([queries, jnp.zeros_like(queries)], axis=1)
    pair_new = proj[:, RATIO * HD :].astype(bf16)
    pairs = pairs_ref[...]
    scores = lax.dot_general(queries, pairs, CONTRACT_LAST, preferred_element_type=f32)
    own_scores = lax.dot_general(queries, pair_new, CONTRACT_LAST, preferred_element_type=f32)
    rows = RATIO * HALF
    stream = lax.rem(lax.broadcasted_iota(i32, (rows, 1), 0), HALF)
    place = lax.broadcasted_iota(i32, (rows, HALF * CACHE), 1)
    visible = jnp.logical_and(place >= stream * CACHE, place < ends)
    scores = jnp.where(visible, scores, -jnp.inf)
    own_place = lax.broadcasted_iota(i32, (rows, HALF), 1)
    own_scores = jnp.where(own_place == stream, own_scores, -jnp.inf)
    row_max = jnp.maximum(
        jnp.max(scores, axis=-1, keepdims=True), jnp.max(own_scores, axis=-1, keepdims=True)
    )
    weights = jnp.exp(scores - row_max)
    own_weights = jnp.exp(own_scores - row_max)
    total = jnp.sum(weights, axis=-1, keepdims=True) + jnp.sum(own_weights, axis=-1, keepdims=True)
    share = 1.0 / total
    mixed = jnp.dot((weights * share).astype(bf16), pairs, preferred_element_type=f32)
    mixed = mixed + jnp.dot(
        (own_weights * share).astype(bf16), pair_new, preferred_element_type=f32
    )
    mixed = mixed[:, HD:].astype(bf16)
    heads = jnp.concatenate([mixed[r * HALF : (r + 1) * HALF] for r in range(RATIO)], axis=1)
    for j in range(shards):
        span = slice(j * block, (j + 1) * block)
        own = jnp.dot(heads, o_own[:, span], preferred_element_type=f32)
        oth = jnp.dot(heads, o_oth[:, span], preferred_element_type=f32)
        out_ref[j, :, :block] = own.astype(bf16)
        out_ref[j, :, block:] = oth.astype(bf16)


def pack_kernel(rows_src, gain_src, adapt_src, books_src, out_ref, gain_ref, semaphores):
    columns, entries = adapt_src.shape[1:]
    tables = [adapt_src.at[i] for i in range(adapt_src.shape[0])]
    tables += [books_src.at[q] for q in range(NQ)]
    below = pl.ds(B, columns)
    copies = [pltpu.make_async_copy(gain_src, gain_ref, semaphores.at[0])]
    copies += [pltpu.make_async_copy(rows_src, out_ref.at[:B], semaphores.at[1])]
    for i, source in enumerate(tables):
        target = out_ref.at[below, pl.ds(i * entries, entries)]
        copies += [pltpu.make_async_copy(source, target, semaphores.at[2 + i])]
    for copy in copies:
        copy.start()
    start = len(tables) * entries
    free = out_ref.shape[1] - start
    copies[0].wait()
    gain = gain_ref[...].astype(f32)
    pieces = [gain[:, j : j + free] for j in range(0, gain.shape[1], free)]
    pieces += [jnp.zeros((columns - len(pieces), free), f32)]
    out_ref[B:, start:] = jnp.concatenate(pieces, axis=0).astype(bf16)
    for copy in copies[1:]:
        copy.wait()


def unpacked_gain(packed_ref):
    width = packed_ref.shape[1]
    start = (2 + NQ) * (width // 8)
    held = packed_ref[B:, start:].astype(f32)
    count = width // (width - start)
    return jnp.concatenate([held[j : j + 1] for j in range(count)], axis=1)


def first_kernel(
    place_ref, packed_own, packed_oth, w_oth, o_oth, lens_src, w_src, o_src, cache_src,
    out_ref, shard_ref, g_own_ref, g_oth_ref, lengths_ref, w_own, o_own, cache_ref, semaphores,
):
    sources = (lens_src, w_src, o_src, cache_src)
    held = (lengths_ref, w_own, o_own, cache_ref)
    copies = [
        pltpu.make_async_copy(source, target, semaphores.at[i])
        for i, (source, target) in enumerate(zip(sources, held))
    ]
    for copy in copies:
        copy.start()
    side, column = place_ref[0], place_ref[2]
    block = shard_ref.shape[1] // 2
    mine = pl.ds(pl.multiple_of(side * HALF, HALF), HALF)
    own = packed_own[mine, :].astype(f32)
    oth = packed_oth[mine, :].astype(f32)
    squares = jnp.sum(own * own + oth * oth, axis=-1, keepdims=True)
    gains = [unpacked_gain(packed_own), unpacked_gain(packed_oth)]
    g_own_ref[...], g_oth_ref[...] = gains
    scaled_own = (own * gains[0]).astype(bf16)
    scaled_oth = (oth * gains[1]).astype(bf16)
    part = pl.ds(pl.multiple_of(column * block, block), block)
    shard_ref[:, :block] = packed_own[mine, part]
    shard_ref[:, block:] = packed_oth[mine, part]
    copies[0].wait()
    ends = last_visible(0, place_ref, lengths_ref)
    proj = jnp.dot(scaled_oth, w_oth[...], preferred_element_type=f32)
    copies[1].wait()
    proj = proj + jnp.dot(scaled_own, w_own[...], preferred_element_type=f32)
    proj = proj * lax.rsqrt(squares / D + epsilon)
    for copy in copies[2:]:
        copy.wait()
    attention_terms(proj, ends, o_own, o_oth, cache_ref.at[0], out_ref)


def later_kernel(
    tick, place_ref, lengths_ref, g_own, g_oth, w_own, w_oth, o_own, o_oth, cache_ref, x_ref,
    out_ref, inverse_ref,
):
    shards, block = x_ref.shape[0], x_ref.shape[2] // 2
    squares = jnp.zeros(x_ref.shape[1:], f32)
    proj = jnp.zeros((HALF, w_own.shape[1]), f32)
    for j in range(shards):
        span = slice(j * block, (j + 1) * block)
        rows = x_ref[j].astype(f32)
        squares = squares + rows * rows
        own = (rows[:, :block] * g_own[:, span]).astype(bf16)
        oth = (rows[:, block:] * g_oth[:, span]).astype(bf16)
        proj = proj + jnp.dot(own, w_own[span, :], preferred_element_type=f32)
        proj = proj + jnp.dot(oth, w_oth[span, :], preferred_element_type=f32)
    inverse_rms = lax.rsqrt(jnp.sum(squares, axis=-1, keepdims=True) / D + epsilon)
    inverse_ref[...] = jnp.broadcast_to(inverse_rms, inverse_ref.shape)
    proj = proj * inverse_rms
    ends = last_visible(tick, place_ref, lengths_ref)
    attention_terms(proj, ends, o_own, o_oth, cache_ref.at[tick], out_ref)


def sum_kernel(tick, place_ref, got_ref, shard_ref, inverse_ref, out_ref):
    section = place_ref[1]
    shard = shard_ref[...].astype(f32)
    total = shard
    for j in range(got_ref.shape[0]):
        total = total + got_ref[j].astype(f32)
    if tick:
        passed = shard * jnp.where(section == 0, inverse_ref[:, :1], 1.0)
        total = jnp.where(section >= tick, total, passed)
    out_ref[...] = total.astype(bf16)


def last_sum_kernel(
    place_ref, got_ref, shard_ref, inverse_ref, early_0, early_1, early_2, out_ref, latest_ref
):
    sum_kernel(EARLY, place_ref, got_ref, shard_ref, inverse_ref, out_ref)
    section = place_ref[1]
    latest = out_ref[...].astype(f32)
    for tick, early in ((2, early_2), (1, early_1), (0, early_0)):
        latest = jnp.where(section <= tick, early[...].astype(f32), latest)
    latest_ref[...] = latest.astype(bf16)


def holder_of(tick):
    return EARLY if tick == EARLY else EARLY - 1 - tick


def talk_kernel(
    place_ref, rows_ref, latest_ref, talk_gain, packed_own, packed_oth, codes_ref, out_ref
):
    side, column = place_ref[0], place_ref[2]
    block = rows_ref.shape[2] // 2
    columns, entries = packed_own.shape[0] - B, packed_own.shape[1] // 8
    first = side == 0
    gains = talk_gain[...].astype(f32)

    def halves(rows):
        own, oth = rows[:, :block].astype(f32), rows[:, block:].astype(f32)
        return jnp.where(first, own, oth), jnp.where(first, oth, own)

    def table(i):
        span = slice(i * entries, (i + 1) * entries)
        own, oth = packed_own[B:, span].astype(f32), packed_oth[B:, span].astype(f32)
        both = [jnp.where(first, own, oth), jnp.where(first, oth, own)]
        return jnp.concatenate(both, axis=0).astype(bf16)

    def beside(terms):
        return jnp.concatenate([terms[:columns], terms[columns:]], axis=1)

    def embedded(tick):
        total = jnp.zeros((2 * columns, B), f32)
        for q in range(NQ):
            ids = codes_ref[tick, q : q + 1, :] - column * entries
            hot = lax.broadcasted_iota(i32, (entries, B), 0) == ids
            hot = jnp.where(hot, 1.0, 0.0).astype(bf16)
            total = total + jnp.dot(books[q], hot, preferred_element_type=f32)
        return beside(jnp.where(first, total[:, :HALF], total[:, HALF:]))

    adapt = [table(0), table(1)]
    books = [table(2 + q) for q in range(NQ)]
    pieces = []
    for tick in range(TICKS):
        low, high = halves(rows_ref[holder_of(tick)])
        terms = jnp.zeros((2 * columns, HALF), f32)
        for i, part in enumerate((low, high)):
            scaled = (part * gains[i : i + 1]).astype(bf16)
            terms = terms + lax.dot_general(
                adapt[i], scaled, CONTRACT_LAST, preferred_element_type=f32
            )
        terms = beside(terms)
        pieces += [terms + embedded(tick)] if tick < EARLY else [terms, embedded(tick)]
    squares = jnp.sum(low * low + high * high, axis=1, keepdims=True)
    squares = jnp.concatenate([squares, squares], axis=0)
    upper = squares.astype(bf16).astype(f32)
    grid = jnp.concatenate(pieces, axis=0)
    grid = jnp.concatenate([grid, jnp.zeros((grid.shape[0], LANES - B), f32)], axis=1)
    grid = jnp.concatenate([grid, jnp.zeros((2 * LANES - grid.shape[0], LANES), f32)], axis=0)
    grid = grid.T[:B]
    lane = lax.broadcasted_iota(i32, grid.shape, 1)
    grid = jnp.where(lane == (TICKS + 1) * columns, upper, grid)
    grid = jnp.where(lane == (TICKS + 1) * columns + 1, squares - upper, grid)
    for c, part in enumerate(halves(latest_ref[...])):
        out_ref[c, :HALF] = grid[c * HALF : (c + 1) * HALF].astype(bf16)
        out_ref[c, HALF:] = part.astype(bf16)


def finish_kernel(got_ref, out_ref, leaving_ref):
    columns, block = out_ref.shape[1], got_ref.shape[2]
    shards = got_ref.shape[0] // 2
    tables = []
    for c in range(2):
        table = got_ref[c * shards, :HALF].astype(f32)
        for j in range(1, shards):
            table = table + got_ref[c * shards + j, :HALF].astype(f32)
        tables.append(table)
        for j in range(shards):
            rows = got_ref[c * shards + j, HALF:].astype(f32)
            leaving_ref[c * HALF : (c + 1) * HALF, j * block : (j + 1) * block] = rows
    table = jnp.concatenate(tables, axis=0)
    table = jnp.concatenate([table, jnp.zeros((LANES - B, block), f32)], axis=0).T
    for tick in range(EARLY):
        out_ref[tick] = table[tick * columns : (tick + 1) * columns, :B]
    base, at = EARLY * columns, (TICKS + 1) * columns
    squares = table[at : at + 1, :] + table[at + 1 : at + 2, :]
    rows = table[base : base + columns] * lax.rsqrt(squares / D + epsilon)
    rows = rows + table[base + columns : base + 2 * columns]
    out_ref[EARLY] = rows[:, :B]


def run(kernel, outs, *operands, scalars=True, limit=16):
    specs = [pl.BlockSpec(memory_space=pltpu.VMEM)] * len(operands)
    if scalars:
        specs[0] = pl.BlockSpec(memory_space=pltpu.SMEM)
    out_specs = jax.tree.map(lambda _: pl.BlockSpec(memory_space=pltpu.VMEM), outs)
    return pl.pallas_call(
        kernel,
        out_shape=outs,
        in_specs=specs,
        out_specs=out_specs,
        compiler_params=pltpu.CompilerParams(vmem_limit_bytes=limit * 2**20),
    )(*operands)


def shaped(*shape, dtype=bf16):
    return jax.ShapeDtypeStruct(shape, dtype)


SECTION = ("line", "place", "core")
LINES, PLACES = 8, 4
LINE = 2 * PLACES


def to_partner(value):
    return lax.ppermute(value, "core", [(0, 1), (1, 0)])


def to_next(value):
    count = LINES * LINE
    return lax.ppermute(value, SECTION, [(i, (i + 2) % count) for i in range(count)])


def exchange(blocks, axis="tp"):
    return lax.all_to_all(blocks, axis, 0, 0, tiled=True)


def replicate(block, count):
    return jnp.broadcast_to(block[None], (count,) + block.shape)


def across_lines(value, line):
    home = [LINES - 1 if place == EARLY else 0 for place in range(PLACES)]

    def sent(rows, start, step):
        return lax.ppermute(
            rows,
            SECTION,
            [
                ((home[i // 2] + d) % LINES * LINE + i, (home[i // 2] + d + step) % LINES * LINE + i)
                for d in start
                for i in range(LINE)
            ],
        )

    place = lax.axis_index("place")
    offset = lax.rem(line - jnp.where(place == EARLY, LINES - 1, 0) + LINES, LINES)
    some = jnp.where(offset == 0, value, jnp.zeros_like(value))
    for step in (4, 2, 6):
        some = some + sent(value, (0,), step)
    return some + sent(some, (0, 2, 4, 6), 1)


def body(arriving, norm_gain, w_qkv, w_out, cache, lengths, talk_gain, w_adapt, codebooks, codes):
    position = lax.axis_index(SECTION)
    column = lax.axis_index("tp")
    shards = lax.axis_size("tp")
    section = position // 2
    width = arriving.shape[2]
    block = width // shards
    columns = w_adapt.shape[2]
    place = jnp.stack([lax.rem(position, 2), section, column]).astype(i32)

    w_own, o_own = w_qkv[0], w_out[0]
    w_oth = to_partner(w_own)
    o_oth = to_partner(o_own)
    there = pl.BlockSpec(memory_space=pltpu.HBM)
    here = pl.BlockSpec(memory_space=pltpu.VMEM)
    sources = [arriving[0], norm_gain, w_adapt.transpose(0, 2, 1), codebooks.transpose(0, 2, 1)]
    packed_own = pl.pallas_call(
        pack_kernel,
        out_shape=shaped(B + columns, width),
        in_specs=[there] * len(sources),
        out_specs=here,
        scratch_shapes=[
            pltpu.VMEM(norm_gain.shape, bf16), pltpu.SemaphoreType.DMA((4 + NQ,))
        ],
        compiler_params=pltpu.CompilerParams(vmem_limit_bytes=8 * 2**20),
    )(*(pltpu.with_memory_space_constraint(v, pltpu.HBM) for v in sources))
    packed_oth = to_partner(packed_own)
    cache_rows = cache[0].reshape(TICKS, HALF * CACHE, -1)
    blocks = shaped(shards, HALF, 2 * block)
    piece = shaped(HALF, 2 * block)

    sources = [lengths, w_own, o_own, cache_rows]
    gain = shaped(1, width, dtype=f32)
    held = [gain, gain] + [shaped(*v.shape, dtype=v.dtype) for v in sources]
    terms, shard, g_own, g_oth, lengths, w_own, o_own, cache_rows = pl.pallas_call(
        first_kernel,
        out_shape=(blocks, piece, *held),
        in_specs=[pl.BlockSpec(memory_space=pltpu.SMEM)] + [here] * 4 + [there] * len(sources),
        out_specs=(here,) * (len(held) + 2),
        scratch_shapes=[pltpu.SemaphoreType.DMA((len(sources),))],
        compiler_params=pltpu.CompilerParams(vmem_limit_bytes=FIRST * 2**20),
    )(
        place, packed_own, packed_oth, w_oth, o_oth,
        *(pltpu.with_memory_space_constraint(v, pltpu.HBM) for v in sources),
    )
    shared = (place, lengths, g_own, g_oth, w_own, w_oth, o_own, o_oth, cache_rows)
    finals = []
    inverse = jnp.zeros((HALF, LANES), f32)
    for tick in range(EARLY):
        got = exchange(terms)
        finals.append(run(functools.partial(sum_kernel, tick), piece, place, got, shard, inverse))
        shard = to_next(finals[-1])
        rows = exchange(replicate(shard, shards))
        terms, inverse = run(
            functools.partial(later_kernel, tick + 1),
            (blocks, shaped(HALF, LANES, dtype=f32)),
            *shared, rows,
        )
    got = exchange(terms)
    held_rows, latest = run(
        last_sum_kernel, (piece, piece), place, got, shard, inverse, *finals
    )

    talk_rows = across_lines(held_rows, lax.axis_index("line"))
    talk_rows = exchange(replicate(talk_rows, PLACES), "place")
    payload = run(
        talk_kernel,
        shaped(2, B, block),
        place, talk_rows, latest, talk_gain, packed_own, packed_oth, codes.transpose(0, 2, 1),
    )
    payload = jnp.broadcast_to(payload[:, None], (2, shards, B, block))
    sums = exchange(payload.reshape(2 * shards, B, block), ("core", "tp"))
    talk, leaving = run(
        finish_kernel,
        (shaped(TICKS, columns, B, dtype=f32), shaped(B, width, dtype=f32)),
        sums,
        scalars=False,
    )
    return (leaving[None], talk.transpose(0, 2, 1))


def solution(mesh):
    devices = mesh.devices
    grid = jax.sharding.Mesh(
        devices.reshape(LINES, PLACES, 2, devices.shape[1]), SECTION + ("tp",)
    )
    placed = (
        P(SECTION, None, None),
        P(SECTION, None),
        P(SECTION, None, "tp"),
        P(SECTION, "tp", None),
        P(SECTION, None, None, None, "tp"),
        P(),
        P(None, "tp"),
        P(None, "tp", SECTION),
        P(None, "tp", SECTION),
        P(),
    )
    return jax.shard_map(
        body,
        mesh=grid,
        in_specs=placed,
        out_specs=(P(SECTION, None, None), P(None, None, SECTION)),
        check_vma=False,
    )
```

time: 190 us -> 184 us (0.968)
  starting transfers between devices: 49.7 us -> 27.2 us
  blocking collectives: 93.6 us -> 108 us
    ppermute x6 -> x3, starting transfers between devices: 33 us -> 13.1 us  [to_partner(): return lax.ppermute(value, 'core', [(0, 1), (1, 0)])]
    all_to_all x9, blocking collectives: 93.6 us -> 108 us  [exchange(): return lax.all_to_all(blocks, axis, 0, 0, tiled=True)]
    ppermute x7 -> x4, starting transfers between devices: 9.31 us -> 6.77 us  [sent(): lax.ppermute(rows, SECTION, [((home[i // 2] + d) % LINES * LINE + i, (hom...]
    ppermute x7 -> x4, waiting for transfers between devices: 0.02 us -> 2.29 us  [sent(): lax.ppermute(rows, SECTION, [((home[i // 2] + d) % LINES * LINE + i, (hom...]
    pallas_call x1 -> x2, Pallas kernels: 5.18 us -> 5.72 us  [the longest x1 4.63 us: body(): pl.pallas_call(first_kernel, out_shape=(blocks, piece, *held), in_specs=[...]
    pallas_call x10 -> x9, Pallas kernels: 12.9 us -> 13.2 us  [run(): pl.pallas_call(kernel, out_shape=outs, in_specs=specs, out_specs=out_spec...]
  transfers between devices with their start and end apart: 16 -> 10, of which waited for: 6 -> 6; matrix products, arithmetic and copies ran while one was open for 0% -> 0% of each run, Pallas kernels for 0% -> 1%
where the time goes in v3:
time: 184 us; the launch traced here: 182 us
  blocking collectives  108 us (59%)
  starting transfers between devices  27.2 us (15%)
  waiting for transfers between devices  27 us (15%)
  Pallas kernels  18.9 us (10%)
    all_to_all x9, blocking collectives, exchange(): return lax.all_to_all(blocks, axis, 0, 0, tiled=True)  108 us
    ppermute x3, waiting for transfers between devices, to_next(): lax.ppermute(value, SECTION, [(i, (i + 2) % count) for i in range(count)])  23 us
    pallas_call x9, Pallas kernels, run(): pl.pallas_call(kernel, out_shape=outs, in_specs=specs, out_specs=out_spec...  13.2 us
    ppermute x3, starting transfers between devices, to_partner(): return lax.ppermute(value, 'core', [(0, 1), (1, 0)])  13.1 us
    ppermute x3, starting transfers between devices, to_next(): lax.ppermute(value, SECTION, [(i, (i + 2) % count) for i in range(count)])  7.34 us
    ppermute x4, starting transfers between devices, sent(): lax.ppermute(rows, SECTION, [((home[i // 2] + d) % LINES * LINE + i, (hom...  6.77 us
    pallas_call x1, Pallas kernels, body(): pl.pallas_call(first_kernel, out_shape=(blocks, piece, *held), in_specs=[...  4.63 us
  transfers between devices with their start and end apart: 10, of which 6 were waited for; matrix products, arithmetic and copies ran while one was open for 0% of the time, Pallas kernels for 1%

profile of v3, /device:TPU:1, one launch (start us, length us, event | category | flops | bytes accessed | tf_op | source)
XLA Modules:
  0.0 182.2 jit_solution(17843738970345948616)
XLA Ops:
  0.6 8.8 %collective-permute-start.1 = (bf16[2048,384]{1,0:T(8,128)(2,1)}, bf16[2048,384]{1,0:T(8,128)(2,1)S(1)}, u32[]{:S(2)}, u32[]{:S(2)}) collective-permute-start(bf16[2048,384]{1,0:T(8,128)(2,1)} %bitcast.15), channel_id=1, source_target_pairs={{0,8},{8,0},{1,9},{9,1},{2,10},{10,2},{3,11},{11,3},{4,12},{12,4},... | collective-permute-start | bytes 4718600 | tf_op jit(solution)/shard_map/ppermute | solution.py:301
  9.4 1.9 %collective-permute-start.2 = (bf16[256,2048]{1,0:T(8,128)(2,1)}, bf16[256,2048]{1,0:T(8,128)(2,1)S(1)}, u32[]{:S(2)}, u32[]{:S(2)}) collective-permute-start(bf16[256,2048]{1,0:T(8,128)(2,1)} %bitcast.17), channel_id=1, source_target_pairs={{0,8},{8,0},{1,9},{9,1},{2,10},{10,2},{3,11},{11,3},{4,12},{12,4},... | collective-permute-start | bytes 3145736 | tf_op jit(solution)/shard_map/ppermute | solution.py:301
  11.4 1.1 shard_map.113.packed_own
  12.5 2.4 %collective-permute-start = (bf16[144,2048]{1,0:T(8,128)(2,1)S(1)}, bf16[144,2048]{1,0:T(8,128)(2,1)}, u32[]{:S(2)}, u32[]{:S(2)}) collective-permute-start(bf16[144,2048]{1,0:T(8,128)(2,1)S(1)} %shard_map.113.packed_own), channel_id=1, source_target_pairs={{0,8},{8,0},{1,9},{9,1},{2,10},{10,2},{3,11},{11,3},{4,12},{12,4},... | collective-permute-start | bytes 1769480 | tf_op jit(solution)/shard_map/ppermute | solution.py:301
  14.9 0.1 pad_add_fusion.place_ref
  15.0 1.6 collective-permute-done.packed_oth
  16.6 0.0 collective-permute-done.2.o_oth
  16.6 0.0 collective-permute-done.1.w_oth
  16.6 4.6 %shard_map.114 = (bf16[8,48,512]{2,1,0:T(8,128)(2,1)S(1)}, bf16[48,512]{1,0:T(8,128)(2,1)S(1)}, f32[1,2048]{1,0:T(1,128)S(1)}, f32[1,2048]{1,0:T(1,128)S(1)}, s3...) custom-call(s32[3]{0:T(128)S(1)} %pad_add_fusion.place_ref, ...), custom_call_target="tpu_custom_call" | custom-call | tf_op jit(solution)/shard_map/pallas_call | solution.py:373
  21.3 10.3 %all_to_all.45.got_ref = bf16[8,48,512]{2,1,0:T(8,128)(2,1)S(1)} all-to-all(bf16[8,48,512]{2,1,0:T(8,128)(2,1)S(1)} %get-tuple-element.26), channel_id=1, replica_groups=mesh['line'=8,'place'=4,'core'=2,'tp'=8] {'tp'}, dimensions={0} | all-to-all | bytes 786432 | tf_op jit(solution)/shard_map/all_to_all | solution.py:310
  31.6 0.6 shard_map.115.early_0
  32.2 3.5 %collective-permute-start.3 = (bf16[48,512]{1,0:T(8,128)(2,1)S(1)}, bf16[48,512]{1,0:T(8,128)(2,1)S(1)}, u32[]{:S(2)}, u32[]{:S(2)}) collective-permute-start(bf16[48,512]{1,0:T(8,128)(2,1)S(1)} %shard_map.115.early_0), channel_id=1, source_target_pairs={{0,16},{8,24},{16,32},{24,40},{32,48},{40,56},{48,64},{56,72},{64,... | collective-permute-start | bytes 147464 | tf_op jit(solution)/shard_map/ppermute | solution.py:306
  35.7 8.3 %collective-permute-done.3.shard_ref = bf16[48,512]{1,0:T(8,128)(2,1)S(1)} collective-permute-done((bf16[48,512]{1,0:T(8,128)(2,1)S(1)}, bf16[48,512]{1,0:T(8,128)(2,1)S(1)}, u32[]{:S(2)}, u32[]{:S(2)}) %collective-permute-start.3) | collective-permute-done | bytes 49184 | tf_op jit(solution)/shard_map/ppermute | solution.py:306
  44.1 10.5 %all_to_all.46.x_ref = bf16[8,48,512]{2,1,0:T(8,128)(2,1)S(1)} all-to-all(bf16[8,48,512]{2,1,0:T(8,128)(2,1)S(1)} %broadcast_in_dim.17), channel_id=1, replica_groups=mesh['line'=8,'place'=4,'core'=2,'tp'=8] {'tp'}, dimensions={0} | all-to-all | bytes 786432 | tf_op jit(solution)/shard_map/all_to_all | solution.py:310
  54.5 2.6 %shard_map.116 = (bf16[8,48,512]{2,1,0:T(8,128)(2,1)S(1)}, f32[48,128]{1,0:T(8,128)S(1)}) custom-call(s32[3]{0:T(128)S(1)} %pad_add_fusion.place_ref, s32[32,96]{1,0:T(8,128)S(1)} %get-tuple-element.20.lengths_ref, f32[1,2048]{1,0:T(1,128)S(1)} %get-tuple-element.21.g_own, f32[1,2048]{1,0:T(1,128)S(1)} %get-tuple-element.22.g_oth, ...), custom_call_target="tpu_custom_call" | custom-call | tf_op jit(solution)/shard_map/pallas_call | solution.py:282
  57.2 9.2 %all_to_all.47.got_ref = bf16[8,48,512]{2,1,0:T(8,128)(2,1)S(1)} all-to-all(bf16[8,48,512]{2,1,0:T(8,128)(2,1)S(1)} %get-tuple-element.28), channel_id=1, replica_groups=mesh['line'=8,'place'=4,'core'=2,'tp'=8] {'tp'}, dimensions={0} | all-to-all | bytes 786432 | tf_op jit(solution)/shard_map/all_to_all | solution.py:310
  66.4 0.6 shard_map.117.early_1
  67.0 1.9 %collective-permute-start.4 = (bf16[48,512]{1,0:T(8,128)(2,1)S(1)}, bf16[48,512]{1,0:T(8,128)(2,1)S(1)}, u32[]{:S(2)}, u32[]{:S(2)}) collective-permute-start(bf16[48,512]{1,0:T(8,128)(2,1)S(1)} %shard_map.117.early_1), channel_id=1, source_target_pairs={{0,16},{8,24},{16,32},{24,40},{32,48},{40,56},{48,64},{56,72},{64,... | collective-permute-start | bytes 147464 | tf_op jit(solution)/shard_map/ppermute | solution.py:306
  69.0 7.5 %collective-permute-done.4.shard_ref = bf16[48,512]{1,0:T(8,128)(2,1)S(1)} collective-permute-done((bf16[48,512]{1,0:T(8,128)(2,1)S(1)}, bf16[48,512]{1,0:T(8,128)(2,1)S(1)}, u32[]{:S(2)}, u32[]{:S(2)}) %collective-permute-start.4) | collective-permute-done | bytes 49184 | tf_op jit(solution)/shard_map/ppermute | solution.py:306
  76.5 9.3 %all_to_all.48.x_ref = bf16[8,48,512]{2,1,0:T(8,128)(2,1)S(1)} all-to-all(bf16[8,48,512]{2,1,0:T(8,128)(2,1)S(1)} %broadcast_in_dim.18), channel_id=1, replica_groups=mesh['line'=8,'place'=4,'core'=2,'tp'=8] {'tp'}, dimensions={0} | all-to-all | bytes 786432 | tf_op jit(solution)/shard_map/all_to_all | solution.py:310
  85.7 2.6 %shard_map.118 = (bf16[8,48,512]{2,1,0:T(8,128)(2,1)S(1)}, f32[48,128]{1,0:T(8,128)S(1)}) custom-call(s32[3]{0:T(128)S(1)} %pad_add_fusion.place_ref, s32[32,96]{1,0:T(8,128)S(1)} %get-tuple-element.20.lengths_ref, f32[1,2048]{1,0:T(1,128)S(1)} %get-tuple-element.21.g_own, f32[1,2048]{1,0:T(1,128)S(1)} %get-tuple-element.22.g_oth, ...), custom_call_target="tpu_custom_call" | custom-call | tf_op jit(solution)/shard_map/pallas_call | solution.py:282
  88.4 9.2 %all_to_all.49.got_ref = bf16[8,48,512]{2,1,0:T(8,128)(2,1)S(1)} all-to-all(bf16[8,48,512]{2,1,0:T(8,128)(2,1)S(1)} %get-tuple-element.30), channel_id=1, replica_groups=mesh['line'=8,'place'=4,'core'=2,'tp'=8] {'tp'}, dimensions={0} | all-to-all | bytes 786432 | tf_op jit(solution)/shard_map/all_to_all | solution.py:310
  97.6 0.6 shard_map.119.early_2
  98.2 1.9 %collective-permute-start.5 = (bf16[48,512]{1,0:T(8,128)(2,1)S(1)}, bf16[48,512]{1,0:T(8,128)(2,1)S(1)}, u32[]{:S(2)}, u32[]{:S(2)}) collective-permute-start(bf16[48,512]{1,0:T(8,128)(2,1)S(1)} %shard_map.119.early_2), channel_id=1, source_target_pairs={{0,16},{8,24},{16,32},{24,40},{32,48},{40,56},{48,64},{56,72},{64,... | collective-permute-start | bytes 147464 | tf_op jit(solution)/shard_map/ppermute | solution.py:306
  100.2 7.2 %collective-permute-done.5.shard_ref = bf16[48,512]{1,0:T(8,128)(2,1)S(1)} collective-permute-done((bf16[48,512]{1,0:T(8,128)(2,1)S(1)}, bf16[48,512]{1,0:T(8,128)(2,1)S(1)}, u32[]{:S(2)}, u32[]{:S(2)}) %collective-permute-start.5) | collective-permute-done | bytes 49184 | tf_op jit(solution)/shard_map/ppermute | solution.py:306
  107.4 9.2 %all_to_all.50.x_ref = bf16[8,48,512]{2,1,0:T(8,128)(2,1)S(1)} all-to-all(bf16[8,48,512]{2,1,0:T(8,128)(2,1)S(1)} %broadcast_in_dim.19), channel_id=1, replica_groups=mesh['line'=8,'place'=4,'core'=2,'tp'=8] {'tp'}, dimensions={0} | all-to-all | bytes 786432 | tf_op jit(solution)/shard_map/all_to_all | solution.py:310
  116.7 2.6 %shard_map.120 = (bf16[8,48,512]{2,1,0:T(8,128)(2,1)S(1)}, f32[48,128]{1,0:T(8,128)S(1)}) custom-call(s32[3]{0:T(128)S(1)} %pad_add_fusion.place_ref, s32[32,96]{1,0:T(8,128)S(1)} %get-tuple-element.20.lengths_ref, f32[1,2048]{1,0:T(1,128)S(1)} %get-tuple-element.21.g_own, f32[1,2048]{1,0:T(1,128)S(1)} %get-tuple-element.22.g_oth, ...), custom_call_target="tpu_custom_call" | custom-call | tf_op jit(solution)/shard_map/pallas_call | solution.py:282
  119.3 0.0 copy-start
  119.3 0.0 copy-start.1
  119.3 9.2 %all_to_all.51.got_ref = bf16[8,48,512]{2,1,0:T(8,128)(2,1)S(1)} all-to-all(bf16[8,48,512]{2,1,0:T(8,128)(2,1)S(1)} %get-tuple-element.32), channel_id=1, replica_groups=mesh['line'=8,'place'=4,'core'=2,'tp'=8] {'tp'}, dimensions={0} | all-to-all | bytes 786432 | tf_op jit(solution)/shard_map/all_to_all | solution.py:310
  128.6 0.6 shard_map.121
  129.2 1.3 collective-permute-start.8
  130.5 1.3 collective-permute-start.7
  131.8 2.9 %collective-permute-start.6 = (bf16[48,512]{1,0:T(8,128)(2,1)S(1)}, bf16[48,512]{1,0:T(8,128)(2,1)S(1)}, u32[]{:S(2)}, u32[]{:S(2)}) collective-permute-start(bf16[48,512]{1,0:T(8,128)(2,1)S(1)} %get-tuple-element.34), channel_id=1, source_target_pairs={{0,256},{8,264},{16,272},{24,280},{32,288},{40,296},{496,240},{504... | collective-permute-start | bytes 147464 | tf_op jit(solution)/shard_map/ppermute | solution.py:321
  134.7 0.0 collective-permute-done.8
  134.7 0.0 collective-permute-done.7
  134.8 1.1 collective-permute-done.6
  135.9 1.3 collective-permute-start.9
  137.2 1.2 collective-permute-done.9
  138.4 10.3 %all_to_all.52.rows_ref = bf16[4,48,512]{2,1,0:T(8,128)(2,1)S(1)} all-to-all(bf16[4,48,512]{2,1,0:T(8,128)(2,1)S(1)} %broadcast_in_dim.21), channel_id=1, replica_groups=mesh['line'=8,'place'=4,'core'=2,'tp'=8] {'place'}, dimensions={0} | all-to-all | bytes 393216 | tf_op jit(solution)/shard_map/all_to_all | solution.py:310
  148.7 0.0 copy-done
  148.7 0.0 copy-done.1
  148.7 1.8 shard_map.122
  150.5 0.1 broadcast_in_dim.22
  150.6 30.6 %all_to_all.53.got_ref = bf16[16,96,256]{2,1,0:T(8,128)(2,1)S(1)} all-to-all(bf16[16,96,256]{2,1,0:T(8,128)(2,1)S(1)} %bitcast.14), channel_id=1, replica_groups=mesh['line'=8,'place'=4,'core'=2,'tp'=8] {'core','tp'}, dimensions={0} | all-to-all | bytes 1572864 | tf_op jit(solution)/shard_map/all_to_all | solution.py:310
  181.2 1.0 shard_map.123
  (7 shorter events, 0.1 us)
Async XLA Ops:
  0.6 16.0 %collective-permute-start.1 = (bf16[2048,384]{1,0:T(8,128)(2,1)}, bf16[2048,384]{1,0:T(8,128)(2,1)S(1)}, u32[]{:S(2)}, u32[]{:S(2)}) collective-permute-start(bf16[2048,384]{1,0:T(8,128)(2,1)} %bitcast.15), channel_id=1, source_target_pairs={{0,8},{8,0},{1,9},{9,1},{2,10},{10,2},{3,11},{11,3},{4,12},{12,4},... | collective-permute-start | bytes 4718600 | tf_op jit(solution)/shard_map/ppermute | solution.py:301
  9.4 7.2 %collective-permute-start.2 = (bf16[256,2048]{1,0:T(8,128)(2,1)}, bf16[256,2048]{1,0:T(8,128)(2,1)S(1)}, u32[]{:S(2)}, u32[]{:S(2)}) collective-permute-start(bf16[256,2048]{1,0:T(8,128)(2,1)} %bitcast.17), channel_id=1, source_target_pairs={{0,8},{8,0},{1,9},{9,1},{2,10},{10,2},{3,11},{11,3},{4,12},{12,4},... | collective-permute-start | bytes 3145736 | tf_op jit(solution)/shard_map/ppermute | solution.py:301
  12.5 4.2 %collective-permute-start = (bf16[144,2048]{1,0:T(8,128)(2,1)S(1)}, bf16[144,2048]{1,0:T(8,128)(2,1)}, u32[]{:S(2)}, u32[]{:S(2)}) collective-permute-start(bf16[144,2048]{1,0:T(8,128)(2,1)S(1)} %shard_map.113.packed_own), channel_id=1, source_target_pairs={{0,8},{8,0},{1,9},{9,1},{2,10},{10,2},{3,11},{11,3},{4,12},{12,4},... | collective-permute-start | bytes 1769480 | tf_op jit(solution)/shard_map/ppermute | solution.py:301
  32.2 11.8 %collective-permute-start.3 = (bf16[48,512]{1,0:T(8,128)(2,1)S(1)}, bf16[48,512]{1,0:T(8,128)(2,1)S(1)}, u32[]{:S(2)}, u32[]{:S(2)}) collective-permute-start(bf16[48,512]{1,0:T(8,128)(2,1)S(1)} %shard_map.115.early_0), channel_id=1, source_target_pairs={{0,16},{8,24},{16,32},{24,40},{32,48},{40,56},{48,64},{56,72},{64,... | collective-permute-start | bytes 147464 | tf_op jit(solution)/shard_map/ppermute | solution.py:306
  67.0 9.4 %collective-permute-start.4 = (bf16[48,512]{1,0:T(8,128)(2,1)S(1)}, bf16[48,512]{1,0:T(8,128)(2,1)S(1)}, u32[]{:S(2)}, u32[]{:S(2)}) collective-permute-start(bf16[48,512]{1,0:T(8,128)(2,1)S(1)} %shard_map.117.early_1), channel_id=1, source_target_pairs={{0,16},{8,24},{16,32},{24,40},{32,48},{40,56},{48,64},{56,72},{64,... | collective-permute-start | bytes 147464 | tf_op jit(solution)/shard_map/ppermute | solution.py:306
  98.2 9.2 %collective-permute-start.5 = (bf16[48,512]{1,0:T(8,128)(2,1)S(1)}, bf16[48,512]{1,0:T(8,128)(2,1)S(1)}, u32[]{:S(2)}, u32[]{:S(2)}) collective-permute-start(bf16[48,512]{1,0:T(8,128)(2,1)S(1)} %shard_map.119.early_2), channel_id=1, source_target_pairs={{0,16},{8,24},{16,32},{24,40},{32,48},{40,56},{48,64},{56,72},{64,... | collective-permute-start | bytes 147464 | tf_op jit(solution)/shard_map/ppermute | solution.py:306
  119.3 29.4 %copy-start = (s32[4,96,4]{1,2,0:T(4,128)S(1)}, s32[4,96,4]{1,2,0:T(4,128)}, u32[]{:S(2)}) copy-start(s32[4,96,4]{1,2,0:T(4,128)} %param.19) | copy-start | bytes 18436
  119.3 29.4 %copy-start.1 = (bf16[2,256]{1,0:T(2,128)(2,1)S(1)}, bf16[2,256]{1,0:T(2,128)(2,1)}, u32[]{:S(2)}) copy-start(bf16[2,256]{1,0:T(2,128)(2,1)} %talk_gain.1) | copy-start | bytes 3076
  129.2 5.5 %collective-permute-start.8 = (bf16[48,512]{1,0:T(8,128)(2,1)S(1)}, bf16[48,512]{1,0:T(8,128)(2,1)S(1)}, u32[]{:S(2)}, u32[]{:S(2)}) collective-permute-start(bf16[48,512]{1,0:T(8,128)(2,1)S(1)} %get-tuple-element.34), channel_id=1, source_target_pairs={{0,384},{8,392},{16,400},{24,408},{32,416},{40,424},{496,368},{504... | collective-permute-start | bytes 147464 | tf_op jit(solution)/shard_map/ppermute | solution.py:321
  130.5 4.2 %collective-permute-start.7 = (bf16[48,512]{1,0:T(8,128)(2,1)S(1)}, bf16[48,512]{1,0:T(8,128)(2,1)S(1)}, u32[]{:S(2)}, u32[]{:S(2)}) collective-permute-start(bf16[48,512]{1,0:T(8,128)(2,1)S(1)} %get-tuple-element.34), channel_id=1, source_target_pairs={{0,128},{8,136},{16,144},{24,152},{32,160},{40,168},{496,112},{504... | collective-permute-start | bytes 147464 | tf_op jit(solution)/shard_map/ppermute | solution.py:321
  131.8 4.1 %collective-permute-start.6 = (bf16[48,512]{1,0:T(8,128)(2,1)S(1)}, bf16[48,512]{1,0:T(8,128)(2,1)S(1)}, u32[]{:S(2)}, u32[]{:S(2)}) collective-permute-start(bf16[48,512]{1,0:T(8,128)(2,1)S(1)} %get-tuple-element.34), channel_id=1, source_target_pairs={{0,256},{8,264},{16,272},{24,280},{32,288},{40,296},{496,240},{504... | collective-permute-start | bytes 147464 | tf_op jit(solution)/shard_map/ppermute | solution.py:321
  135.9 2.5 %collective-permute-start.9 = (bf16[48,512]{1,0:T(8,128)(2,1)S(1)}, bf16[48,512]{1,0:T(8,128)(2,1)S(1)}, u32[]{:S(2)}, u32[]{:S(2)}) collective-permute-start(bf16[48,512]{1,0:T(8,128)(2,1)S(1)} %add_add_fusion), channel_id=1, source_target_pairs={{0,64},{8,72},{16,80},{24,88},{32,96},{40,104},{496,48},{504,56},{... | collective-permute-start | bytes 147464 | tf_op jit(solution)/shard_map/ppermute | solution.py:321

commit v4 on v3

--- a/solution.py
+++ b/solution.py
@@ -19,7 +19,6 @@
 RATIO = H // KVH
 EARLY = TICKS - 1
 LANES = 128
-FIRST = 24
 
 epsilon = 1e-05
 f32 = jnp.float32
@@ -107,18 +106,21 @@
     return jnp.concatenate([held[j : j + 1] for j in range(count)], axis=1)
 
 
-def first_kernel(
-    place_ref, packed_own, packed_oth, w_oth, o_oth, lens_src, w_src, o_src, cache_src,
-    out_ref, shard_ref, g_own_ref, g_oth_ref, lengths_ref, w_own, o_own, cache_ref, semaphores,
-):
-    sources = (lens_src, w_src, o_src, cache_src)
-    held = (lengths_ref, w_own, o_own, cache_ref)
+def load_kernel(*refs):
+    count = (len(refs) - 1) // 2
     copies = [
-        pltpu.make_async_copy(source, target, semaphores.at[i])
-        for i, (source, target) in enumerate(zip(sources, held))
+        pltpu.make_async_copy(refs[i], refs[count + i], refs[-1].at[i]) for i in range(count)
     ]
     for copy in copies:
         copy.start()
+    for copy in copies:
+        copy.wait()
+
+
+def first_kernel(
+    place_ref, lengths_ref, packed_own, packed_oth, w_own, w_oth, o_own, o_oth, cache_ref,
+    out_ref, shard_ref, g_own_ref, g_oth_ref,
+):
     side, column = place_ref[0], place_ref[2]
     block = shard_ref.shape[1] // 2
     mine = pl.ds(pl.multiple_of(side * HALF, HALF), HALF)
@@ -127,19 +129,15 @@
     squares = jnp.sum(own * own + oth * oth, axis=-1, keepdims=True)
     gains = [unpacked_gain(packed_own), unpacked_gain(packed_oth)]
     g_own_ref[...], g_oth_ref[...] = gains
-    scaled_own = (own * gains[0]).astype(bf16)
-    scaled_oth = (oth * gains[1]).astype(bf16)
     part = pl.ds(pl.multiple_of(column * block, block), block)
     shard_ref[:, :block] = packed_own[mine, part]
     shard_ref[:, block:] = packed_oth[mine, part]
-    copies[0].wait()
+    scaled = (own * gains[0]).astype(bf16)
+    proj = jnp.dot(scaled, w_own[...], preferred_element_type=f32)
+    scaled = (oth * gains[1]).astype(bf16)
+    proj = proj + jnp.dot(scaled, w_oth[...], preferred_element_type=f32)
+    proj = proj * lax.rsqrt(squares / D + epsilon)
     ends = last_visible(0, place_ref, lengths_ref)
-    proj = jnp.dot(scaled_oth, w_oth[...], preferred_element_type=f32)
-    copies[1].wait()
-    proj = proj + jnp.dot(scaled_own, w_own[...], preferred_element_type=f32)
-    proj = proj * lax.rsqrt(squares / D + epsilon)
-    for copy in copies[2:]:
-        copy.wait()
     attention_terms(proj, ends, o_own, o_oth, cache_ref.at[0], out_ref)
 
 
@@ -172,7 +170,7 @@
     for j in range(got_ref.shape[0]):
         total = total + got_ref[j].astype(f32)
     if tick:
-        passed = shard * jnp.where(section == 0, inverse_ref[:, :1], 1.0)
+        passed = shard * jnp.where(section == tick - 1, inverse_ref[:, :1], 1.0)
         total = jnp.where(section >= tick, total, passed)
     out_ref[...] = total.astype(bf16)
 
@@ -188,10 +186,6 @@
     latest_ref[...] = latest.astype(bf16)
 
 
-def holder_of(tick):
-    return EARLY if tick == EARLY else EARLY - 1 - tick
-
-
 def talk_kernel(
     place_ref, rows_ref, latest_ref, talk_gain, packed_own, packed_oth, codes_ref, out_ref
 ):
@@ -211,31 +205,31 @@
         both = [jnp.where(first, own, oth), jnp.where(first, oth, own)]
         return jnp.concatenate(both, axis=0).astype(bf16)
 
-    def beside(terms):
+    def beside(terms, tick):
+        terms = terms[:, tick * HALF : (tick + 1) * HALF]
         return jnp.concatenate([terms[:columns], terms[columns:]], axis=1)
 
-    def embedded(tick):
-        total = jnp.zeros((2 * columns, B), f32)
-        for q in range(NQ):
-            ids = codes_ref[tick, q : q + 1, :] - column * entries
-            hot = lax.broadcasted_iota(i32, (entries, B), 0) == ids
-            hot = jnp.where(hot, 1.0, 0.0).astype(bf16)
-            total = total + jnp.dot(books[q], hot, preferred_element_type=f32)
-        return beside(jnp.where(first, total[:, :HALF], total[:, HALF:]))
-
-    adapt = [table(0), table(1)]
-    books = [table(2 + q) for q in range(NQ)]
-    pieces = []
-    for tick in range(TICKS):
-        low, high = halves(rows_ref[holder_of(tick)])
-        terms = jnp.zeros((2 * columns, HALF), f32)
-        for i, part in enumerate((low, high)):
-            scaled = (part * gains[i : i + 1]).astype(bf16)
-            terms = terms + lax.dot_general(
-                adapt[i], scaled, CONTRACT_LAST, preferred_element_type=f32
-            )
-        terms = beside(terms)
-        pieces += [terms + embedded(tick)] if tick < EARLY else [terms, embedded(tick)]
+    def my_ids(tick, q):
+        ids = codes_ref[tick, q : q + 1, :]
+        return jnp.where(first, ids[:, :HALF], ids[:, HALF:]) - column * entries
+
+    embedded = jnp.zeros((2 * columns, TICKS * HALF), f32)
+    for q in range(NQ):
+        ids = jnp.concatenate([my_ids(tick, q) for tick in range(TICKS)], axis=1)
+        hot = lax.broadcasted_iota(i32, (entries, TICKS * HALF), 0) == ids
+        hot = jnp.where(hot, 1.0, 0.0).astype(bf16)
+        embedded = embedded + jnp.dot(table(2 + q), hot, preferred_element_type=f32)
+    adapted = jnp.zeros((2 * columns, TICKS * HALF), f32)
+    low, high = halves(rows_ref[...].reshape(TICKS * HALF, 2 * block))
+    for i, part in enumerate((low, high)):
+        scaled = (part * gains[i : i + 1]).astype(bf16)
+        adapted = adapted + lax.dot_general(
+            table(i), scaled, CONTRACT_LAST, preferred_element_type=f32
+        )
+    low, high = low[EARLY * HALF :], high[EARLY * HALF :]
+    both = adapted + embedded
+    pieces = [beside(both, tick) for tick in range(EARLY)]
+    pieces += [beside(adapted, EARLY), beside(embedded, EARLY)]
     squares = jnp.sum(low * low + high * high, axis=1, keepdims=True)
     squares = jnp.concatenate([squares, squares], axis=0)
     upper = squares.astype(bf16).astype(f32)
@@ -301,9 +295,10 @@
     return lax.ppermute(value, "core", [(0, 1), (1, 0)])
 
 
-def to_next(value):
-    count = LINES * LINE
-    return lax.ppermute(value, SECTION, [(i, (i + 2) % count) for i in range(count)])
+def to_next(value, tick):
+    count, kept = LINES * LINE, 2 * tick
+    pairs = [(i, i) for i in range(kept)] + [(i, i + 2) for i in range(kept, count - 2)]
+    return lax.ppermute(value, SECTION, pairs + [(count - 2 + c, kept + c) for c in range(2)])
 
 
 def exchange(blocks, axis="tp"):
@@ -317,23 +312,16 @@
 def across_lines(value, line):
     home = [LINES - 1 if place == EARLY else 0 for place in range(PLACES)]
 
-    def sent(rows, start, step):
-        return lax.ppermute(
-            rows,
-            SECTION,
-            [
-                ((home[i // 2] + d) % LINES * LINE + i, (home[i // 2] + d + step) % LINES * LINE + i)
-                for d in start
-                for i in range(LINE)
-            ],
-        )
+    def sent(rows, *hops):
+        at = lambda i, d: (home[i // 2] + d) % LINES * LINE + i
+        pairs = [(at(i, start), at(i, end)) for start, end in hops for i in range(LINE)]
+        return lax.ppermute(rows, SECTION, pairs)
 
     place = lax.axis_index("place")
     offset = lax.rem(line - jnp.where(place == EARLY, LINES - 1, 0) + LINES, LINES)
     some = jnp.where(offset == 0, value, jnp.zeros_like(value))
-    for step in (4, 2, 6):
-        some = some + sent(value, (0,), step)
-    return some + sent(some, (0, 2, 4, 6), 1)
+    some = some + sent(value, (0, 7)) + sent(value, (0, 1))
+    return some + sent(some, (1, 2), (7, 6)) + sent(some, (0, 4), (1, 3), (7, 5))
 
 
 def body(arriving, norm_gain, w_qkv, w_out, cache, lengths, talk_gain, w_adapt, codebooks, codes):
@@ -367,27 +355,28 @@
     blocks = shaped(shards, HALF, 2 * block)
     piece = shaped(HALF, 2 * block)
 
-    sources = [lengths, w_own, o_own, cache_rows]
+    sources, _ = lax.optimization_barrier(([lengths, w_own, o_own, cache_rows], packed_own))
+    lengths, w_own, o_own, cache_rows = pl.pallas_call(
+        load_kernel,
+        out_shape=tuple(shaped(*v.shape, dtype=v.dtype) for v in sources),
+        in_specs=[there] * len(sources),
+        out_specs=(here,) * len(sources),
+        scratch_shapes=[pltpu.SemaphoreType.DMA((len(sources),))],
+        compiler_params=pltpu.CompilerParams(vmem_limit_bytes=8 * 2**20),
+        cost_estimate=pl.CostEstimate(flops=0, bytes_accessed=7 * 2**20, transcendentals=0),
+    )(*(pltpu.with_memory_space_constraint(v, pltpu.HBM) for v in sources))
+    weights = (w_own, w_oth, o_own, o_oth, cache_rows)
     gain = shaped(1, width, dtype=f32)
-    held = [gain, gain] + [shaped(*v.shape, dtype=v.dtype) for v in sources]
-    terms, shard, g_own, g_oth, lengths, w_own, o_own, cache_rows = pl.pallas_call(
-        first_kernel,
-        out_shape=(blocks, piece, *held),
-        in_specs=[pl.BlockSpec(memory_space=pltpu.SMEM)] + [here] * 4 + [there] * len(sources),
-        out_specs=(here,) * (len(held) + 2),
-        scratch_shapes=[pltpu.SemaphoreType.DMA((len(sources),))],
-        compiler_params=pltpu.CompilerParams(vmem_limit_bytes=FIRST * 2**20),
-    )(
-        place, packed_own, packed_oth, w_oth, o_oth,
-        *(pltpu.with_memory_space_constraint(v, pltpu.HBM) for v in sources),
-    )
-    shared = (place, lengths, g_own, g_oth, w_own, w_oth, o_own, o_oth, cache_rows)
+    terms, shard, g_own, g_oth = run(
+        first_kernel, (blocks, piece, gain, gain), place, lengths, packed_own, packed_oth, *weights
+    )
+    shared = (place, lengths, g_own, g_oth, *weights)
     finals = []
     inverse = jnp.zeros((HALF, LANES), f32)
     for tick in range(EARLY):
         got = exchange(terms)
         finals.append(run(functools.partial(sum_kernel, tick), piece, place, got, shard, inverse))
-        shard = to_next(finals[-1])
+        shard = to_next(finals[-1], tick)
         rows = exchange(replicate(shard, shards))
         terms, inverse = run(
             functools.partial(later_kernel, tick + 1),

time: 184 us -> 179 us (0.973)
  waiting for transfers between devices: 27 us -> 10.1 us
  starting transfers between devices: 27.2 us -> 39.3 us
    ppermute x7, waiting for transfers between devices: 25.3 us -> 10 us  [the longest x3 8.42 us: to_next(): lax.ppermute(value, SECTION, pairs + [(count - 2 + c, kept + c) for c in...]
    ppermute x7, starting transfers between devices: 14.1 us -> 26.2 us  [the longest x4 21.6 us: sent(): return lax.ppermute(rows, SECTION, pairs)]
    pallas_call x9 -> x10, Pallas kernels: 13.2 us -> 16.2 us  [run(): pl.pallas_call(kernel, out_shape=outs, in_specs=specs, out_specs=out_spec...]
    pallas_call x1, Pallas kernels: 4.63 us -> 1.98 us  [body(): pl.pallas_call(load_kernel, out_shape=tuple((shaped(*v.shape, dtype=v.dty...]
  transfers between devices with their start and end apart: 10 -> 10, of which waited for: 6 -> 3; matrix products, arithmetic and copies ran while one was open for 0% -> 0% of each run, Pallas kernels for 1% -> 2%
where the time goes in v4:
time: 179 us; the launch traced here: 178 us
  blocking collectives  108 us (60%)
  starting transfers between devices  39.3 us (22%)
  Pallas kernels  19.3 us (11%)
  waiting for transfers between devices  10.1 us (6%)
    all_to_all x9, blocking collectives, exchange(): return lax.all_to_all(blocks, axis, 0, 0, tiled=True)  108 us
    ppermute x4, starting transfers between devices, sent(): return lax.ppermute(rows, SECTION, pairs)  21.6 us
    pallas_call x10, Pallas kernels, run(): pl.pallas_call(kernel, out_shape=outs, in_specs=specs, out_specs=out_spec...  16.2 us
    ppermute x3, starting transfers between devices, to_partner(): return lax.ppermute(value, 'core', [(0, 1), (1, 0)])  13.1 us
    ppermute x3, waiting for transfers between devices, to_next(): lax.ppermute(value, SECTION, pairs + [(count - 2 + c, kept + c) for c in...  8.42 us
    ppermute x3, starting transfers between devices, to_next(): lax.ppermute(value, SECTION, pairs + [(count - 2 + c, kept + c) for c in...  4.63 us
  transfers between devices with their start and end apart: 10, of which 3 were waited for; matrix products, arithmetic and copies ran while one was open for 0% of the time, Pallas kernels for 2%

profile of v4, /device:TPU:1, one launch (start us, length us, event | category | flops | bytes accessed | tf_op | source)
XLA Modules:
  0.0 178.0 jit_solution(4166624624871865648)
XLA Ops:
  0.6 8.8 %collective-permute-start.1 = (bf16[2048,384]{1,0:T(8,128)(2,1)}, bf16[2048,384]{1,0:T(8,128)(2,1)S(1)}, u32[]{:S(2)}, u32[]{:S(2)}) collective-permute-start(bf16[2048,384]{1,0:T(8,128)(2,1)} %bitcast.15), channel_id=1, source_target_pairs={{0,8},{8,0},{1,9},{9,1},{2,10},{10,2},{3,11},{11,3},{4,12},{12,4},... | collective-permute-start | bytes 4718600 | tf_op jit(solution)/shard_map/ppermute | solution.py:295
  9.4 1.9 %collective-permute-start.2 = (bf16[256,2048]{1,0:T(8,128)(2,1)}, bf16[256,2048]{1,0:T(8,128)(2,1)S(1)}, u32[]{:S(2)}, u32[]{:S(2)}) collective-permute-start(bf16[256,2048]{1,0:T(8,128)(2,1)} %bitcast.17), channel_id=1, source_target_pairs={{0,8},{8,0},{1,9},{9,1},{2,10},{10,2},{3,11},{11,3},{4,12},{12,4},... | collective-permute-start | bytes 3145736 | tf_op jit(solution)/shard_map/ppermute | solution.py:295
  11.4 1.1 shard_map.113.packed_own
  12.5 2.4 %collective-permute-start = (bf16[144,2048]{1,0:T(8,128)(2,1)S(1)}, bf16[144,2048]{1,0:T(8,128)(2,1)}, u32[]{:S(2)}, u32[]{:S(2)}) collective-permute-start(bf16[144,2048]{1,0:T(8,128)(2,1)S(1)} %shard_map.113.packed_own), channel_id=1, source_target_pairs={{0,8},{8,0},{1,9},{9,1},{2,10},{10,2},{3,11},{11,3},{4,12},{12,4},... | collective-permute-start | bytes 1769480 | tf_op jit(solution)/shard_map/ppermute | solution.py:295
  14.9 2.0 %shard_map.114 = (s32[32,96]{1,0:T(8,128)S(1)}, bf16[2048,384]{1,0:T(8,128)(2,1)S(1)}, bf16[256,2048]{1,0:T(8,128)(2,1)S(1)}, bf16[4,768,128]{2,1,0:T(8,128)(2,1)S(1)}) custom-call(s32[32,96]{1,0:T(8,128)} %refs_0_, bf16[2048,384]{1,0:T(8,128)(2,1)} %bitcast.16, bf16[256,2048]{1,0:T(8,128)(2,1)} %bitcast.18, bf16[4,768,128]{2,1,0:T(8,128)(2,1)} %bitcast.19), custom_call_target="tpu_custom_call" | custom-call | bytes 7340032 | tf_op jit(solution)/shard_map/pallas_call | solution.py:359
  16.9 0.1 pad_add_fusion.place_ref
  17.0 0.0 collective-permute-done.packed_oth
  17.0 0.0 collective-permute-done.2.o_oth
  17.0 0.0 collective-permute-done.1.w_oth
  17.0 3.1 %shard_map.115 = (bf16[8,48,512]{2,1,0:T(8,128)(2,1)S(1)}, bf16[48,512]{1,0:T(8,128)(2,1)S(1)}, f32[1,2048]{1,0:T(1,128)S(1)}, f32[1,2048]{1,0:T(1,128)S(1)}) custom-call(s32[3]{0:T(128)S(1)} %pad_add_fusion.place_ref, s32[32,96]{1,0:T(8,128)S(1)} %get-tuple-element.28.lengths_ref, bf16[144,2048]{1,0:T(8,128)(2,1)S(1)} %shard_map.113.packed_own, ...), custom_call_target="tpu_custom_call" | custom-call | tf_op jit(solution)/shard_map/pallas_call | solution.py:276
  20.1 10.6 %all_to_all.45.got_ref = bf16[8,48,512]{2,1,0:T(8,128)(2,1)S(1)} all-to-all(bf16[8,48,512]{2,1,0:T(8,128)(2,1)S(1)} %get-tuple-element.34), channel_id=1, replica_groups=mesh['line'=8,'place'=4,'core'=2,'tp'=8] {'tp'}, dimensions={0} | all-to-all | bytes 786432 | tf_op jit(solution)/shard_map/all_to_all | solution.py:305
  30.8 0.6 shard_map.116.early_0
  31.4 3.3 %collective-permute-start.3 = (bf16[48,512]{1,0:T(8,128)(2,1)S(1)}, bf16[48,512]{1,0:T(8,128)(2,1)S(1)}, u32[]{:S(2)}, u32[]{:S(2)}) collective-permute-start(bf16[48,512]{1,0:T(8,128)(2,1)S(1)} %shard_map.116.early_0), channel_id=1, source_target_pairs={{0,16},{8,24},{16,32},{24,40},{32,48},{40,56},{48,64},{56,72},{64,... | collective-permute-start | bytes 147464 | tf_op jit(solution)/shard_map/ppermute | solution.py:301
  34.7 8.4 %collective-permute-done.3.shard_ref = bf16[48,512]{1,0:T(8,128)(2,1)S(1)} collective-permute-done((bf16[48,512]{1,0:T(8,128)(2,1)S(1)}, bf16[48,512]{1,0:T(8,128)(2,1)S(1)}, u32[]{:S(2)}, u32[]{:S(2)}) %collective-permute-start.3) | collective-permute-done | bytes 49184 | tf_op jit(solution)/shard_map/ppermute | solution.py:301
  43.1 10.5 %all_to_all.46.x_ref = bf16[8,48,512]{2,1,0:T(8,128)(2,1)S(1)} all-to-all(bf16[8,48,512]{2,1,0:T(8,128)(2,1)S(1)} %broadcast_in_dim.17), channel_id=1, replica_groups=mesh['line'=8,'place'=4,'core'=2,'tp'=8] {'tp'}, dimensions={0} | all-to-all | bytes 786432 | tf_op jit(solution)/shard_map/all_to_all | solution.py:305
  53.7 2.6 %shard_map.117 = (bf16[8,48,512]{2,1,0:T(8,128)(2,1)S(1)}, f32[48,128]{1,0:T(8,128)S(1)}) custom-call(s32[3]{0:T(128)S(1)} %pad_add_fusion.place_ref, s32[32,96]{1,0:T(8,128)S(1)} %get-tuple-element.28.lengths_ref, f32[1,2048]{1,0:T(1,128)S(1)} %get-tuple-element.32.g_own, f32[1,2048]{1,0:T(1,128)S(1)} %get-tuple-element.33.g_oth, ...), custom_call_target="tpu_custom_call" | custom-call | tf_op jit(solution)/shard_map/pallas_call | solution.py:276
  56.3 10.1 %all_to_all.47.got_ref = bf16[8,48,512]{2,1,0:T(8,128)(2,1)S(1)} all-to-all(bf16[8,48,512]{2,1,0:T(8,128)(2,1)S(1)} %get-tuple-element.36), channel_id=1, replica_groups=mesh['line'=8,'place'=4,'core'=2,'tp'=8] {'tp'}, dimensions={0} | all-to-all | bytes 786432 | tf_op jit(solution)/shard_map/all_to_all | solution.py:305
  66.4 0.6 shard_map.118.early_1
  67.0 0.7 collective-permute-start.4
  67.7 0.0 collective-permute-done.4.shard_ref
  67.7 9.2 %all_to_all.48.x_ref = bf16[8,48,512]{2,1,0:T(8,128)(2,1)S(1)} all-to-all(bf16[8,48,512]{2,1,0:T(8,128)(2,1)S(1)} %broadcast_in_dim.18), channel_id=1, replica_groups=mesh['line'=8,'place'=4,'core'=2,'tp'=8] {'tp'}, dimensions={0} | all-to-all | bytes 786432 | tf_op jit(solution)/shard_map/all_to_all | solution.py:305
  76.9 2.6 %shard_map.119 = (bf16[8,48,512]{2,1,0:T(8,128)(2,1)S(1)}, f32[48,128]{1,0:T(8,128)S(1)}) custom-call(s32[3]{0:T(128)S(1)} %pad_add_fusion.place_ref, s32[32,96]{1,0:T(8,128)S(1)} %get-tuple-element.28.lengths_ref, f32[1,2048]{1,0:T(1,128)S(1)} %get-tuple-element.32.g_own, f32[1,2048]{1,0:T(1,128)S(1)} %get-tuple-element.33.g_oth, ...), custom_call_target="tpu_custom_call" | custom-call | tf_op jit(solution)/shard_map/pallas_call | solution.py:276
  79.6 9.2 %all_to_all.49.got_ref = bf16[8,48,512]{2,1,0:T(8,128)(2,1)S(1)} all-to-all(bf16[8,48,512]{2,1,0:T(8,128)(2,1)S(1)} %get-tuple-element.38), channel_id=1, replica_groups=mesh['line'=8,'place'=4,'core'=2,'tp'=8] {'tp'}, dimensions={0} | all-to-all | bytes 786432 | tf_op jit(solution)/shard_map/all_to_all | solution.py:305
  88.8 0.6 shard_map.120.early_2
  89.4 0.7 collective-permute-start.5
  90.1 0.0 collective-permute-done.5.shard_ref
  90.2 9.2 %all_to_all.50.x_ref = bf16[8,48,512]{2,1,0:T(8,128)(2,1)S(1)} all-to-all(bf16[8,48,512]{2,1,0:T(8,128)(2,1)S(1)} %broadcast_in_dim.19), channel_id=1, replica_groups=mesh['line'=8,'place'=4,'core'=2,'tp'=8] {'tp'}, dimensions={0} | all-to-all | bytes 786432 | tf_op jit(solution)/shard_map/all_to_all | solution.py:305
  99.4 2.6 %shard_map.121 = (bf16[8,48,512]{2,1,0:T(8,128)(2,1)S(1)}, f32[48,128]{1,0:T(8,128)S(1)}) custom-call(s32[3]{0:T(128)S(1)} %pad_add_fusion.place_ref, s32[32,96]{1,0:T(8,128)S(1)} %get-tuple-element.28.lengths_ref, f32[1,2048]{1,0:T(1,128)S(1)} %get-tuple-element.32.g_own, f32[1,2048]{1,0:T(1,128)S(1)} %get-tuple-element.33.g_oth, ...), custom_call_target="tpu_custom_call" | custom-call | tf_op jit(solution)/shard_map/pallas_call | solution.py:276
  102.0 0.0 copy-start
  102.0 0.0 copy-start.1
  102.0 9.2 %all_to_all.51.got_ref = bf16[8,48,512]{2,1,0:T(8,128)(2,1)S(1)} all-to-all(bf16[8,48,512]{2,1,0:T(8,128)(2,1)S(1)} %get-tuple-element.40), channel_id=1, replica_groups=mesh['line'=8,'place'=4,'core'=2,'tp'=8] {'tp'}, dimensions={0} | all-to-all | bytes 786432 | tf_op jit(solution)/shard_map/all_to_all | solution.py:305
  111.3 0.6 shard_map.122
  111.9 14.1 %collective-permute-start.7 = (bf16[48,512]{1,0:T(8,128)(2,1)S(1)}, bf16[48,512]{1,0:T(8,128)(2,1)S(1)}, u32[]{:S(2)}, u32[]{:S(2)}) collective-permute-start(bf16[48,512]{1,0:T(8,128)(2,1)S(1)} %get-tuple-element.42), channel_id=1, source_target_pairs={{0,64},{8,72},{16,80},{24,88},{32,96},{40,104},{496,48},{504,56},{... | collective-permute-start | bytes 147464 | tf_op jit(solution)/shard_map/ppermute | solution.py:318
  126.0 3.4 %collective-permute-start.6 = (bf16[48,512]{1,0:T(8,128)(2,1)S(1)}, bf16[48,512]{1,0:T(8,128)(2,1)S(1)}, u32[]{:S(2)}, u32[]{:S(2)}) collective-permute-start(bf16[48,512]{1,0:T(8,128)(2,1)S(1)} %get-tuple-element.42), channel_id=1, source_target_pairs={{0,448},{8,456},{16,464},{24,472},{32,480},{40,488},{496,432},{504... | collective-permute-start | bytes 147464 | tf_op jit(solution)/shard_map/ppermute | solution.py:318
  129.4 0.0 collective-permute-done.7
  129.4 1.1 collective-permute-done.6
  130.6 3.5 %collective-permute-start.9 = (bf16[48,512]{1,0:T(8,128)(2,1)S(1)}, bf16[48,512]{1,0:T(8,128)(2,1)S(1)}, u32[]{:S(2)}, u32[]{:S(2)}) collective-permute-start(bf16[48,512]{1,0:T(8,128)(2,1)S(1)} %add_add_fusion.1), channel_id=1, source_target_pairs={{0,256},{8,264},{16,272},{24,280},{32,288},{40,296},{496,240},{504... | collective-permute-start | bytes 147464 | tf_op jit(solution)/shard_map/ppermute | solution.py:318
  134.1 0.7 collective-permute-start.8
  134.7 0.5 collective-permute-done.9
  135.2 0.0 collective-permute-done.8
  135.3 10.3 %all_to_all.52.rows_ref = bf16[4,48,512]{2,1,0:T(8,128)(2,1)S(1)} all-to-all(bf16[4,48,512]{2,1,0:T(8,128)(2,1)S(1)} %broadcast_in_dim.21), channel_id=1, replica_groups=mesh['line'=8,'place'=4,'core'=2,'tp'=8] {'place'}, dimensions={0} | all-to-all | bytes 393216 | tf_op jit(solution)/shard_map/all_to_all | solution.py:305
  145.6 0.0 copy-done
  145.6 0.0 copy-done.1
  145.6 1.7 shard_map.123
  147.2 0.1 broadcast_in_dim.22
  147.3 29.6 %all_to_all.53.got_ref = bf16[16,96,256]{2,1,0:T(8,128)(2,1)S(1)} all-to-all(bf16[16,96,256]{2,1,0:T(8,128)(2,1)S(1)} %bitcast.14), channel_id=1, replica_groups=mesh['line'=8,'place'=4,'core'=2,'tp'=8] {'core','tp'}, dimensions={0} | all-to-all | bytes 1572864 | tf_op jit(solution)/shard_map/all_to_all | solution.py:305
  177.0 1.0 shard_map.124
  (7 shorter events, 0.1 us)
Async XLA Ops:
  0.6 16.3 %collective-permute-start.1 = (bf16[2048,384]{1,0:T(8,128)(2,1)}, bf16[2048,384]{1,0:T(8,128)(2,1)S(1)}, u32[]{:S(2)}, u32[]{:S(2)}) collective-permute-start(bf16[2048,384]{1,0:T(8,128)(2,1)} %bitcast.15), channel_id=1, source_target_pairs={{0,8},{8,0},{1,9},{9,1},{2,10},{10,2},{3,11},{11,3},{4,12},{12,4},... | collective-permute-start | bytes 4718600 | tf_op jit(solution)/shard_map/ppermute | solution.py:295
  9.4 7.5 %collective-permute-start.2 = (bf16[256,2048]{1,0:T(8,128)(2,1)}, bf16[256,2048]{1,0:T(8,128)(2,1)S(1)}, u32[]{:S(2)}, u32[]{:S(2)}) collective-permute-start(bf16[256,2048]{1,0:T(8,128)(2,1)} %bitcast.17), channel_id=1, source_target_pairs={{0,8},{8,0},{1,9},{9,1},{2,10},{10,2},{3,11},{11,3},{4,12},{12,4},... | collective-permute-start | bytes 3145736 | tf_op jit(solution)/shard_map/ppermute | solution.py:295
  12.5 4.5 %collective-permute-start = (bf16[144,2048]{1,0:T(8,128)(2,1)S(1)}, bf16[144,2048]{1,0:T(8,128)(2,1)}, u32[]{:S(2)}, u32[]{:S(2)}) collective-permute-start(bf16[144,2048]{1,0:T(8,128)(2,1)S(1)} %shard_map.113.packed_own), channel_id=1, source_target_pairs={{0,8},{8,0},{1,9},{9,1},{2,10},{10,2},{3,11},{11,3},{4,12},{12,4},... | collective-permute-start | bytes 1769480 | tf_op jit(solution)/shard_map/ppermute | solution.py:295
  31.4 11.7 %collective-permute-start.3 = (bf16[48,512]{1,0:T(8,128)(2,1)S(1)}, bf16[48,512]{1,0:T(8,128)(2,1)S(1)}, u32[]{:S(2)}, u32[]{:S(2)}) collective-permute-start(bf16[48,512]{1,0:T(8,128)(2,1)S(1)} %shard_map.116.early_0), channel_id=1, source_target_pairs={{0,16},{8,24},{16,32},{24,40},{32,48},{40,56},{48,64},{56,72},{64,... | collective-permute-start | bytes 147464 | tf_op jit(solution)/shard_map/ppermute | solution.py:301
  67.0 0.7 collective-permute-start.4
  89.4 0.7 collective-permute-start.5
  102.0 43.5 %copy-start = (s32[4,96,4]{1,2,0:T(4,128)S(1)}, s32[4,96,4]{1,2,0:T(4,128)}, u32[]{:S(2)}) copy-start(s32[4,96,4]{1,2,0:T(4,128)} %param.19) | copy-start | bytes 18436
  102.0 43.5 %copy-start.1 = (bf16[2,256]{1,0:T(2,128)(2,1)S(1)}, bf16[2,256]{1,0:T(2,128)(2,1)}, u32[]{:S(2)}) copy-start(bf16[2,256]{1,0:T(2,128)(2,1)} %talk_gain.1) | copy-start | bytes 3076
  111.9 17.5 %collective-permute-start.7 = (bf16[48,512]{1,0:T(8,128)(2,1)S(1)}, bf16[48,512]{1,0:T(8,128)(2,1)S(1)}, u32[]{:S(2)}, u32[]{:S(2)}) collective-permute-start(bf16[48,512]{1,0:T(8,128)(2,1)S(1)} %get-tuple-element.42), channel_id=1, source_target_pairs={{0,64},{8,72},{16,80},{24,88},{32,96},{40,104},{496,48},{504,56},{... | collective-permute-start | bytes 147464 | tf_op jit(solution)/shard_map/ppermute | solution.py:318
  126.0 4.6 %collective-permute-start.6 = (bf16[48,512]{1,0:T(8,128)(2,1)S(1)}, bf16[48,512]{1,0:T(8,128)(2,1)S(1)}, u32[]{:S(2)}, u32[]{:S(2)}) collective-permute-start(bf16[48,512]{1,0:T(8,128)(2,1)S(1)} %get-tuple-element.42), channel_id=1, source_target_pairs={{0,448},{8,456},{16,464},{24,472},{32,480},{40,488},{496,432},{504... | collective-permute-start | bytes 147464 | tf_op jit(solution)/shard_map/ppermute | solution.py:318
  130.6 4.6 %collective-permute-start.9 = (bf16[48,512]{1,0:T(8,128)(2,1)S(1)}, bf16[48,512]{1,0:T(8,128)(2,1)S(1)}, u32[]{:S(2)}, u32[]{:S(2)}) collective-permute-start(bf16[48,512]{1,0:T(8,128)(2,1)S(1)} %add_add_fusion.1), channel_id=1, source_target_pairs={{0,256},{8,264},{16,272},{24,280},{32,288},{40,296},{496,240},{504... | collective-permute-start | bytes 147464 | tf_op jit(solution)/shard_map/ppermute | solution.py:318
  134.1 1.2 collective-permute-start.8

commit v5 on v4

--- a/solution.py
+++ b/solution.py
@@ -75,26 +75,24 @@
         out_ref[j, :, block:] = oth.astype(bf16)
 
 
-def pack_kernel(rows_src, gain_src, adapt_src, books_src, out_ref, gain_ref, semaphores):
+def pack_kernel(gain_ref, rows_src, adapt_src, books_src, out_ref, semaphores):
     columns, entries = adapt_src.shape[1:]
     tables = [adapt_src.at[i] for i in range(adapt_src.shape[0])]
     tables += [books_src.at[q] for q in range(NQ)]
     below = pl.ds(B, columns)
-    copies = [pltpu.make_async_copy(gain_src, gain_ref, semaphores.at[0])]
-    copies += [pltpu.make_async_copy(rows_src, out_ref.at[:B], semaphores.at[1])]
+    copies = [pltpu.make_async_copy(rows_src, out_ref.at[:B], semaphores.at[0])]
     for i, source in enumerate(tables):
         target = out_ref.at[below, pl.ds(i * entries, entries)]
-        copies += [pltpu.make_async_copy(source, target, semaphores.at[2 + i])]
+        copies += [pltpu.make_async_copy(source, target, semaphores.at[1 + i])]
     for copy in copies:
         copy.start()
     start = len(tables) * entries
     free = out_ref.shape[1] - start
-    copies[0].wait()
     gain = gain_ref[...].astype(f32)
     pieces = [gain[:, j : j + free] for j in range(0, gain.shape[1], free)]
     pieces += [jnp.zeros((columns - len(pieces), free), f32)]
     out_ref[B:, start:] = jnp.concatenate(pieces, axis=0).astype(bf16)
-    for copy in copies[1:]:
+    for copy in copies:
         copy.wait()
 
 
@@ -339,17 +337,15 @@
     o_oth = to_partner(o_own)
     there = pl.BlockSpec(memory_space=pltpu.HBM)
     here = pl.BlockSpec(memory_space=pltpu.VMEM)
-    sources = [arriving[0], norm_gain, w_adapt.transpose(0, 2, 1), codebooks.transpose(0, 2, 1)]
+    sources = [arriving[0], w_adapt.transpose(0, 2, 1), codebooks.transpose(0, 2, 1)]
     packed_own = pl.pallas_call(
         pack_kernel,
         out_shape=shaped(B + columns, width),
-        in_specs=[there] * len(sources),
+        in_specs=[here] + [there] * len(sources),
         out_specs=here,
-        scratch_shapes=[
-            pltpu.VMEM(norm_gain.shape, bf16), pltpu.SemaphoreType.DMA((4 + NQ,))
-        ],
+        scratch_shapes=[pltpu.SemaphoreType.DMA((3 + NQ,))],
         compiler_params=pltpu.CompilerParams(vmem_limit_bytes=8 * 2**20),
-    )(*(pltpu.with_memory_space_constraint(v, pltpu.HBM) for v in sources))
+    )(norm_gain, *(pltpu.with_memory_space_constraint(v, pltpu.HBM) for v in sources))
     packed_oth = to_partner(packed_own)
     cache_rows = cache[0].reshape(TICKS, HALF * CACHE, -1)
     blocks = shaped(shards, HALF, 2 * block)

time: 179 us -> 180 us (level)
  no operation moved by 1% of the time
where the time goes in v5:
time: 180 us; the launch traced here: 179 us
  blocking collectives  108 us (60%)
  starting transfers between devices  39.3 us (22%)
  Pallas kernels  19.3 us (11%)
  waiting for transfers between devices  10.1 us (6%)
    all_to_all x9, blocking collectives, exchange(): return lax.all_to_all(blocks, axis, 0, 0, tiled=True)  108 us
    ppermute x4, starting transfers between devices, sent(): return lax.ppermute(rows, SECTION, pairs)  21.6 us
    pallas_call x10, Pallas kernels, run(): pl.pallas_call(kernel, out_shape=outs, in_specs=specs, out_specs=out_spec...  16.2 us
    ppermute x3, starting transfers between devices, to_partner(): return lax.ppermute(value, 'core', [(0, 1), (1, 0)])  13.1 us
    ppermute x3, waiting for transfers between devices, to_next(): lax.ppermute(value, SECTION, pairs + [(count - 2 + c, kept + c) for c in...  8.42 us
    ppermute x3, starting transfers between devices, to_next(): lax.ppermute(value, SECTION, pairs + [(count - 2 + c, kept + c) for c in...  4.63 us
  transfers between devices with their start and end apart: 10, of which 3 were waited for; matrix products, arithmetic and copies ran while one was open for 0% of the time, Pallas kernels for 2%

profile of v5, /device:TPU:1, one launch (start us, length us, event | category | flops | bytes accessed | tf_op | source)
XLA Modules:
  0.0 178.6 jit_solution(14891501275825085043)
XLA Ops:
  0.6 8.8 %collective-permute-start.1 = (bf16[2048,384]{1,0:T(8,128)(2,1)}, bf16[2048,384]{1,0:T(8,128)(2,1)S(1)}, u32[]{:S(2)}, u32[]{:S(2)}) collective-permute-start(bf16[2048,384]{1,0:T(8,128)(2,1)} %bitcast.15), channel_id=1, source_target_pairs={{0,8},{8,0},{1,9},{9,1},{2,10},{10,2},{3,11},{11,3},{4,12},{12,4},... | collective-permute-start | bytes 4718600 | tf_op jit(solution)/shard_map/ppermute | solution.py:293
  9.4 1.9 %collective-permute-start.2 = (bf16[256,2048]{1,0:T(8,128)(2,1)}, bf16[256,2048]{1,0:T(8,128)(2,1)S(1)}, u32[]{:S(2)}, u32[]{:S(2)}) collective-permute-start(bf16[256,2048]{1,0:T(8,128)(2,1)} %bitcast.17), channel_id=1, source_target_pairs={{0,8},{8,0},{1,9},{9,1},{2,10},{10,2},{3,11},{11,3},{4,12},{12,4},... | collective-permute-start | bytes 3145736 | tf_op jit(solution)/shard_map/ppermute | solution.py:293
  11.4 0.0 copy-start
  11.4 0.7 copy-done
  12.1 1.1 shard_map.113.packed_own
  13.1 2.4 %collective-permute-start = (bf16[144,2048]{1,0:T(8,128)(2,1)S(1)}, bf16[144,2048]{1,0:T(8,128)(2,1)}, u32[]{:S(2)}, u32[]{:S(2)}) collective-permute-start(bf16[144,2048]{1,0:T(8,128)(2,1)S(1)} %shard_map.113.packed_own), channel_id=1, source_target_pairs={{0,8},{8,0},{1,9},{9,1},{2,10},{10,2},{3,11},{11,3},{4,12},{12,4},... | collective-permute-start | bytes 1769480 | tf_op jit(solution)/shard_map/ppermute | solution.py:293
  15.6 2.0 %shard_map.114 = (s32[32,96]{1,0:T(8,128)S(1)}, bf16[2048,384]{1,0:T(8,128)(2,1)S(1)}, bf16[256,2048]{1,0:T(8,128)(2,1)S(1)}, bf16[4,768,128]{2,1,0:T(8,128)(2,1)S(1)}) custom-call(s32[32,96]{1,0:T(8,128)} %refs_0_, bf16[2048,384]{1,0:T(8,128)(2,1)} %bitcast.16, bf16[256,2048]{1,0:T(8,128)(2,1)} %bitcast.18, bf16[4,768,128]{2,1,0:T(8,128)(2,1)} %bitcast.19), custom_call_target="tpu_custom_call" | custom-call | bytes 7340032 | tf_op jit(solution)/shard_map/pallas_call | solution.py:355
  17.6 0.1 pad_add_fusion.place_ref
  17.6 0.0 collective-permute-done.packed_oth
  17.6 0.0 collective-permute-done.2.o_oth
  17.6 0.0 collective-permute-done.1.w_oth
  17.6 3.1 %shard_map.115 = (bf16[8,48,512]{2,1,0:T(8,128)(2,1)S(1)}, bf16[48,512]{1,0:T(8,128)(2,1)S(1)}, f32[1,2048]{1,0:T(1,128)S(1)}, f32[1,2048]{1,0:T(1,128)S(1)}) custom-call(s32[3]{0:T(128)S(1)} %pad_add_fusion.place_ref, s32[32,96]{1,0:T(8,128)S(1)} %get-tuple-element.28.lengths_ref, bf16[144,2048]{1,0:T(8,128)(2,1)S(1)} %shard_map.113.packed_own, ...), custom_call_target="tpu_custom_call" | custom-call | tf_op jit(solution)/shard_map/pallas_call | solution.py:274
  20.8 10.6 %all_to_all.45.got_ref = bf16[8,48,512]{2,1,0:T(8,128)(2,1)S(1)} all-to-all(bf16[8,48,512]{2,1,0:T(8,128)(2,1)S(1)} %get-tuple-element.34), channel_id=1, replica_groups=mesh['line'=8,'place'=4,'core'=2,'tp'=8] {'tp'}, dimensions={0} | all-to-all | bytes 786432 | tf_op jit(solution)/shard_map/all_to_all | solution.py:303
  31.4 0.6 shard_map.116.early_0
  32.0 3.3 %collective-permute-start.3 = (bf16[48,512]{1,0:T(8,128)(2,1)S(1)}, bf16[48,512]{1,0:T(8,128)(2,1)S(1)}, u32[]{:S(2)}, u32[]{:S(2)}) collective-permute-start(bf16[48,512]{1,0:T(8,128)(2,1)S(1)} %shard_map.116.early_0), channel_id=1, source_target_pairs={{0,16},{8,24},{16,32},{24,40},{32,48},{40,56},{48,64},{56,72},{64,... | collective-permute-start | bytes 147464 | tf_op jit(solution)/shard_map/ppermute | solution.py:299
  35.4 8.4 %collective-permute-done.3.shard_ref = bf16[48,512]{1,0:T(8,128)(2,1)S(1)} collective-permute-done((bf16[48,512]{1,0:T(8,128)(2,1)S(1)}, bf16[48,512]{1,0:T(8,128)(2,1)S(1)}, u32[]{:S(2)}, u32[]{:S(2)}) %collective-permute-start.3) | collective-permute-done | bytes 49184 | tf_op jit(solution)/shard_map/ppermute | solution.py:299
  43.8 10.5 %all_to_all.46.x_ref = bf16[8,48,512]{2,1,0:T(8,128)(2,1)S(1)} all-to-all(bf16[8,48,512]{2,1,0:T(8,128)(2,1)S(1)} %broadcast_in_dim.17), channel_id=1, replica_groups=mesh['line'=8,'place'=4,'core'=2,'tp'=8] {'tp'}, dimensions={0} | all-to-all | bytes 786432 | tf_op jit(solution)/shard_map/all_to_all | solution.py:303
  54.4 2.6 %shard_map.117 = (bf16[8,48,512]{2,1,0:T(8,128)(2,1)S(1)}, f32[48,128]{1,0:T(8,128)S(1)}) custom-call(s32[3]{0:T(128)S(1)} %pad_add_fusion.place_ref, s32[32,96]{1,0:T(8,128)S(1)} %get-tuple-element.28.lengths_ref, f32[1,2048]{1,0:T(1,128)S(1)} %get-tuple-element.32.g_own, f32[1,2048]{1,0:T(1,128)S(1)} %get-tuple-element.33.g_oth, ...), custom_call_target="tpu_custom_call" | custom-call | tf_op jit(solution)/shard_map/pallas_call | solution.py:274
  57.0 10.1 %all_to_all.47.got_ref = bf16[8,48,512]{2,1,0:T(8,128)(2,1)S(1)} all-to-all(bf16[8,48,512]{2,1,0:T(8,128)(2,1)S(1)} %get-tuple-element.36), channel_id=1, replica_groups=mesh['line'=8,'place'=4,'core'=2,'tp'=8] {'tp'}, dimensions={0} | all-to-all | bytes 786432 | tf_op jit(solution)/shard_map/all_to_all | solution.py:303
  67.0 0.6 shard_map.118.early_1
  67.7 0.7 collective-permute-start.4
  68.3 0.0 collective-permute-done.4.shard_ref
  68.4 9.2 %all_to_all.48.x_ref = bf16[8,48,512]{2,1,0:T(8,128)(2,1)S(1)} all-to-all(bf16[8,48,512]{2,1,0:T(8,128)(2,1)S(1)} %broadcast_in_dim.18), channel_id=1, replica_groups=mesh['line'=8,'place'=4,'core'=2,'tp'=8] {'tp'}, dimensions={0} | all-to-all | bytes 786432 | tf_op jit(solution)/shard_map/all_to_all | solution.py:303
  77.6 2.6 %shard_map.119 = (bf16[8,48,512]{2,1,0:T(8,128)(2,1)S(1)}, f32[48,128]{1,0:T(8,128)S(1)}) custom-call(s32[3]{0:T(128)S(1)} %pad_add_fusion.place_ref, s32[32,96]{1,0:T(8,128)S(1)} %get-tuple-element.28.lengths_ref, f32[1,2048]{1,0:T(1,128)S(1)} %get-tuple-element.32.g_own, f32[1,2048]{1,0:T(1,128)S(1)} %get-tuple-element.33.g_oth, ...), custom_call_target="tpu_custom_call" | custom-call | tf_op jit(solution)/shard_map/pallas_call | solution.py:274
  80.3 9.2 %all_to_all.49.got_ref = bf16[8,48,512]{2,1,0:T(8,128)(2,1)S(1)} all-to-all(bf16[8,48,512]{2,1,0:T(8,128)(2,1)S(1)} %get-tuple-element.38), channel_id=1, replica_groups=mesh['line'=8,'place'=4,'core'=2,'tp'=8] {'tp'}, dimensions={0} | all-to-all | bytes 786432 | tf_op jit(solution)/shard_map/all_to_all | solution.py:303
  89.5 0.6 shard_map.120.early_2
  90.1 0.7 collective-permute-start.5
  90.8 0.0 collective-permute-done.5.shard_ref
  90.8 9.2 %all_to_all.50.x_ref = bf16[8,48,512]{2,1,0:T(8,128)(2,1)S(1)} all-to-all(bf16[8,48,512]{2,1,0:T(8,128)(2,1)S(1)} %broadcast_in_dim.19), channel_id=1, replica_groups=mesh['line'=8,'place'=4,'core'=2,'tp'=8] {'tp'}, dimensions={0} | all-to-all | bytes 786432 | tf_op jit(solution)/shard_map/all_to_all | solution.py:303
  100.1 2.6 %shard_map.121 = (bf16[8,48,512]{2,1,0:T(8,128)(2,1)S(1)}, f32[48,128]{1,0:T(8,128)S(1)}) custom-call(s32[3]{0:T(128)S(1)} %pad_add_fusion.place_ref, s32[32,96]{1,0:T(8,128)S(1)} %get-tuple-element.28.lengths_ref, f32[1,2048]{1,0:T(1,128)S(1)} %get-tuple-element.32.g_own, f32[1,2048]{1,0:T(1,128)S(1)} %get-tuple-element.33.g_oth, ...), custom_call_target="tpu_custom_call" | custom-call | tf_op jit(solution)/shard_map/pallas_call | solution.py:274
  102.7 0.0 copy-start.1
  102.7 0.0 copy-start.2
  102.7 9.2 %all_to_all.51.got_ref = bf16[8,48,512]{2,1,0:T(8,128)(2,1)S(1)} all-to-all(bf16[8,48,512]{2,1,0:T(8,128)(2,1)S(1)} %get-tuple-element.40), channel_id=1, replica_groups=mesh['line'=8,'place'=4,'core'=2,'tp'=8] {'tp'}, dimensions={0} | all-to-all | bytes 786432 | tf_op jit(solution)/shard_map/all_to_all | solution.py:303
  112.0 0.6 shard_map.122
  112.6 14.1 %collective-permute-start.7 = (bf16[48,512]{1,0:T(8,128)(2,1)S(1)}, bf16[48,512]{1,0:T(8,128)(2,1)S(1)}, u32[]{:S(2)}, u32[]{:S(2)}) collective-permute-start(bf16[48,512]{1,0:T(8,128)(2,1)S(1)} %get-tuple-element.42), channel_id=1, source_target_pairs={{0,64},{8,72},{16,80},{24,88},{32,96},{40,104},{496,48},{504,56},{... | collective-permute-start | bytes 147464 | tf_op jit(solution)/shard_map/ppermute | solution.py:316
  126.7 3.4 %collective-permute-start.6 = (bf16[48,512]{1,0:T(8,128)(2,1)S(1)}, bf16[48,512]{1,0:T(8,128)(2,1)S(1)}, u32[]{:S(2)}, u32[]{:S(2)}) collective-permute-start(bf16[48,512]{1,0:T(8,128)(2,1)S(1)} %get-tuple-element.42), channel_id=1, source_target_pairs={{0,448},{8,456},{16,464},{24,472},{32,480},{40,488},{496,432},{504... | collective-permute-start | bytes 147464 | tf_op jit(solution)/shard_map/ppermute | solution.py:316
  130.1 0.0 collective-permute-done.7
  130.1 1.1 collective-permute-done.6
  131.2 3.5 %collective-permute-start.9 = (bf16[48,512]{1,0:T(8,128)(2,1)S(1)}, bf16[48,512]{1,0:T(8,128)(2,1)S(1)}, u32[]{:S(2)}, u32[]{:S(2)}) collective-permute-start(bf16[48,512]{1,0:T(8,128)(2,1)S(1)} %add_add_fusion.1), channel_id=1, source_target_pairs={{0,256},{8,264},{16,272},{24,280},{32,288},{40,296},{496,240},{504... | collective-permute-start | bytes 147464 | tf_op jit(solution)/shard_map/ppermute | solution.py:316
  134.7 0.7 collective-permute-start.8
  135.4 0.5 collective-permute-done.9
  135.9 0.0 collective-permute-done.8
  135.9 10.3 %all_to_all.52.rows_ref = bf16[4,48,512]{2,1,0:T(8,128)(2,1)S(1)} all-to-all(bf16[4,48,512]{2,1,0:T(8,128)(2,1)S(1)} %broadcast_in_dim.21), channel_id=1, replica_groups=mesh['line'=8,'place'=4,'core'=2,'tp'=8] {'place'}, dimensions={0} | all-to-all | bytes 393216 | tf_op jit(solution)/shard_map/all_to_all | solution.py:303
  146.2 0.0 copy-done.1
  146.2 0.0 copy-done.2
  146.2 1.7 shard_map.123
  147.9 0.1 broadcast_in_dim.22
  148.0 29.6 %all_to_all.53.got_ref = bf16[16,96,256]{2,1,0:T(8,128)(2,1)S(1)} all-to-all(bf16[16,96,256]{2,1,0:T(8,128)(2,1)S(1)} %bitcast.14), channel_id=1, replica_groups=mesh['line'=8,'place'=4,'core'=2,'tp'=8] {'core','tp'}, dimensions={0} | all-to-all | bytes 1572864 | tf_op jit(solution)/shard_map/all_to_all | solution.py:303
  177.6 1.0 shard_map.124
  (7 shorter events, 0.1 us)
Async XLA Ops:
  0.6 17.0 %collective-permute-start.1 = (bf16[2048,384]{1,0:T(8,128)(2,1)}, bf16[2048,384]{1,0:T(8,128)(2,1)S(1)}, u32[]{:S(2)}, u32[]{:S(2)}) collective-permute-start(bf16[2048,384]{1,0:T(8,128)(2,1)} %bitcast.15), channel_id=1, source_target_pairs={{0,8},{8,0},{1,9},{9,1},{2,10},{10,2},{3,11},{11,3},{4,12},{12,4},... | collective-permute-start | bytes 4718600 | tf_op jit(solution)/shard_map/ppermute | solution.py:293
  9.4 8.2 %collective-permute-start.2 = (bf16[256,2048]{1,0:T(8,128)(2,1)}, bf16[256,2048]{1,0:T(8,128)(2,1)S(1)}, u32[]{:S(2)}, u32[]{:S(2)}) collective-permute-start(bf16[256,2048]{1,0:T(8,128)(2,1)} %bitcast.17), channel_id=1, source_target_pairs={{0,8},{8,0},{1,9},{9,1},{2,10},{10,2},{3,11},{11,3},{4,12},{12,4},... | collective-permute-start | bytes 3145736 | tf_op jit(solution)/shard_map/ppermute | solution.py:293
  11.4 0.7 copy-start
  13.1 4.5 %collective-permute-start = (bf16[144,2048]{1,0:T(8,128)(2,1)S(1)}, bf16[144,2048]{1,0:T(8,128)(2,1)}, u32[]{:S(2)}, u32[]{:S(2)}) collective-permute-start(bf16[144,2048]{1,0:T(8,128)(2,1)S(1)} %shard_map.113.packed_own), channel_id=1, source_target_pairs={{0,8},{8,0},{1,9},{9,1},{2,10},{10,2},{3,11},{11,3},{4,12},{12,4},... | collective-permute-start | bytes 1769480 | tf_op jit(solution)/shard_map/ppermute | solution.py:293
  32.0 11.7 %collective-permute-start.3 = (bf16[48,512]{1,0:T(8,128)(2,1)S(1)}, bf16[48,512]{1,0:T(8,128)(2,1)S(1)}, u32[]{:S(2)}, u32[]{:S(2)}) collective-permute-start(bf16[48,512]{1,0:T(8,128)(2,1)S(1)} %shard_map.116.early_0), channel_id=1, source_target_pairs={{0,16},{8,24},{16,32},{24,40},{32,48},{40,56},{48,64},{56,72},{64,... | collective-permute-start | bytes 147464 | tf_op jit(solution)/shard_map/ppermute | solution.py:299
  67.7 0.7 collective-permute-start.4
  90.1 0.7 collective-permute-start.5
  102.7 43.5 %copy-start.1 = (s32[4,96,4]{1,2,0:T(4,128)S(1)}, s32[4,96,4]{1,2,0:T(4,128)}, u32[]{:S(2)}) copy-start(s32[4,96,4]{1,2,0:T(4,128)} %param.19) | copy-start | bytes 18436
  102.7 43.5 %copy-start.2 = (bf16[2,256]{1,0:T(2,128)(2,1)S(1)}, bf16[2,256]{1,0:T(2,128)(2,1)}, u32[]{:S(2)}) copy-start(bf16[2,256]{1,0:T(2,128)(2,1)} %talk_gain.1) | copy-start | bytes 3076
  112.6 17.5 %collective-permute-start.7 = (bf16[48,512]{1,0:T(8,128)(2,1)S(1)}, bf16[48,512]{1,0:T(8,128)(2,1)S(1)}, u32[]{:S(2)}, u32[]{:S(2)}) collective-permute-start(bf16[48,512]{1,0:T(8,128)(2,1)S(1)} %get-tuple-element.42), channel_id=1, source_target_pairs={{0,64},{8,72},{16,80},{24,88},{32,96},{40,104},{496,48},{504,56},{... | collective-permute-start | bytes 147464 | tf_op jit(solution)/shard_map/ppermute | solution.py:316
  126.7 4.6 %collective-permute-start.6 = (bf16[48,512]{1,0:T(8,128)(2,1)S(1)}, bf16[48,512]{1,0:T(8,128)(2,1)S(1)}, u32[]{:S(2)}, u32[]{:S(2)}) collective-permute-start(bf16[48,512]{1,0:T(8,128)(2,1)S(1)} %get-tuple-element.42), channel_id=1, source_target_pairs={{0,448},{8,456},{16,464},{24,472},{32,480},{40,488},{496,432},{504... | collective-permute-start | bytes 147464 | tf_op jit(solution)/shard_map/ppermute | solution.py:316
  131.2 4.6 %collective-permute-start.9 = (bf16[48,512]{1,0:T(8,128)(2,1)S(1)}, bf16[48,512]{1,0:T(8,128)(2,1)S(1)}, u32[]{:S(2)}, u32[]{:S(2)}) collective-permute-start(bf16[48,512]{1,0:T(8,128)(2,1)S(1)} %add_add_fusion.1), channel_id=1, source_target_pairs={{0,256},{8,264},{16,272},{24,280},{32,288},{40,296},{496,240},{504... | collective-permute-start | bytes 147464 | tf_op jit(solution)/shard_map/ppermute | solution.py:316
  134.7 1.2 collective-permute-start.8

commit v6 on v5

--- a/solution.py
+++ b/solution.py
@@ -46,25 +46,20 @@
     pair_new = proj[:, RATIO * HD :].astype(bf16)
     pairs = pairs_ref[...]
     scores = lax.dot_general(queries, pairs, CONTRACT_LAST, preferred_element_type=f32)
-    own_scores = lax.dot_general(queries, pair_new, CONTRACT_LAST, preferred_element_type=f32)
+    beside_new = jnp.concatenate([pair_new.astype(f32)] * RATIO, axis=0)
+    own_scores = jnp.sum(queries.astype(f32) * beside_new, axis=-1, keepdims=True)
     rows = RATIO * HALF
     stream = lax.rem(lax.broadcasted_iota(i32, (rows, 1), 0), HALF)
     place = lax.broadcasted_iota(i32, (rows, HALF * CACHE), 1)
     visible = jnp.logical_and(place >= stream * CACHE, place < ends)
     scores = jnp.where(visible, scores, -jnp.inf)
-    own_place = lax.broadcasted_iota(i32, (rows, HALF), 1)
-    own_scores = jnp.where(own_place == stream, own_scores, -jnp.inf)
-    row_max = jnp.maximum(
-        jnp.max(scores, axis=-1, keepdims=True), jnp.max(own_scores, axis=-1, keepdims=True)
-    )
+    row_max = jnp.maximum(jnp.max(scores, axis=-1, keepdims=True), own_scores)
     weights = jnp.exp(scores - row_max)
     own_weights = jnp.exp(own_scores - row_max)
-    total = jnp.sum(weights, axis=-1, keepdims=True) + jnp.sum(own_weights, axis=-1, keepdims=True)
+    total = jnp.sum(weights, axis=-1, keepdims=True) + own_weights
     share = 1.0 / total
     mixed = jnp.dot((weights * share).astype(bf16), pairs, preferred_element_type=f32)
-    mixed = mixed + jnp.dot(
-        (own_weights * share).astype(bf16), pair_new, preferred_element_type=f32
-    )
+    mixed = mixed + (own_weights * share).astype(bf16).astype(f32) * beside_new
     mixed = mixed[:, HD:].astype(bf16)
     heads = jnp.concatenate([mixed[r * HALF : (r + 1) * HALF] for r in range(RATIO)], axis=1)
     for j in range(shards):
@@ -184,45 +179,55 @@
     latest_ref[...] = latest.astype(bf16)
 
 
+def pair_table(i, first, packed_own, packed_oth):
+    entries = packed_own.shape[1] // 8
+    span = slice(i * entries, (i + 1) * entries)
+    own, oth = packed_own[B:, span].astype(f32), packed_oth[B:, span].astype(f32)
+    both = [jnp.where(first, own, oth), jnp.where(first, oth, own)]
+    return jnp.concatenate(both, axis=0).astype(bf16)
+
+
+def embed_kernel(place_ref, packed_own, packed_oth, codes_ref, out_ref):
+    column, first = place_ref[2], place_ref[0] == 0
+    entries = packed_own.shape[1] // 8
+    embedded = jnp.zeros(out_ref.shape, f32)
+    for q in range(NQ):
+        ids = [codes_ref[tick, q : q + 1, :] for tick in range(TICKS)]
+        ids = [jnp.where(first, row[:, :HALF], row[:, HALF:]) for row in ids]
+        ids = jnp.concatenate(ids, axis=1) - column * entries
+        hot = lax.broadcasted_iota(i32, (entries, TICKS * HALF), 0) == ids
+        hot = jnp.where(hot, 1.0, 0.0).astype(bf16)
+        table = pair_table(2 + q, first, packed_own, packed_oth)
+        embedded = embedded + jnp.dot(table, hot, preferred_element_type=f32)
+    out_ref[...] = embedded
+
+
 def talk_kernel(
-    place_ref, rows_ref, latest_ref, talk_gain, packed_own, packed_oth, codes_ref, out_ref
+    place_ref, rows_ref, latest_ref, talk_gain, packed_own, packed_oth, embedded_ref, out_ref
 ):
-    side, column = place_ref[0], place_ref[2]
+    first = place_ref[0] == 0
     block = rows_ref.shape[2] // 2
-    columns, entries = packed_own.shape[0] - B, packed_own.shape[1] // 8
-    first = side == 0
+    columns = packed_own.shape[0] - B
     gains = talk_gain[...].astype(f32)
 
     def halves(rows):
         own, oth = rows[:, :block].astype(f32), rows[:, block:].astype(f32)
         return jnp.where(first, own, oth), jnp.where(first, oth, own)
 
-    def table(i):
-        span = slice(i * entries, (i + 1) * entries)
-        own, oth = packed_own[B:, span].astype(f32), packed_oth[B:, span].astype(f32)
-        both = [jnp.where(first, own, oth), jnp.where(first, oth, own)]
-        return jnp.concatenate(both, axis=0).astype(bf16)
-
     def beside(terms, tick):
         terms = terms[:, tick * HALF : (tick + 1) * HALF]
         return jnp.concatenate([terms[:columns], terms[columns:]], axis=1)
 
-    def my_ids(tick, q):
-        ids = codes_ref[tick, q : q + 1, :]
-        return jnp.where(first, ids[:, :HALF], ids[:, HALF:]) - column * entries
-
-    embedded = jnp.zeros((2 * columns, TICKS * HALF), f32)
-    for q in range(NQ):
-        ids = jnp.concatenate([my_ids(tick, q) for tick in range(TICKS)], axis=1)
-        hot = lax.broadcasted_iota(i32, (entries, TICKS * HALF), 0) == ids
-        hot = jnp.where(hot, 1.0, 0.0).astype(bf16)
-        embedded = embedded + jnp.dot(table(2 + q), hot, preferred_element_type=f32)
+    embedded = embedded_ref[...]
     adapted = jnp.zeros((2 * columns, TICKS * HALF), f32)
     low, high = halves(rows_ref[...].reshape(TICKS * HALF, 2 * block))
     for i, part in enumerate((low, high)):
         scaled = (part * gains[i : i + 1]).astype(bf16)
         adapted = adapted + lax.dot_general(
-            table(i), scaled, CONTRACT_LAST, preferred_element_type=f32
+            pair_table(i, first, packed_own, packed_oth),
+            scaled,
+            CONTRACT_LAST,
+            preferred_element_type=f32,
         )
     low, high = low[EARLY * HALF :], high[EARLY * HALF :]
     both = adapted + embedded
@@ -318,8 +323,9 @@
     place = lax.axis_index("place")
     offset = lax.rem(line - jnp.where(place == EARLY, LINES - 1, 0) + LINES, LINES)
     some = jnp.where(offset == 0, value, jnp.zeros_like(value))
+    far = sent(value, (0, 4))
     some = some + sent(value, (0, 7)) + sent(value, (0, 1))
-    return some + sent(some, (1, 2), (7, 6)) + sent(some, (0, 4), (1, 3), (7, 5))
+    return some + sent(some, (1, 2), (7, 6)) + sent(some, (1, 3), (7, 5)) + far
 
 
 def body(arriving, norm_gain, w_qkv, w_out, cache, lengths, talk_gain, w_adapt, codebooks, codes):
@@ -373,6 +379,13 @@
         got = exchange(terms)
         finals.append(run(functools.partial(sum_kernel, tick), piece, place, got, shard, inverse))
         shard = to_next(finals[-1], tick)
+        if tick == 0:
+            tokens, _ = lax.optimization_barrier((codes.transpose(0, 2, 1), finals[0]))
+            embedded = run(
+                embed_kernel, shaped(2 * columns, TICKS * HALF, dtype=f32),
+                place, packed_own, packed_oth, tokens,
+            )
+            shard, embedded = lax.optimization_barrier((shard, embedded))
         rows = exchange(replicate(shard, shards))
         terms, inverse = run(
             functools.partial(later_kernel, tick + 1),
@@ -389,7 +402,7 @@
     payload = run(
         talk_kernel,
         shaped(2, B, block),
-        place, talk_rows, latest, talk_gain, packed_own, packed_oth, codes.transpose(0, 2, 1),
+        place, talk_rows, latest, talk_gain, packed_own, packed_oth, embedded,
     )
     payload = jnp.broadcast_to(payload[:, None], (2, shards, B, block))
     sums = exchange(payload.reshape(2 * shards, B, block), ("core", "tp"))

time: 180 us -> 179 us (level)
  waiting for transfers between devices: 10.1 us -> 6.93 us
  starting transfers between devices: 39.3 us -> 41.1 us
    ppermute x4 -> x5, starting transfers between devices: 21.6 us -> 23.4 us  [sent(): return lax.ppermute(rows, SECTION, pairs)]
    pallas_call x10 -> x11, Pallas kernels: 16.2 us -> 17.2 us  [run(): pl.pallas_call(kernel, out_shape=outs, in_specs=specs, out_specs=out_spec...]
  transfers between devices with their start and end apart: 10 -> 11, of which waited for: 3 -> 1; matrix products, arithmetic and copies ran while one was open for 0% -> 0% of each run, Pallas kernels for 2% -> 3%
where the time goes in v6:
time: 179 us; the launch traced here: 178 us
  blocking collectives  108 us (60%)
  starting transfers between devices  41.1 us (23%)
  Pallas kernels  20.3 us (11%)
  waiting for transfers between devices  6.93 us (4%)
    all_to_all x9, blocking collectives, exchange(): return lax.all_to_all(blocks, axis, 0, 0, tiled=True)  108 us
    ppermute x5, starting transfers between devices, sent(): return lax.ppermute(rows, SECTION, pairs)  23.4 us
    pallas_call x11, Pallas kernels, run(): pl.pallas_call(kernel, out_shape=outs, in_specs=specs, out_specs=out_spec...  17.2 us
    ppermute x3, starting transfers between devices, to_partner(): return lax.ppermute(value, 'core', [(0, 1), (1, 0)])  13.1 us
    ppermute x3, waiting for transfers between devices, to_next(): lax.ppermute(value, SECTION, pairs + [(count - 2 + c, kept + c) for c in...  6.91 us
    ppermute x3, starting transfers between devices, to_next(): lax.ppermute(value, SECTION, pairs + [(count - 2 + c, kept + c) for c in...  4.63 us
  transfers between devices with their start and end apart: 11, of which 1 were waited for; matrix products, arithmetic and copies ran while one was open for 0% of the time, Pallas kernels for 3%

profile of v6, /device:TPU:1, one launch (start us, length us, event | category | flops | bytes accessed | tf_op | source)
XLA Modules:
  0.0 178.1 jit_solution(13881422376360170128)
XLA Ops:
  0.6 8.8 %collective-permute-start.1 = (bf16[2048,384]{1,0:T(8,128)(2,1)}, bf16[2048,384]{1,0:T(8,128)(2,1)S(1)}, u32[]{:S(2)}, u32[]{:S(2)}) collective-permute-start(bf16[2048,384]{1,0:T(8,128)(2,1)} %bitcast.15), channel_id=1, source_target_pairs={{0,8},{8,0},{1,9},{9,1},{2,10},{10,2},{3,11},{11,3},{4,12},{12,4},... | collective-permute-start | bytes 4718600 | tf_op jit(solution)/shard_map/ppermute | solution.py:298
  9.4 1.9 %collective-permute-start.2 = (bf16[256,2048]{1,0:T(8,128)(2,1)}, bf16[256,2048]{1,0:T(8,128)(2,1)S(1)}, u32[]{:S(2)}, u32[]{:S(2)}) collective-permute-start(bf16[256,2048]{1,0:T(8,128)(2,1)} %bitcast.17), channel_id=1, source_target_pairs={{0,8},{8,0},{1,9},{9,1},{2,10},{10,2},{3,11},{11,3},{4,12},{12,4},... | collective-permute-start | bytes 3145736 | tf_op jit(solution)/shard_map/ppermute | solution.py:298
  11.4 0.0 copy-start
  11.4 0.7 copy-done
  12.1 1.1 shard_map.113.packed_own
  13.1 2.4 %collective-permute-start = (bf16[144,2048]{1,0:T(8,128)(2,1)S(1)}, bf16[144,2048]{1,0:T(8,128)(2,1)}, u32[]{:S(2)}, u32[]{:S(2)}) collective-permute-start(bf16[144,2048]{1,0:T(8,128)(2,1)S(1)} %shard_map.113.packed_own), channel_id=1, source_target_pairs={{0,8},{8,0},{1,9},{9,1},{2,10},{10,2},{3,11},{11,3},{4,12},{12,4},... | collective-permute-start | bytes 1769480 | tf_op jit(solution)/shard_map/ppermute | solution.py:298
  15.6 2.0 %shard_map.114 = (s32[32,96]{1,0:T(8,128)S(1)}, bf16[2048,384]{1,0:T(8,128)(2,1)S(1)}, bf16[256,2048]{1,0:T(8,128)(2,1)S(1)}, bf16[4,768,128]{2,1,0:T(8,128)(2,1)S(1)}) custom-call(s32[32,96]{1,0:T(8,128)} %refs_0_, bf16[2048,384]{1,0:T(8,128)(2,1)} %bitcast.16, bf16[256,2048]{1,0:T(8,128)(2,1)} %bitcast.18, bf16[4,768,128]{2,1,0:T(8,128)(2,1)} %bitcast.19), custom_call_target="tpu_custom_call" | custom-call | bytes 7340032 | tf_op jit(solution)/shard_map/pallas_call | solution.py:361
  17.6 0.1 pad_add_fusion.place_ref
  17.6 0.0 collective-permute-done.packed_oth
  17.6 0.0 collective-permute-done.2.o_oth
  17.6 0.0 collective-permute-done.1.w_oth
  17.6 0.0 copy-start.1
  17.7 3.1 %shard_map.115 = (bf16[8,48,512]{2,1,0:T(8,128)(2,1)S(1)}, bf16[48,512]{1,0:T(8,128)(2,1)S(1)}, f32[1,2048]{1,0:T(1,128)S(1)}, f32[1,2048]{1,0:T(1,128)S(1)}) custom-call(s32[3]{0:T(128)S(1)} %pad_add_fusion.place_ref, s32[32,96]{1,0:T(8,128)S(1)} %get-tuple-element.31.lengths_ref, bf16[144,2048]{1,0:T(8,128)(2,1)S(1)} %shard_map.113.packed_own, ...), custom_call_target="tpu_custom_call" | custom-call | tf_op jit(solution)/shard_map/pallas_call | solution.py:279
  20.7 10.6 %all_to_all.45.got_ref = bf16[8,48,512]{2,1,0:T(8,128)(2,1)S(1)} all-to-all(bf16[8,48,512]{2,1,0:T(8,128)(2,1)S(1)} %get-tuple-element.37), channel_id=1, replica_groups=mesh['line'=8,'place'=4,'core'=2,'tp'=8] {'tp'}, dimensions={0} | all-to-all | bytes 786432 | tf_op jit(solution)/shard_map/all_to_all | solution.py:308
  31.4 0.6 shard_map.116.early_0
  32.0 3.3 %collective-permute-start.3 = (bf16[48,512]{1,0:T(8,128)(2,1)S(1)}, bf16[48,512]{1,0:T(8,128)(2,1)S(1)}, u32[]{:S(2)}, u32[]{:S(2)}) collective-permute-start(bf16[48,512]{1,0:T(8,128)(2,1)S(1)} %shard_map.116.early_0), channel_id=1, source_target_pairs={{0,16},{8,24},{16,32},{24,40},{32,48},{40,56},{48,64},{56,72},{64,... | collective-permute-start | bytes 147464 | tf_op jit(solution)/shard_map/ppermute | solution.py:304
  35.3 0.0 copy-done.1
  35.3 1.5 shard_map.117.embedded_ref
  36.8 6.9 %collective-permute-done.3.shard_ref = bf16[48,512]{1,0:T(8,128)(2,1)S(1)} collective-permute-done((bf16[48,512]{1,0:T(8,128)(2,1)S(1)}, bf16[48,512]{1,0:T(8,128)(2,1)S(1)}, u32[]{:S(2)}, u32[]{:S(2)}) %collective-permute-start.3) | collective-permute-done | bytes 49184 | tf_op jit(solution)/shard_map/ppermute | solution.py:304
  43.8 10.5 %all_to_all.46.x_ref = bf16[8,48,512]{2,1,0:T(8,128)(2,1)S(1)} all-to-all(bf16[8,48,512]{2,1,0:T(8,128)(2,1)S(1)} %broadcast_in_dim.17), channel_id=1, replica_groups=mesh['line'=8,'place'=4,'core'=2,'tp'=8] {'tp'}, dimensions={0} | all-to-all | bytes 786432 | tf_op jit(solution)/shard_map/all_to_all | solution.py:308
  54.3 2.6 %shard_map.118 = (bf16[8,48,512]{2,1,0:T(8,128)(2,1)S(1)}, f32[48,128]{1,0:T(8,128)S(1)}) custom-call(s32[3]{0:T(128)S(1)} %pad_add_fusion.place_ref, s32[32,96]{1,0:T(8,128)S(1)} %get-tuple-element.31.lengths_ref, f32[1,2048]{1,0:T(1,128)S(1)} %get-tuple-element.35.g_own, f32[1,2048]{1,0:T(1,128)S(1)} %get-tuple-element.36.g_oth, ...), custom_call_target="tpu_custom_call" | custom-call | tf_op jit(solution)/shard_map/pallas_call | solution.py:279
  56.9 10.1 %all_to_all.47.got_ref = bf16[8,48,512]{2,1,0:T(8,128)(2,1)S(1)} all-to-all(bf16[8,48,512]{2,1,0:T(8,128)(2,1)S(1)} %get-tuple-element.41), channel_id=1, replica_groups=mesh['line'=8,'place'=4,'core'=2,'tp'=8] {'tp'}, dimensions={0} | all-to-all | bytes 786432 | tf_op jit(solution)/shard_map/all_to_all | solution.py:308
  66.9 0.6 shard_map.119.early_1
  67.6 0.7 collective-permute-start.4
  68.2 0.0 collective-permute-done.4.shard_ref
  68.3 9.2 %all_to_all.48.x_ref = bf16[8,48,512]{2,1,0:T(8,128)(2,1)S(1)} all-to-all(bf16[8,48,512]{2,1,0:T(8,128)(2,1)S(1)} %broadcast_in_dim.18), channel_id=1, replica_groups=mesh['line'=8,'place'=4,'core'=2,'tp'=8] {'tp'}, dimensions={0} | all-to-all | bytes 786432 | tf_op jit(solution)/shard_map/all_to_all | solution.py:308
  77.5 2.6 %shard_map.120 = (bf16[8,48,512]{2,1,0:T(8,128)(2,1)S(1)}, f32[48,128]{1,0:T(8,128)S(1)}) custom-call(s32[3]{0:T(128)S(1)} %pad_add_fusion.place_ref, s32[32,96]{1,0:T(8,128)S(1)} %get-tuple-element.31.lengths_ref, f32[1,2048]{1,0:T(1,128)S(1)} %get-tuple-element.35.g_own, f32[1,2048]{1,0:T(1,128)S(1)} %get-tuple-element.36.g_oth, ...), custom_call_target="tpu_custom_call" | custom-call | tf_op jit(solution)/shard_map/pallas_call | solution.py:279
  80.1 9.2 %all_to_all.49.got_ref = bf16[8,48,512]{2,1,0:T(8,128)(2,1)S(1)} all-to-all(bf16[8,48,512]{2,1,0:T(8,128)(2,1)S(1)} %get-tuple-element.43), channel_id=1, replica_groups=mesh['line'=8,'place'=4,'core'=2,'tp'=8] {'tp'}, dimensions={0} | all-to-all | bytes 786432 | tf_op jit(solution)/shard_map/all_to_all | solution.py:308
  89.3 0.6 shard_map.121.early_2
  89.9 0.7 collective-permute-start.5
  90.6 0.0 collective-permute-done.5.shard_ref
  90.6 9.2 %all_to_all.50.x_ref = bf16[8,48,512]{2,1,0:T(8,128)(2,1)S(1)} all-to-all(bf16[8,48,512]{2,1,0:T(8,128)(2,1)S(1)} %broadcast_in_dim.19), channel_id=1, replica_groups=mesh['line'=8,'place'=4,'core'=2,'tp'=8] {'tp'}, dimensions={0} | all-to-all | bytes 786432 | tf_op jit(solution)/shard_map/all_to_all | solution.py:308
  99.9 2.6 %shard_map.122 = (bf16[8,48,512]{2,1,0:T(8,128)(2,1)S(1)}, f32[48,128]{1,0:T(8,128)S(1)}) custom-call(s32[3]{0:T(128)S(1)} %pad_add_fusion.place_ref, s32[32,96]{1,0:T(8,128)S(1)} %get-tuple-element.31.lengths_ref, f32[1,2048]{1,0:T(1,128)S(1)} %get-tuple-element.35.g_own, f32[1,2048]{1,0:T(1,128)S(1)} %get-tuple-element.36.g_oth, ...), custom_call_target="tpu_custom_call" | custom-call | tf_op jit(solution)/shard_map/pallas_call | solution.py:279
  102.4 0.0 copy-start.2
  102.5 9.2 %all_to_all.51.got_ref = bf16[8,48,512]{2,1,0:T(8,128)(2,1)S(1)} all-to-all(bf16[8,48,512]{2,1,0:T(8,128)(2,1)S(1)} %get-tuple-element.45), channel_id=1, replica_groups=mesh['line'=8,'place'=4,'core'=2,'tp'=8] {'tp'}, dimensions={0} | all-to-all | bytes 786432 | tf_op jit(solution)/shard_map/all_to_all | solution.py:308
  111.7 0.6 shard_map.123
  112.3 14.1 %collective-permute-start.7 = (bf16[48,512]{1,0:T(8,128)(2,1)S(1)}, bf16[48,512]{1,0:T(8,128)(2,1)S(1)}, u32[]{:S(2)}, u32[]{:S(2)}) collective-permute-start(bf16[48,512]{1,0:T(8,128)(2,1)S(1)} %get-tuple-element.47), channel_id=1, source_target_pairs={{0,64},{8,72},{16,80},{24,88},{32,96},{40,104},{496,48},{504,56},{... | collective-permute-start | bytes 147464 | tf_op jit(solution)/shard_map/ppermute | solution.py:321
  126.4 3.4 %collective-permute-start.6 = (bf16[48,512]{1,0:T(8,128)(2,1)S(1)}, bf16[48,512]{1,0:T(8,128)(2,1)S(1)}, u32[]{:S(2)}, u32[]{:S(2)}) collective-permute-start(bf16[48,512]{1,0:T(8,128)(2,1)S(1)} %get-tuple-element.47), channel_id=1, source_target_pairs={{0,448},{8,456},{16,464},{24,472},{32,480},{40,488},{496,432},{504... | collective-permute-start | bytes 147464 | tf_op jit(solution)/shard_map/ppermute | solution.py:321
  129.8 4.6 %collective-permute-start.10 = (bf16[48,512]{1,0:T(8,128)(2,1)S(1)}, bf16[48,512]{1,0:T(8,128)(2,1)S(1)}, u32[]{:S(2)}, u32[]{:S(2)}) collective-permute-start(bf16[48,512]{1,0:T(8,128)(2,1)S(1)} %get-tuple-element.47), channel_id=1, source_target_pairs={{0,256},{8,264},{16,272},{24,280},{32,288},{40,296},{496,240},{504... | collective-permute-start | bytes 147464 | tf_op jit(solution)/shard_map/ppermute | solution.py:321
  134.4 0.0 collective-permute-done.7
  134.4 0.0 collective-permute-done.6
  134.5 0.7 collective-permute-start.9
  135.1 0.7 collective-permute-start.8
  135.8 0.0 collective-permute-done.10
  135.8 0.0 collective-permute-done.9
  135.8 0.0 collective-permute-done.8
  135.9 10.3 %all_to_all.52.rows_ref = bf16[4,48,512]{2,1,0:T(8,128)(2,1)S(1)} all-to-all(bf16[4,48,512]{2,1,0:T(8,128)(2,1)S(1)} %broadcast_in_dim.21), channel_id=1, replica_groups=mesh['line'=8,'place'=4,'core'=2,'tp'=8] {'place'}, dimensions={0} | all-to-all | bytes 393216 | tf_op jit(solution)/shard_map/all_to_all | solution.py:308
  146.2 0.0 copy-done.2
  146.2 1.5 shard_map.124
  147.7 0.1 broadcast_in_dim.22
  147.7 29.3 %all_to_all.53.got_ref = bf16[16,96,256]{2,1,0:T(8,128)(2,1)S(1)} all-to-all(bf16[16,96,256]{2,1,0:T(8,128)(2,1)S(1)} %bitcast.14), channel_id=1, replica_groups=mesh['line'=8,'place'=4,'core'=2,'tp'=8] {'core','tp'}, dimensions={0} | all-to-all | bytes 1572864 | tf_op jit(solution)/shard_map/all_to_all | solution.py:308
  177.1 1.0 shard_map.125
  (7 shorter events, 0.1 us)
Async XLA Ops:
  0.6 17.0 %collective-permute-start.1 = (bf16[2048,384]{1,0:T(8,128)(2,1)}, bf16[2048,384]{1,0:T(8,128)(2,1)S(1)}, u32[]{:S(2)}, u32[]{:S(2)}) collective-permute-start(bf16[2048,384]{1,0:T(8,128)(2,1)} %bitcast.15), channel_id=1, source_target_pairs={{0,8},{8,0},{1,9},{9,1},{2,10},{10,2},{3,11},{11,3},{4,12},{12,4},... | collective-permute-start | bytes 4718600 | tf_op jit(solution)/shard_map/ppermute | solution.py:298
  9.4 8.2 %collective-permute-start.2 = (bf16[256,2048]{1,0:T(8,128)(2,1)}, bf16[256,2048]{1,0:T(8,128)(2,1)S(1)}, u32[]{:S(2)}, u32[]{:S(2)}) collective-permute-start(bf16[256,2048]{1,0:T(8,128)(2,1)} %bitcast.17), channel_id=1, source_target_pairs={{0,8},{8,0},{1,9},{9,1},{2,10},{10,2},{3,11},{11,3},{4,12},{12,4},... | collective-permute-start | bytes 3145736 | tf_op jit(solution)/shard_map/ppermute | solution.py:298
  11.4 0.7 copy-start
  13.1 4.5 %collective-permute-start = (bf16[144,2048]{1,0:T(8,128)(2,1)S(1)}, bf16[144,2048]{1,0:T(8,128)(2,1)}, u32[]{:S(2)}, u32[]{:S(2)}) collective-permute-start(bf16[144,2048]{1,0:T(8,128)(2,1)S(1)} %shard_map.113.packed_own), channel_id=1, source_target_pairs={{0,8},{8,0},{1,9},{9,1},{2,10},{10,2},{3,11},{11,3},{4,12},{12,4},... | collective-permute-start | bytes 1769480 | tf_op jit(solution)/shard_map/ppermute | solution.py:298
  17.6 17.6 %copy-start.1 = (s32[4,96,4]{1,2,0:T(4,128)S(1)}, s32[4,96,4]{1,2,0:T(4,128)}, u32[]{:S(2)}) copy-start(s32[4,96,4]{1,2,0:T(4,128)} %param.19) | copy-start | bytes 18436
  32.0 11.7 %collective-permute-start.3 = (bf16[48,512]{1,0:T(8,128)(2,1)S(1)}, bf16[48,512]{1,0:T(8,128)(2,1)S(1)}, u32[]{:S(2)}, u32[]{:S(2)}) collective-permute-start(bf16[48,512]{1,0:T(8,128)(2,1)S(1)} %shard_map.116.early_0), channel_id=1, source_target_pairs={{0,16},{8,24},{16,32},{24,40},{32,48},{40,56},{48,64},{56,72},{64,... | collective-permute-start | bytes 147464 | tf_op jit(solution)/shard_map/ppermute | solution.py:304
  67.6 0.7 collective-permute-start.4
  89.9 0.7 collective-permute-start.5
  102.4 43.7 %copy-start.2 = (bf16[2,256]{1,0:T(2,128)(2,1)S(1)}, bf16[2,256]{1,0:T(2,128)(2,1)}, u32[]{:S(2)}) copy-start(bf16[2,256]{1,0:T(2,128)(2,1)} %talk_gain.1) | copy-start | bytes 3076
  112.3 22.1 %collective-permute-start.7 = (bf16[48,512]{1,0:T(8,128)(2,1)S(1)}, bf16[48,512]{1,0:T(8,128)(2,1)S(1)}, u32[]{:S(2)}, u32[]{:S(2)}) collective-permute-start(bf16[48,512]{1,0:T(8,128)(2,1)S(1)} %get-tuple-element.47), channel_id=1, source_target_pairs={{0,64},{8,72},{16,80},{24,88},{32,96},{40,104},{496,48},{504,56},{... | collective-permute-start | bytes 147464 | tf_op jit(solution)/shard_map/ppermute | solution.py:321
  126.4 8.0 %collective-permute-start.6 = (bf16[48,512]{1,0:T(8,128)(2,1)S(1)}, bf16[48,512]{1,0:T(8,128)(2,1)S(1)}, u32[]{:S(2)}, u32[]{:S(2)}) collective-permute-start(bf16[48,512]{1,0:T(8,128)(2,1)S(1)} %get-tuple-element.47), channel_id=1, source_target_pairs={{0,448},{8,456},{16,464},{24,472},{32,480},{40,488},{496,432},{504... | collective-permute-start | bytes 147464 | tf_op jit(solution)/shard_map/ppermute | solution.py:321
  129.8 6.0 %collective-permute-start.10 = (bf16[48,512]{1,0:T(8,128)(2,1)S(1)}, bf16[48,512]{1,0:T(8,128)(2,1)S(1)}, u32[]{:S(2)}, u32[]{:S(2)}) collective-permute-start(bf16[48,512]{1,0:T(8,128)(2,1)S(1)} %get-tuple-element.47), channel_id=1, source_target_pairs={{0,256},{8,264},{16,272},{24,280},{32,288},{40,296},{496,240},{504... | collective-permute-start | bytes 147464 | tf_op jit(solution)/shard_map/ppermute | solution.py:321
  134.5 1.4 collective-permute-start.9
  135.1 0.7 collective-permute-start.8

commit v7 on v6

--- a/solution.py
+++ b/solution.py
@@ -187,7 +187,7 @@
     return jnp.concatenate(both, axis=0).astype(bf16)
 
 
-def embed_kernel(place_ref, packed_own, packed_oth, codes_ref, out_ref):
+def embed_kernel(place_ref, packed_own, packed_oth, codes_ref, out_ref, adapt_ref):
     column, first = place_ref[2], place_ref[0] == 0
     entries = packed_own.shape[1] // 8
     embedded = jnp.zeros(out_ref.shape, f32)
@@ -200,14 +200,16 @@
         table = pair_table(2 + q, first, packed_own, packed_oth)
         embedded = embedded + jnp.dot(table, hot, preferred_element_type=f32)
     out_ref[...] = embedded
+    for i in range(adapt_ref.shape[0]):
+        adapt_ref[i] = pair_table(i, first, packed_own, packed_oth)
 
 
 def talk_kernel(
-    place_ref, rows_ref, latest_ref, talk_gain, packed_own, packed_oth, embedded_ref, out_ref
+    place_ref, rows_ref, latest_ref, talk_gain, adapt_ref, embedded_ref, out_ref
 ):
     first = place_ref[0] == 0
     block = rows_ref.shape[2] // 2
-    columns = packed_own.shape[0] - B
+    columns = adapt_ref.shape[1] // 2
     gains = talk_gain[...].astype(f32)
 
     def halves(rows):
@@ -224,7 +226,7 @@
     for i, part in enumerate((low, high)):
         scaled = (part * gains[i : i + 1]).astype(bf16)
         adapted = adapted + lax.dot_general(
-            pair_table(i, first, packed_own, packed_oth),
+            adapt_ref[i],
             scaled,
             CONTRACT_LAST,
             preferred_element_type=f32,
@@ -381,11 +383,12 @@
         shard = to_next(finals[-1], tick)
         if tick == 0:
             tokens, _ = lax.optimization_barrier((codes.transpose(0, 2, 1), finals[0]))
-            embedded = run(
-                embed_kernel, shaped(2 * columns, TICKS * HALF, dtype=f32),
+            embedded, adapt = run(
+                embed_kernel,
+                (shaped(2 * columns, TICKS * HALF, dtype=f32), shaped(2, 2 * columns, block)),
                 place, packed_own, packed_oth, tokens,
             )
-            shard, embedded = lax.optimization_barrier((shard, embedded))
+            shard, embedded, adapt = lax.optimization_barrier((shard, embedded, adapt))
         rows = exchange(replicate(shard, shards))
         terms, inverse = run(
             functools.partial(later_kernel, tick + 1),
@@ -402,7 +405,7 @@
     payload = run(
         talk_kernel,
         shaped(2, B, block),
-        place, talk_rows, latest, talk_gain, packed_own, packed_oth, embedded,
+        place, talk_rows, latest, talk_gain, adapt, embedded,
     )
     payload = jnp.broadcast_to(payload[:, None], (2, shards, B, block))
     sums = exchange(payload.reshape(2 * shards, B, block), ("core", "tp"))

time: 179 us -> 180 us (level)
  no operation moved by 1% of the time
where the time goes in v7:
time: 180 us; the launch traced here: 178 us
  blocking collectives  108 us (60%)
  starting transfers between devices  41.1 us (23%)
  Pallas kernels  19.7 us (11%)
  waiting for transfers between devices  6.93 us (4%)
    all_to_all x9, blocking collectives, exchange(): return lax.all_to_all(blocks, axis, 0, 0, tiled=True)  108 us
    ppermute x5, starting transfers between devices, sent(): return lax.ppermute(rows, SECTION, pairs)  23.4 us
    pallas_call x11, Pallas kernels, run(): pl.pallas_call(kernel, out_shape=outs, in_specs=specs, out_specs=out_spec...  16.7 us
    ppermute x3, starting transfers between devices, to_partner(): return lax.ppermute(value, 'core', [(0, 1), (1, 0)])  13.1 us
    ppermute x3, waiting for transfers between devices, to_next(): lax.ppermute(value, SECTION, pairs + [(count - 2 + c, kept + c) for c in...  6.91 us
    ppermute x3, starting transfers between devices, to_next(): lax.ppermute(value, SECTION, pairs + [(count - 2 + c, kept + c) for c in...  4.63 us
  transfers between devices with their start and end apart: 11, of which 1 were waited for; matrix products, arithmetic and copies ran while one was open for 0% of the time, Pallas kernels for 3%

profile of v7, /device:TPU:1, one launch (start us, length us, event | category | flops | bytes accessed | tf_op | source)
XLA Modules:
  0.0 177.5 jit_solution(17238595606096683404)
XLA Ops:
  0.6 8.8 %collective-permute-start.1 = (bf16[2048,384]{1,0:T(8,128)(2,1)}, bf16[2048,384]{1,0:T(8,128)(2,1)S(1)}, u32[]{:S(2)}, u32[]{:S(2)}) collective-permute-start(bf16[2048,384]{1,0:T(8,128)(2,1)} %bitcast.15), channel_id=1, source_target_pairs={{0,8},{8,0},{1,9},{9,1},{2,10},{10,2},{3,11},{11,3},{4,12},{12,4},... | collective-permute-start | bytes 4718600 | tf_op jit(solution)/shard_map/ppermute | solution.py:300
  9.4 1.9 %collective-permute-start.2 = (bf16[256,2048]{1,0:T(8,128)(2,1)}, bf16[256,2048]{1,0:T(8,128)(2,1)S(1)}, u32[]{:S(2)}, u32[]{:S(2)}) collective-permute-start(bf16[256,2048]{1,0:T(8,128)(2,1)} %bitcast.17), channel_id=1, source_target_pairs={{0,8},{8,0},{1,9},{9,1},{2,10},{10,2},{3,11},{11,3},{4,12},{12,4},... | collective-permute-start | bytes 3145736 | tf_op jit(solution)/shard_map/ppermute | solution.py:300
  11.4 0.0 copy-start
  11.4 0.7 copy-done
  12.1 1.1 shard_map.113.packed_own
  13.1 2.4 %collective-permute-start = (bf16[144,2048]{1,0:T(8,128)(2,1)S(1)}, bf16[144,2048]{1,0:T(8,128)(2,1)}, u32[]{:S(2)}, u32[]{:S(2)}) collective-permute-start(bf16[144,2048]{1,0:T(8,128)(2,1)S(1)} %shard_map.113.packed_own), channel_id=1, source_target_pairs={{0,8},{8,0},{1,9},{9,1},{2,10},{10,2},{3,11},{11,3},{4,12},{12,4},... | collective-permute-start | bytes 1769480 | tf_op jit(solution)/shard_map/ppermute | solution.py:300
  15.6 2.0 %shard_map.114 = (s32[32,96]{1,0:T(8,128)S(1)}, bf16[2048,384]{1,0:T(8,128)(2,1)S(1)}, bf16[256,2048]{1,0:T(8,128)(2,1)S(1)}, bf16[4,768,128]{2,1,0:T(8,128)(2,1)S(1)}) custom-call(s32[32,96]{1,0:T(8,128)} %refs_0_, bf16[2048,384]{1,0:T(8,128)(2,1)} %bitcast.16, bf16[256,2048]{1,0:T(8,128)(2,1)} %bitcast.18, bf16[4,768,128]{2,1,0:T(8,128)(2,1)} %bitcast.19), custom_call_target="tpu_custom_call" | custom-call | bytes 7340032 | tf_op jit(solution)/shard_map/pallas_call | solution.py:363
  17.6 0.1 pad_add_fusion.place_ref
  17.6 0.0 collective-permute-done.packed_oth
  17.6 0.0 collective-permute-done.2.o_oth
  17.6 0.0 collective-permute-done.1.w_oth
  17.7 0.0 copy-start.1
  17.7 3.1 %shard_map.115 = (bf16[8,48,512]{2,1,0:T(8,128)(2,1)S(1)}, bf16[48,512]{1,0:T(8,128)(2,1)S(1)}, f32[1,2048]{1,0:T(1,128)S(1)}, f32[1,2048]{1,0:T(1,128)S(1)}) custom-call(s32[3]{0:T(128)S(1)} %pad_add_fusion.place_ref, s32[32,96]{1,0:T(8,128)S(1)} %get-tuple-element.34.lengths_ref, bf16[144,2048]{1,0:T(8,128)(2,1)S(1)} %shard_map.113.packed_own, ...), custom_call_target="tpu_custom_call" | custom-call | tf_op jit(solution)/shard_map/pallas_call | solution.py:281
  20.8 10.6 %all_to_all.45.got_ref = bf16[8,48,512]{2,1,0:T(8,128)(2,1)S(1)} all-to-all(bf16[8,48,512]{2,1,0:T(8,128)(2,1)S(1)} %get-tuple-element.40), channel_id=1, replica_groups=mesh['line'=8,'place'=4,'core'=2,'tp'=8] {'tp'}, dimensions={0} | all-to-all | bytes 786432 | tf_op jit(solution)/shard_map/all_to_all | solution.py:310
  31.4 0.6 shard_map.116.early_0
  32.0 3.3 %collective-permute-start.3 = (bf16[48,512]{1,0:T(8,128)(2,1)S(1)}, bf16[48,512]{1,0:T(8,128)(2,1)S(1)}, u32[]{:S(2)}, u32[]{:S(2)}) collective-permute-start(bf16[48,512]{1,0:T(8,128)(2,1)S(1)} %shard_map.116.early_0), channel_id=1, source_target_pairs={{0,16},{8,24},{16,32},{24,40},{32,48},{40,56},{48,64},{56,72},{64,... | collective-permute-start | bytes 147464 | tf_op jit(solution)/shard_map/ppermute | solution.py:306
  35.3 0.0 copy-done.1
  35.3 1.5 shard_map.117
  36.8 6.9 %collective-permute-done.3.shard_ref = bf16[48,512]{1,0:T(8,128)(2,1)S(1)} collective-permute-done((bf16[48,512]{1,0:T(8,128)(2,1)S(1)}, bf16[48,512]{1,0:T(8,128)(2,1)S(1)}, u32[]{:S(2)}, u32[]{:S(2)}) %collective-permute-start.3) | collective-permute-done | bytes 49184 | tf_op jit(solution)/shard_map/ppermute | solution.py:306
  43.8 10.5 %all_to_all.46.x_ref = bf16[8,48,512]{2,1,0:T(8,128)(2,1)S(1)} all-to-all(bf16[8,48,512]{2,1,0:T(8,128)(2,1)S(1)} %broadcast_in_dim.17), channel_id=1, replica_groups=mesh['line'=8,'place'=4,'core'=2,'tp'=8] {'tp'}, dimensions={0} | all-to-all | bytes 786432 | tf_op jit(solution)/shard_map/all_to_all | solution.py:310
  54.3 2.6 %shard_map.118 = (bf16[8,48,512]{2,1,0:T(8,128)(2,1)S(1)}, f32[48,128]{1,0:T(8,128)S(1)}) custom-call(s32[3]{0:T(128)S(1)} %pad_add_fusion.place_ref, s32[32,96]{1,0:T(8,128)S(1)} %get-tuple-element.34.lengths_ref, f32[1,2048]{1,0:T(1,128)S(1)} %get-tuple-element.38.g_own, f32[1,2048]{1,0:T(1,128)S(1)} %get-tuple-element.39.g_oth, ...), custom_call_target="tpu_custom_call" | custom-call | tf_op jit(solution)/shard_map/pallas_call | solution.py:281
  56.9 10.0 %all_to_all.47.got_ref = bf16[8,48,512]{2,1,0:T(8,128)(2,1)S(1)} all-to-all(bf16[8,48,512]{2,1,0:T(8,128)(2,1)S(1)} %get-tuple-element.46), channel_id=1, replica_groups=mesh['line'=8,'place'=4,'core'=2,'tp'=8] {'tp'}, dimensions={0} | all-to-all | bytes 786432 | tf_op jit(solution)/shard_map/all_to_all | solution.py:310
  66.9 0.6 shard_map.119.early_1
  67.5 0.7 collective-permute-start.4
  68.2 0.0 collective-permute-done.4.shard_ref
  68.3 9.2 %all_to_all.48.x_ref = bf16[8,48,512]{2,1,0:T(8,128)(2,1)S(1)} all-to-all(bf16[8,48,512]{2,1,0:T(8,128)(2,1)S(1)} %broadcast_in_dim.18), channel_id=1, replica_groups=mesh['line'=8,'place'=4,'core'=2,'tp'=8] {'tp'}, dimensions={0} | all-to-all | bytes 786432 | tf_op jit(solution)/shard_map/all_to_all | solution.py:310
  77.5 2.6 %shard_map.120 = (bf16[8,48,512]{2,1,0:T(8,128)(2,1)S(1)}, f32[48,128]{1,0:T(8,128)S(1)}) custom-call(s32[3]{0:T(128)S(1)} %pad_add_fusion.place_ref, s32[32,96]{1,0:T(8,128)S(1)} %get-tuple-element.34.lengths_ref, f32[1,2048]{1,0:T(1,128)S(1)} %get-tuple-element.38.g_own, f32[1,2048]{1,0:T(1,128)S(1)} %get-tuple-element.39.g_oth, ...), custom_call_target="tpu_custom_call" | custom-call | tf_op jit(solution)/shard_map/pallas_call | solution.py:281
  80.1 9.2 %all_to_all.49.got_ref = bf16[8,48,512]{2,1,0:T(8,128)(2,1)S(1)} all-to-all(bf16[8,48,512]{2,1,0:T(8,128)(2,1)S(1)} %get-tuple-element.48), channel_id=1, replica_groups=mesh['line'=8,'place'=4,'core'=2,'tp'=8] {'tp'}, dimensions={0} | all-to-all | bytes 786432 | tf_op jit(solution)/shard_map/all_to_all | solution.py:310
  89.3 0.6 shard_map.121.early_2
  89.9 0.7 collective-permute-start.5
  90.6 0.0 collective-permute-done.5.shard_ref
  90.6 9.2 %all_to_all.50.x_ref = bf16[8,48,512]{2,1,0:T(8,128)(2,1)S(1)} all-to-all(bf16[8,48,512]{2,1,0:T(8,128)(2,1)S(1)} %broadcast_in_dim.19), channel_id=1, replica_groups=mesh['line'=8,'place'=4,'core'=2,'tp'=8] {'tp'}, dimensions={0} | all-to-all | bytes 786432 | tf_op jit(solution)/shard_map/all_to_all | solution.py:310
  99.9 2.6 %shard_map.122 = (bf16[8,48,512]{2,1,0:T(8,128)(2,1)S(1)}, f32[48,128]{1,0:T(8,128)S(1)}) custom-call(s32[3]{0:T(128)S(1)} %pad_add_fusion.place_ref, s32[32,96]{1,0:T(8,128)S(1)} %get-tuple-element.34.lengths_ref, f32[1,2048]{1,0:T(1,128)S(1)} %get-tuple-element.38.g_own, f32[1,2048]{1,0:T(1,128)S(1)} %get-tuple-element.39.g_oth, ...), custom_call_target="tpu_custom_call" | custom-call | tf_op jit(solution)/shard_map/pallas_call | solution.py:281
  102.4 0.0 copy-start.2
  102.4 9.2 %all_to_all.51.got_ref = bf16[8,48,512]{2,1,0:T(8,128)(2,1)S(1)} all-to-all(bf16[8,48,512]{2,1,0:T(8,128)(2,1)S(1)} %get-tuple-element.50), channel_id=1, replica_groups=mesh['line'=8,'place'=4,'core'=2,'tp'=8] {'tp'}, dimensions={0} | all-to-all | bytes 786432 | tf_op jit(solution)/shard_map/all_to_all | solution.py:310
  111.7 0.6 shard_map.123
  112.3 16.8 %collective-permute-start.6 = (bf16[48,512]{1,0:T(8,128)(2,1)S(1)}, bf16[48,512]{1,0:T(8,128)(2,1)S(1)}, u32[]{:S(2)}, u32[]{:S(2)}) collective-permute-start(bf16[48,512]{1,0:T(8,128)(2,1)S(1)} %get-tuple-element.52), channel_id=1, source_target_pairs={{0,448},{8,456},{16,464},{24,472},{32,480},{40,488},{496,432},{504... | collective-permute-start | bytes 147464 | tf_op jit(solution)/shard_map/ppermute | solution.py:323
  129.1 1.3 collective-permute-start.7
  130.4 4.0 %collective-permute-start.10 = (bf16[48,512]{1,0:T(8,128)(2,1)S(1)}, bf16[48,512]{1,0:T(8,128)(2,1)S(1)}, u32[]{:S(2)}, u32[]{:S(2)}) collective-permute-start(bf16[48,512]{1,0:T(8,128)(2,1)S(1)} %get-tuple-element.52), channel_id=1, source_target_pairs={{0,256},{8,264},{16,272},{24,280},{32,288},{40,296},{496,240},{504... | collective-permute-start | bytes 147464 | tf_op jit(solution)/shard_map/ppermute | solution.py:323
  134.4 0.0 collective-permute-done.6
  134.4 0.0 collective-permute-done.7
  134.5 0.7 collective-permute-start.8
  135.1 0.7 collective-permute-start.9
  135.8 0.0 collective-permute-done.10
  135.8 0.0 collective-permute-done.8
  135.8 0.0 collective-permute-done.9
  135.9 10.3 %all_to_all.52.rows_ref = bf16[4,48,512]{2,1,0:T(8,128)(2,1)S(1)} all-to-all(bf16[4,48,512]{2,1,0:T(8,128)(2,1)S(1)} %broadcast_in_dim.21), channel_id=1, replica_groups=mesh['line'=8,'place'=4,'core'=2,'tp'=8] {'place'}, dimensions={0} | all-to-all | bytes 393216 | tf_op jit(solution)/shard_map/all_to_all | solution.py:310
  146.2 0.0 copy-done.2
  146.2 0.9 shard_map.124
  147.1 0.1 broadcast_in_dim.22
  147.2 29.3 %all_to_all.53.got_ref = bf16[16,96,256]{2,1,0:T(8,128)(2,1)S(1)} all-to-all(bf16[16,96,256]{2,1,0:T(8,128)(2,1)S(1)} %bitcast.14), channel_id=1, replica_groups=mesh['line'=8,'place'=4,'core'=2,'tp'=8] {'core','tp'}, dimensions={0} | all-to-all | bytes 1572864 | tf_op jit(solution)/shard_map/all_to_all | solution.py:310
  176.5 1.0 shard_map.125
  (7 shorter events, 0.1 us)
Async XLA Ops:
  0.6 17.0 %collective-permute-start.1 = (bf16[2048,384]{1,0:T(8,128)(2,1)}, bf16[2048,384]{1,0:T(8,128)(2,1)S(1)}, u32[]{:S(2)}, u32[]{:S(2)}) collective-permute-start(bf16[2048,384]{1,0:T(8,128)(2,1)} %bitcast.15), channel_id=1, source_target_pairs={{0,8},{8,0},{1,9},{9,1},{2,10},{10,2},{3,11},{11,3},{4,12},{12,4},... | collective-permute-start | bytes 4718600 | tf_op jit(solution)/shard_map/ppermute | solution.py:300
  9.4 8.2 %collective-permute-start.2 = (bf16[256,2048]{1,0:T(8,128)(2,1)}, bf16[256,2048]{1,0:T(8,128)(2,1)S(1)}, u32[]{:S(2)}, u32[]{:S(2)}) collective-permute-start(bf16[256,2048]{1,0:T(8,128)(2,1)} %bitcast.17), channel_id=1, source_target_pairs={{0,8},{8,0},{1,9},{9,1},{2,10},{10,2},{3,11},{11,3},{4,12},{12,4},... | collective-permute-start | bytes 3145736 | tf_op jit(solution)/shard_map/ppermute | solution.py:300
  11.4 0.7 copy-start
  13.1 4.5 %collective-permute-start = (bf16[144,2048]{1,0:T(8,128)(2,1)S(1)}, bf16[144,2048]{1,0:T(8,128)(2,1)}, u32[]{:S(2)}, u32[]{:S(2)}) collective-permute-start(bf16[144,2048]{1,0:T(8,128)(2,1)S(1)} %shard_map.113.packed_own), channel_id=1, source_target_pairs={{0,8},{8,0},{1,9},{9,1},{2,10},{10,2},{3,11},{11,3},{4,12},{12,4},... | collective-permute-start | bytes 1769480 | tf_op jit(solution)/shard_map/ppermute | solution.py:300
  17.7 17.7 %copy-start.1 = (s32[4,96,4]{1,2,0:T(4,128)S(1)}, s32[4,96,4]{1,2,0:T(4,128)}, u32[]{:S(2)}) copy-start(s32[4,96,4]{1,2,0:T(4,128)} %param.19) | copy-start | bytes 18436
  32.0 11.7 %collective-permute-start.3 = (bf16[48,512]{1,0:T(8,128)(2,1)S(1)}, bf16[48,512]{1,0:T(8,128)(2,1)S(1)}, u32[]{:S(2)}, u32[]{:S(2)}) collective-permute-start(bf16[48,512]{1,0:T(8,128)(2,1)S(1)} %shard_map.116.early_0), channel_id=1, source_target_pairs={{0,16},{8,24},{16,32},{24,40},{32,48},{40,56},{48,64},{56,72},{64,... | collective-permute-start | bytes 147464 | tf_op jit(solution)/shard_map/ppermute | solution.py:306
  67.5 0.7 collective-permute-start.4
  89.9 0.7 collective-permute-start.5
  102.4 43.8 %copy-start.2 = (bf16[2,256]{1,0:T(2,128)(2,1)S(1)}, bf16[2,256]{1,0:T(2,128)(2,1)}, u32[]{:S(2)}) copy-start(bf16[2,256]{1,0:T(2,128)(2,1)} %talk_gain.1) | copy-start | bytes 3076
  112.3 22.1 %collective-permute-start.6 = (bf16[48,512]{1,0:T(8,128)(2,1)S(1)}, bf16[48,512]{1,0:T(8,128)(2,1)S(1)}, u32[]{:S(2)}, u32[]{:S(2)}) collective-permute-start(bf16[48,512]{1,0:T(8,128)(2,1)S(1)} %get-tuple-element.52), channel_id=1, source_target_pairs={{0,448},{8,456},{16,464},{24,472},{32,480},{40,488},{496,432},{504... | collective-permute-start | bytes 147464 | tf_op jit(solution)/shard_map/ppermute | solution.py:323
  129.1 5.3 %collective-permute-start.7 = (bf16[48,512]{1,0:T(8,128)(2,1)S(1)}, bf16[48,512]{1,0:T(8,128)(2,1)S(1)}, u32[]{:S(2)}, u32[]{:S(2)}) collective-permute-start(bf16[48,512]{1,0:T(8,128)(2,1)S(1)} %get-tuple-element.52), channel_id=1, source_target_pairs={{0,64},{8,72},{16,80},{24,88},{32,96},{40,104},{496,48},{504,56},{... | collective-permute-start | bytes 147464 | tf_op jit(solution)/shard_map/ppermute | solution.py:323
  130.4 5.4 %collective-permute-start.10 = (bf16[48,512]{1,0:T(8,128)(2,1)S(1)}, bf16[48,512]{1,0:T(8,128)(2,1)S(1)}, u32[]{:S(2)}, u32[]{:S(2)}) collective-permute-start(bf16[48,512]{1,0:T(8,128)(2,1)S(1)} %get-tuple-element.52), channel_id=1, source_target_pairs={{0,256},{8,264},{16,272},{24,280},{32,288},{40,296},{496,240},{504... | collective-permute-start | bytes 147464 | tf_op jit(solution)/shard_map/ppermute | solution.py:323
  134.5 1.4 collective-permute-start.8
  135.1 0.7 collective-permute-start.9
